TPU v7x, 32 devices: a whole 2x2x4 slice. The times are simulated.
32 devices in a mesh: parts: 2 (over y), ctx: 4 (over z), head: 2 (over x), fsdp: 2 (over core).
Axes of the slice: x: 2, y: 2, z: 4, core: 2. Of those that a mesh axis runs over, the one named last changes fastest.
Arguments:
- mixer_input_channels: bfloat16 [4096, 4096], P(('parts', 'ctx'), ('head', 'fsdp')), parts along dimension 0, may hold values from -6 to 6
- gate_channels: bfloat16 [4096, 4096], P(('parts', 'ctx'), ('head', 'fsdp')), parts along dimension 0, may hold values from -6 to 6
- input_group_maps: bfloat16 [4096, 1024], P(('parts', 'ctx'), ('head', 'fsdp')), parts along dimension 0, may hold values from -6 to 6
- output_group_maps: bfloat16 [4096, 1024], P(('parts', 'ctx'), ('head', 'fsdp')), parts along dimension 0, may hold values from -6 to 6
- step_size_input: float32 [64, 4096], P(('head', 'fsdp'), ('parts', 'ctx')), parts along dimension 1, may hold values from -4 to 4
- resets: int32 [4096], P(('parts', 'ctx')), parts along dimension 0, may hold values 0 or 1
- head_decay_rate: float32 [64], P(('head', 'fsdp')), may hold values from 2e-07 to 0.035
- step_size_bias: float32 [64], P(('head', 'fsdp')), may hold values from -1 to 1
- skip: float32 [64], P(('head', 'fsdp')), may hold values from 0.5 to 1.5
- gated_norm_gain: float32 [4096], P(('head', 'fsdp')), may hold values from 0.5 to 1.5
- adapter_down_map: bfloat16 [4096, 64], P(('head', 'fsdp')), may hold values from -0.09375 to 0.09375
- adapter_up_map: bfloat16 [64, 4096], P(None, ('head', 'fsdp')), may hold values from -0.75 to 0.75
- frozen_mixed_gradient: bfloat16 [4096, 4096], P(('parts', 'ctx'), ('head', 'fsdp')), parts along dimension 0, may hold values from -6 to 6
- layer_output_gradient: bfloat16 [4096, 4096], P(('parts', 'ctx'), ('head', 'fsdp')), parts along dimension 0, may hold values from -6 to 6
Outputs:
- mixed: bfloat16 [4096, 4096], P(('parts', 'ctx'), ('head', 'fsdp')), parts along dimension 0
- adapter_output: bfloat16 [4096, 4096], P(('parts', 'ctx'), ('head', 'fsdp')), parts along dimension 0
- mixer_input_gradient: bfloat16 [4096, 4096], P(('parts', 'ctx'), ('head', 'fsdp')), parts along dimension 0
- gate_input_gradient: bfloat16 [4096, 4096], P(('parts', 'ctx'), ('head', 'fsdp')), parts along dimension 0
- input_maps_gradient: bfloat16 [4096, 1024], P(('parts', 'ctx'), ('head', 'fsdp')), parts along dimension 0
- output_maps_gradient: bfloat16 [4096, 1024], P(('parts', 'ctx'), ('head', 'fsdp')), parts along dimension 0
- step_size_gradient: float32 [64, 4096], P(('head', 'fsdp'), ('parts', 'ctx')), parts along dimension 1
- adapter_down_gradient: float32 [8192, 64], P(('parts', 'head', 'fsdp')), parts along dimension 0
- adapter_up_gradient: float32 [128, 4096], P('parts', ('head', 'fsdp')), parts along dimension 0
There are 2 independent parts, one for each index of `parts`. A program takes and returns all parts, laid end to end along the dimension named above; an argument that names none is the same for every part. Nothing has to cross between parts.
All inputs are finite; a program needn't handle non-finite values. No bound on the sum of `resets` on one device may be relied on, other than what follows from the above.
Results may differ from a plain program's by a relative error of at most 0.0057.
Values sent between devices are 32-bit elements; how exact they have to be, the bound alone decides.
No kernel may reach another device: no remote copies, remote signals or barrier semaphores. Data moves between devices by JAX's collectives and lax.ppermute only.
A program may use at most 128 MiB of HBM per device.

v0:
```python
import functools

import jax
import jax.numpy as jnp
from jax import lax
from jax.experimental import pallas as pl
from jax.experimental.pallas import tpu as pltpu
from jax.sharding import PartitionSpec as P

STATE = 128
HEAD = 64
ROWS = 32
EPS = 1e-05
SCALE = 2.0
VMEM = 32 * 2**20

f32 = jnp.float32
bf16 = jnp.bfloat16


def dot(left, right, left_dim, right_dim):
    return lax.dot_general(
        left, right, (((left_dim,), (right_dim,)), ((), ())), preferred_element_type=f32
    )


def split2(v):
    high = v.astype(bf16)
    return high, (v - high.astype(f32)).astype(bf16)


def split3(v):
    high = v.astype(bf16)
    rest = v - high.astype(f32)
    mid = rest.astype(bf16)
    return high, mid, (rest - mid.astype(f32)).astype(bf16)


def head_places(heads, channels):
    lane = lax.broadcasted_iota(jnp.int32, (heads, channels), 1)
    row = lax.broadcasted_iota(jnp.int32, (heads, channels), 0)
    return lane // HEAD == row


def spread(v, places):
    ones = places.astype(bf16)
    return dot(
        jnp.concatenate(split2(v), axis=0), jnp.concatenate([ones, ones], axis=0), 0, 0
    )


def head_column(row, heads, first):
    lane = lax.broadcasted_iota(jnp.int32, (heads, row.shape[1]), 1)
    place = lax.broadcasted_iota(jnp.int32, (heads, row.shape[1]), 0)
    return jnp.sum(jnp.where(lane == place + first, row, 0.0), axis=1, keepdims=True)


def spread_row(v, places):
    return jnp.sum(jnp.where(places, v, 0.0), axis=0, keepdims=True)


def running_sum(v, exclusive):
    rows, length = v.shape
    s = lax.broadcasted_iota(jnp.int32, (length, length), 0)
    r = lax.broadcasted_iota(jnp.int32, (length, length), 1)
    upper = ((s < r) if exclusive else (s <= r)).astype(bf16)
    sums = dot(jnp.concatenate(split3(v), axis=0), upper, 1, 0)
    return sums[:rows] + sums[rows : 2 * rows] + sums[2 * rows :]


def state_kernel(
    x, b, c, step, resets, rates, biases, xw, state, bend, cstart, small, rows, ids_row, ids_col, first
):
    heads, length = step.shape
    rate = head_column(rates[...], heads, first)
    bias = head_column(biases[...], heads, first)
    channels = x.shape[1]
    places = head_places(heads, channels)
    raw = step[...] + bias
    dt = jnp.maximum(raw, 0.0) + jnp.log1p(jnp.exp(-jnp.abs(raw)))
    log_step = -rate * dt
    s = lax.broadcasted_iota(jnp.int32, (length, length), 0)
    r = lax.broadcasted_iota(jnp.int32, (length, length), 1)
    upper = (s <= r).astype(bf16)
    lower = (s >= r).astype(bf16)
    marks = jnp.broadcast_to(resets[...].astype(f32), (8, length)).astype(bf16)
    sums = dot(jnp.concatenate((marks,) + split3(log_step), axis=0), upper, 1, 0)
    ids = sums[:8]
    cum = sums[8 : 8 + heads] + sums[8 + heads : 8 + 2 * heads] + sums[8 + 2 * heads :]
    id_cols = dot(lower, marks, 1, 1)
    ids_row[...] = ids
    ids_col[...] = id_cols
    last = cum[:, length - 1 :]
    last_id = ids[:1, length - 1 :]
    middle = 0.5 * last
    fall = jnp.exp(cum - middle)
    rise = jnp.exp(middle - cum)
    weight = dt * rise
    small[0:heads] = dt
    small[heads : 2 * heads] = fall
    small[2 * heads : 3 * heads] = rise
    small[3 * heads :] = raw
    half_row = spread_row(jnp.exp(middle), places)
    total = jnp.where(last_id == 0, half_row * half_row, 0.0)
    rows[0:1] = total
    rows[1:2] = half_row
    rows[2:8] = jnp.zeros((6, channels), f32)
    xw[...] = (x[...].astype(f32) * spread(weight, places)).astype(bf16)
    to_end = id_cols[:, :1] == last_id
    from_start = id_cols[:, :1] == 0
    bend[...] = jnp.where(to_end, b[...].astype(f32), 0.0).astype(bf16)
    cstart[...] = jnp.where(from_start, c[...].astype(f32), 0.0).astype(bf16)
    state[0:STATE] = dot(bend[...], xw[...], 0, 0) * half_row
    state[STATE:] = jnp.broadcast_to(total, (8, channels))


def score_kernel(b, c, ids_row, ids_col, xw, y_loc):
    length = b.shape[0]
    half = length // 2
    for i in range(2):
        here = pl.ds(i * half, half)
        total = None
        for j in range(i + 1):
            there = pl.ds(j * half, half)
            scores = dot(c[here], b[there], 1, 1)
            same = ids_col[here, 0:1] == ids_row[0:1, there]
            if i == j:
                r = lax.broadcasted_iota(jnp.int32, (half, half), 0)
                s = lax.broadcasted_iota(jnp.int32, (half, half), 1)
                same = same & (r >= s)
            m = jnp.where(same, scores, 0.0).astype(bf16)
            term = dot(m, xw[there], 1, 0)
            total = term if total is None else total + term
        y_loc[here] = total


def gather_incoming(near, far, mid):
    return near[0:STATE] + near[STATE : STATE + 1] * far[...] + mid[...]


def norm_kernel(*refs, first):
    refs = list(refs)
    (y_loc, cstart, near, far, mid, small, rows, x, gate, skips, gain, frozen) = refs[:12]
    (gu_here, gu_there, down) = refs[12:15]
    refs = refs[15:]
    u_before = None if first == 0 else refs.pop(0)
    (mixed, gate_grad, down_part, gye, scaled, state_grad, u_part, y_dot) = refs[:8]
    (inner, falls, g_mixed, product) = refs[8:]
    length, channels = x.shape
    heads = channels // HEAD
    skip = head_column(skips[...], heads, first)
    gu = (SCALE * (gu_here[...] + gu_there[...])).astype(bf16)
    places = head_places(heads, channels)
    scaled[...] = (gather_incoming(near, far, mid) * rows[1:2]).astype(bf16)
    inner[...] = y_loc[...] + dot(cstart[...], scaled[...], 1, 0)
    falls[...] = spread(small[heads : 2 * heads], places)
    g_mixed[...] = frozen[...].astype(f32) + dot(gu, down[...], 0, 0)
    skip_row = spread_row(skip, places)
    gain_row = gain[...]

    def tile(i, carry):
        at = pl.ds(pl.multiple_of(i * ROWS, ROWS), ROWS)
        fall = falls[at]
        within = inner[at]
        z = gate[at].astype(f32)
        y = fall * within + skip_row * x[at].astype(f32)
        sig = 0.5 * jnp.tanh(0.5 * z) + 0.5
        act = z * sig
        grouped = y * act
        inv = lax.rsqrt(jnp.sum(grouped * grouped, axis=1, keepdims=True) * (1.0 / channels) + EPS)
        normed = grouped * inv
        mixed[at] = (normed * gain_row).astype(bf16)
        g_norm = g_mixed[at] * gain_row
        mean = jnp.sum(g_norm * normed, axis=1, keepdims=True) * (1.0 / channels)
        g_grouped = inv * (g_norm - normed * mean)
        gate_grad[at] = (g_grouped * y * (sig + act * (1.0 - sig))).astype(bf16)
        g = (g_grouped * act * fall).astype(bf16)
        gye[at] = g
        high, low = split2(g.astype(f32) * within)
        product[0, at] = high
        product[1, at] = low
        return carry

    lax.fori_loop(0, length // ROWS, tile, 0, unroll=4)
    state_grad[0:STATE] = dot(cstart[...], gye[...], 0, 0) * rows[1:2]
    state_grad[STATE:] = jnp.broadcast_to(rows[0:1], (8, channels))
    u_here = dot(down[...], mixed[...], 1, 1)
    u_part[...] = u_here if first == 0 else u_here + u_before[...]
    down_part[...] = dot(gu, mixed[...], 1, 0)
    ones = places.astype(bf16)
    y_dot[...] = dot(ones, product[0], 1, 1) + dot(ones, product[1], 1, 1)


def pair_kernel(b, c, ids_row, ids_col, xw, gye, scaled_in, c_grad, z_loc, b_loc):
    length = b.shape[0]
    half = length // 2
    scaled = scaled_in[...]
    for i in range(2):
        here = pl.ds(i * half, half)
        carried = dot(gye[here], scaled, 1, 1)
        total = jnp.where(ids_col[here, 0:1] == 0, carried, 0.0)
        for j in range(i + 1):
            there = pl.ds(j * half, half)
            same = ids_col[here, 0:1] == ids_row[0:1, there]
            if i == j:
                r = lax.broadcasted_iota(jnp.int32, (half, half), 0)
                s = lax.broadcasted_iota(jnp.int32, (half, half), 1)
                same = same & (r >= s)
            pair = jnp.where(same, dot(gye[here], xw[there], 1, 1), 0.0).astype(bf16)
            total += dot(pair, b[there], 1, 0)
        c_grad[here] = total.astype(bf16)
    for j in range(2):
        there = pl.ds(j * half, half)
        z_total = None
        for i in range(j, 2):
            here = pl.ds(i * half, half)
            same = ids_col[there, 0:1] == ids_row[0:1, here]
            if i == j:
                s = lax.broadcasted_iota(jnp.int32, (half, half), 0)
                r = lax.broadcasted_iota(jnp.int32, (half, half), 1)
                same = same & (r >= s)
            m = jnp.where(same, dot(b[there], c[here], 1, 1), 0.0).astype(bf16)
            pair = jnp.where(same, dot(xw[there], gye[here], 1, 1), 0.0).astype(bf16)
            z_term = dot(m, gye[here], 1, 0)
            b_term = dot(pair, c[here], 1, 0)
            z_total = z_term if z_total is None else z_total + z_term
            b_total = b_term if i == j else b_total + b_term
        z_loc[there] = z_total
        b_loc[there] = b_total


def input_kernel(
    z_loc, b_loc, bend, ids_col, ids_row, xw, gye, near, far, mid, grad_dev, scaled_in, rows, small, skips,
    rates, y_dot,
    x_grad, b_grad, step_grad,
    inner, weights, rises, product,
    first,
):
    length, channels = xw.shape
    heads = channels // HEAD
    skip = head_column(skips[...], heads, first)
    rate = head_column(rates[...], heads, first)
    places = head_places(heads, channels)
    dt = small[0:heads]
    rise = small[2 * heads : 3 * heads]
    raw = small[3 * heads :]
    incoming = gather_incoming(near, far, mid)
    scaled = (incoming * rows[1:2]).astype(bf16)
    inner[...] = z_loc[...] + dot(bend[...], scaled, 1, 0)
    weights[...] = spread(dt * rise, places)
    rises[...] = spread(skip * rise, places)

    def tile(i, carry):
        at = pl.ds(pl.multiple_of(i * ROWS, ROWS), ROWS)
        z = inner[at]
        x_grad[at] = (weights[at] * z + rises[at] * gye[at].astype(f32)).astype(bf16)
        high, low = split2(xw[at].astype(f32) * z)
        product[0, at] = high
        product[1, at] = low
        return carry

    lax.fori_loop(0, length // ROWS, tile, 0, unroll=4)
    carried = dot(xw[...], scaled, 1, 1)
    to_end = ids_col[:, 0:1] == ids_row[0:1, length - 1 :]
    b_grad[...] = (b_loc[...] + jnp.where(to_end, carried, 0.0)).astype(bf16)
    ones = places.astype(bf16)
    x_dot = dot(ones, product[0], 1, 1) + dot(ones, product[1], 1, 1)
    crossing = jnp.sum(
        (rows[0:1] * incoming + grad_dev[0:STATE]) * scaled_in[...].astype(f32), axis=0, keepdims=True
    ) / rows[1:2]
    constant = jnp.sum(jnp.where(places, crossing, 0.0), axis=1, keepdims=True)
    g_log = running_sum(x_dot - y_dot[...], True) + constant
    g_dt = x_dot / dt - rate * g_log
    step_grad[...] = g_dt / (1.0 + jnp.exp(-raw))


def adapter_kernel(u_here, u_there, up, lo, out, up_part):
    u = (SCALE * (u_here[...] + u_there[...])).astype(bf16)
    out[...] = dot(u, up[...], 0, 0).astype(bf16)
    up_part[...] = dot(u, lo[...], 1, 0)


def rank_kernel(up, lo, part):
    part[...] = dot(up[...], lo[...], 1, 1)


def call(kernel, ins, outs, scratch=(), cost=1.0, name=None):
    in_specs, operands = [], []
    for array, block, index in ins:
        if block is None:
            block, index = array.shape, (0,) * array.ndim
        in_specs.append(pl.BlockSpec(block, functools.partial(lambda at, i: at, index)))
        operands.append(array)
    out_specs, out_shapes, aliases = [], [], {}
    for at, (shape, dtype, block, index, held) in enumerate(outs):
        if block is None:
            block, index = shape, (0,) * len(shape)
        out_specs.append(pl.BlockSpec(block, functools.partial(lambda at, i: at, index)))
        out_shapes.append(jax.ShapeDtypeStruct(shape, dtype))
        if held is not None:
            aliases[len(operands)] = at
            operands.append(held)
            in_specs.append(pl.BlockSpec(memory_space=pl.ANY))
    n_real = len(ins)
    n_held = len(operands) - n_real

    def body(*refs):
        kernel(*refs[:n_real], *refs[n_real + n_held :])

    return pl.pallas_call(
        body,
        grid=(1,),
        in_specs=in_specs,
        out_specs=out_specs,
        out_shape=out_shapes,
        scratch_shapes=list(scratch),
        input_output_aliases=aliases,
        compiler_params=pltpu.CompilerParams(vmem_limit_bytes=VMEM),
        cost_estimate=pl.CostEstimate(
            flops=0, bytes_accessed=int(cost * 3.69e6), transcendentals=0
        ),
        name=name,
    )(*operands)


def passed_on(part, axis, reverse):
    count = lax.axis_size(axis)
    state = part[:STATE]
    decay = part[STATE : STATE + 1]
    if count == 4:
        pairs = [(3, 2), (1, 0)] if reverse else [(0, 1), (2, 3)]
        source, far, mid = (2, 0, 1) if reverse else (1, 3, 2)
        near = lax.ppermute(part, axis, pairs)
        joined = decay * near[:STATE] + state
        return (
            near,
            lax.ppermute(joined, axis, [(source, far)]),
            lax.ppermute(joined, axis, [(source, mid)]),
        )
    incoming = jnp.zeros_like(state)
    out = state
    for hop in range(count - 1):
        pair = (count - 1 - hop, count - 2 - hop) if reverse else (hop, hop + 1)
        got = lax.ppermute(out, axis, [pair])
        incoming = incoming + got
        out = state + decay * got
    return jnp.concatenate([incoming, jnp.zeros_like(part[STATE:])]), incoming, jnp.zeros_like(state)


def exchange_pair(part, axes):
    other = None
    for axis in axes:
        count = lax.axis_size(axis)
        span = 1
        while span < count:
            part = part if other is None else part + other
            other = lax.ppermute(part, axis, [(i, i ^ span) for i in range(count)])
            span *= 2
    return part, other


def exchange_sum(part, axes):
    here, there = exchange_pair(part, axes)
    return here + there


def per_device(
    mixer_input_channels,
    gate_channels,
    input_group_maps,
    output_group_maps,
    step_size_input,
    resets,
    head_decay_rate,
    step_size_bias,
    skip,
    gated_norm_gain,
    adapter_down_map,
    adapter_up_map,
    frozen_mixed_gradient,
    layer_output_gradient,
):
    length, channels = mixer_input_channels.shape
    groups = input_group_maps.shape[1] // STATE
    heads = step_size_input.shape[0] // groups
    width = channels // groups
    rank = adapter_up_map.shape[0]
    resets = resets.reshape(1, length)
    rates = head_decay_rate.reshape(1, -1)
    biases = step_size_bias.reshape(1, -1)
    skips = skip.reshape(1, -1)
    down_map = adapter_down_map.T
    gains = gated_norm_gain.reshape(1, -1)

    def cols(array, g):
        return (array, (array.shape[0], array.shape[1] // groups), (0, g))

    def head_rows(array, g):
        return (array, (heads, array.shape[1]), (g, 0))

    def whole(array):
        return (array, None, None)

    def fresh(shape, dtype):
        return (shape, dtype, None, None, None)

    states = []
    for g in range(groups):
        states.append(
            call(
                functools.partial(state_kernel, first=g * heads),
                [
                    cols(mixer_input_channels, g),
                    cols(input_group_maps, g),
                    cols(output_group_maps, g),
                    head_rows(step_size_input, g),
                    whole(resets),
                    whole(rates),
                    whole(biases),
                ],
                [
                    fresh((length, width), bf16),
                    fresh((STATE + 8, width), f32),
                    fresh((length, STATE), bf16),
                    fresh((length, STATE), bf16),
                    fresh((4 * heads, length), f32),
                    fresh((8, width), f32),
                    fresh((8, length), f32),
                    fresh((length, 8), f32),
                ],
                cost=1.5,
                name="state",
            )
        )
    (gu_part,) = call(
        rank_kernel,
        [whole(adapter_up_map), whole(layer_output_gradient)],
        [fresh((rank, length), f32)],
        cost=1.0,
        name="rank",
    )
    gu = exchange_pair(gu_part, ("fsdp", "head"))
    y_locs = []
    for g in range(groups):
        xw, _, _, _, _, _, ids_row, ids_col = states[g]
        y_locs += call(
            score_kernel,
            [
                cols(input_group_maps, g),
                cols(output_group_maps, g),
                whole(ids_row),
                whole(ids_col),
                whole(xw),
            ],
            [fresh((length, width), f32)],
            cost=1.0,
            name="score",
        )
    entering = [passed_on(states[g][1], "ctx", False) for g in range(groups)]
    mixed = gate_grad = down_part = u_part = None
    normed = []
    for g in range(groups):
        xw, state, bend, cstart, small, rows, ids_row, ids_col = states[g]
        results = call(
            functools.partial(norm_kernel, first=g * heads),
            [
                whole(y_locs[g]),
                whole(cstart),
                *map(whole, entering[g]),
                whole(small),
                whole(rows),
                cols(mixer_input_channels, g),
                cols(gate_channels, g),
                whole(skips),
                cols(gains, g),
                cols(frozen_mixed_gradient, g),
                *map(whole, gu),
                cols(down_map, g),
            ]
            + ([] if g == 0 else [whole(u_part)]),
            [
                ((length, channels), bf16, (length, width), (0, g), mixed),
                ((length, channels), bf16, (length, width), (0, g), gate_grad),
                ((rank, channels), f32, (rank, width), (0, g), down_part),
                fresh((length, width), bf16),
                fresh((STATE, width), bf16),
                fresh((STATE + 8, width), f32),
                fresh((rank, length), f32),
                fresh((heads, length), f32),
            ],
            [
                pltpu.VMEM((length, width), f32),
                pltpu.VMEM((length, width), f32),
                pltpu.VMEM((length, width), f32),
                pltpu.VMEM((2, length, width), bf16),
            ],
            cost=4.0,
            name="norm",
        )
        mixed, gate_grad, down_part, gye, scaled, state_grad, u_part, y_dot = results
        normed.append((gye, scaled, state_grad, y_dot))
    leaving = [passed_on(normed[g][2], "ctx", True) for g in range(groups)]
    u = exchange_pair(u_part, ("fsdp", "head"))
    c_grad = None
    pairs = []
    for g in range(groups):
        xw, state, bend, cstart, small, rows, ids_row, ids_col = states[g]
        c_grad, z_loc, b_loc = call(
            pair_kernel,
            [
                cols(input_group_maps, g),
                cols(output_group_maps, g),
                whole(ids_row),
                whole(ids_col),
                whole(xw),
                whole(normed[g][0]),
                whole(normed[g][1]),
            ],
            [
                ((length, groups * STATE), bf16, (length, STATE), (0, g), c_grad),
                fresh((length, width), f32),
                fresh((length, STATE), f32),
            ],
            cost=2.0,
            name="pair",
        )
        pairs.append((z_loc, b_loc))
    down_sum = exchange_sum(down_part, ("ctx",))
    adapter_output, up_part = call(
        adapter_kernel,
        [*map(whole, u), whole(adapter_up_map), whole(layer_output_gradient)],
        [fresh((length, channels), bf16), fresh((rank, channels), f32)],
        cost=1.5,
        name="adapter",
    )
    up_sum = exchange_sum(up_part, ("ctx",))
    x_grad = b_grad = step_grad = None
    for g in range(groups):
        xw, state, bend, cstart, small, rows, ids_row, ids_col = states[g]
        x_grad, b_grad, step_grad = call(
            functools.partial(input_kernel, first=g * heads),
            [
                whole(pairs[g][0]),
                whole(pairs[g][1]),
                whole(bend),
                whole(ids_col),
                whole(ids_row),
                whole(xw),
                whole(normed[g][0]),
                *map(whole, leaving[g]),
                whole(normed[g][2]),
                whole(normed[g][1]),
                whole(rows),
                whole(small),
                whole(skips),
                whole(rates),
                whole(normed[g][3]),
            ],
            [
                ((length, channels), bf16, (length, width), (0, g), x_grad),
                ((length, groups * STATE), bf16, (length, STATE), (0, g), b_grad),
                ((groups * heads, length), f32, (heads, length), (g, 0), step_grad),
            ],
            [
                pltpu.VMEM((length, width), f32),
                pltpu.VMEM((length, width), f32),
                pltpu.VMEM((length, width), f32),
                pltpu.VMEM((2, length, width), bf16),
            ],
            cost=2.5,
            name="input",
        )
    return (
        mixed,
        adapter_output,
        x_grad,
        gate_grad,
        b_grad,
        c_grad,
        step_grad,
        down_sum.T,
        up_sum,
    )


def solution(mesh):
    rows_cols = P(("parts", "ctx"), ("head", "fsdp"))
    heads = P(("head", "fsdp"))
    in_specs = (
        rows_cols,
        rows_cols,
        rows_cols,
        rows_cols,
        P(("head", "fsdp"), ("parts", "ctx")),
        P(("parts", "ctx")),
        heads,
        heads,
        heads,
        heads,
        P(("head", "fsdp"), None),
        P(None, ("head", "fsdp")),
        rows_cols,
        rows_cols,
    )
    out_specs = (
        rows_cols,
        rows_cols,
        rows_cols,
        rows_cols,
        rows_cols,
        rows_cols,
        P(("head", "fsdp"), ("parts", "ctx")),
        P(("parts", "head", "fsdp"), None),
        P("parts", ("head", "fsdp")),
    )
    return jax.shard_map(
        per_device, mesh=mesh, in_specs=in_specs, out_specs=out_specs, check_vma=False
    )
```

profile of v0, /device:TPU:0, one launch (start us, length us, event | category | flops | bytes accessed | tf_op | source)
XLA Modules:
  0.0 103.6 jit_solution(7947068067362830396)
XLA Ops:
  6.2 5.1 %collective-permute-start.5 = (f32[136,512]{1,0:T(8,128)S(1)}, f32[136,512]{1,0:T(8,128)S(1)}, u32[]{:S(2)}, u32[]{:S(2)}) collective-permute-start(f32[136,512]{1,0:T(8,128)S(1)} %get-tuple-element.66), channel_id=1, source_target_pairs={{0,4},{8,12},{1,5},{9,13},{2,6},{10,14},{3,7},{11,15},{16,20},{24,... | collective-permute-start | bytes 835592 | tf_op jit(solution)/shard_map/ppermute | solution.py:333
  12.3 1.3 %collective-permute-start = (f32[136,512]{1,0:T(8,128)S(1)}, f32[136,512]{1,0:T(8,128)S(1)}, u32[]{:S(2)}, u32[]{:S(2)}) collective-permute-start(f32[136,512]{1,0:T(8,128)S(1)} %get-tuple-element.59), channel_id=1, source_target_pairs={{0,4},{8,12},{1,5},{9,13},{2,6},{10,14},{3,7},{11,15},{16,20},{24,... | collective-permute-start | bytes 835592 | tf_op jit(solution)/shard_map/ppermute | solution.py:333
  14.2 4.2 %collective-permute-done.5.refs_2_ = f32[136,512]{1,0:T(8,128)S(1)} collective-permute-done((f32[136,512]{1,0:T(8,128)S(1)}, f32[136,512]{1,0:T(8,128)S(1)}, u32[]{:S(2)}, u32[]{:S(2)}) %collective-permute-start.5) | collective-permute-done | bytes 278560 | tf_op jit(solution)/shard_map/ppermute | solution.py:333
  19.9 3.3 %collective-permute-done.refs_2_ = f32[136,512]{1,0:T(8,128)S(1)} collective-permute-done((f32[136,512]{1,0:T(8,128)S(1)}, f32[136,512]{1,0:T(8,128)S(1)}, u32[]{:S(2)}, u32[]{:S(2)}) %collective-permute-start) | collective-permute-done | bytes 278560 | tf_op jit(solution)/shard_map/ppermute | solution.py:333
  24.8 1.6 %collective-permute-start.4 = (f32[64,512]{1,0:T(8,128)S(1)}, f32[64,512]{1,0:T(8,128)S(1)}, u32[]{:S(2)}, u32[]{:S(2)}) collective-permute-start(f32[64,512]{1,0:T(8,128)S(1)} %add.31.refs_12_), channel_id=1, source_target_pairs={{0,2},{2,0},{1,3},{3,1},{4,6},{6,4},{5,7},{7,5},{8,10},{10,8},{9,1... | collective-permute-start | bytes 393224 | tf_op jit(solution)/shard_map/ppermute | solution.py:357
  27.0 2.8 %collective-permute-done.4.refs_13_ = f32[64,512]{1,0:T(8,128)S(1)} collective-permute-done((f32[64,512]{1,0:T(8,128)S(1)}, f32[64,512]{1,0:T(8,128)S(1)}, u32[]{:S(2)}, u32[]{:S(2)}) %collective-permute-start.4) | collective-permute-done | bytes 131104 | tf_op jit(solution)/shard_map/ppermute | solution.py:357
  30.5 3.3 %norm.2 = (bf16[512,1024]{1,0:T(8,128)(2,1)}, bf16[512,1024]{1,0:T(8,128)(2,1)}, f32[64,1024]{1,0:T(8,128)S(1)}, bf16[512,512]{1,0:T(8,128)(2,1)S(1)}, bf16[128,...) custom-call(f32[512,512]{1,0:T(8,128)S(1)} %score.3.refs_0_, ...), custom_call_target="tpu_custom_call" | custom-call | bytes 14760000 | tf_op jit(solution)/shard_map/norm/pallas_call | solution.py:310
  35.8 3.4 %norm.3 = (bf16[512,1024]{1,0:T(8,128)(2,1)}, bf16[512,1024]{1,0:T(8,128)(2,1)}, f32[64,1024]{1,0:T(8,128)S(1)}, bf16[512,512]{1,0:T(8,128)(2,1)S(1)}, bf16[128,...) custom-call(f32[512,512]{1,0:T(8,128)S(1)} %score.2.refs_0_, ...), custom_call_target="tpu_custom_call", output_to_operand_aliasing={{0}: (16, {}), {1}: (17, {}), {2}: (18, {})} | custom-call | bytes 14760000 | tf_op jit(solution)/shard_map/norm/pallas_call | solution.py:310
  39.2 10.8 %collective-permute-start.16 = (f32[64,1024]{1,0:T(8,128)S(1)}, f32[64,1024]{1,0:T(8,128)S(1)}, u32[]{:S(2)}, u32[]{:S(2)}) collective-permute-start(f32[64,1024]{1,0:T(8,128)S(1)} %get-tuple-element.99), channel_id=1, source_target_pairs={{0,4},{4,0},{8,12},{12,8},{1,5},{5,1},{9,13},{13,9},{2,6},{6,2},{1... | collective-permute-start | bytes 786440 | tf_op jit(solution)/shard_map/ppermute | solution.py:357
  50.0 1.3 %collective-permute-done.8 = f32[64,512]{1,0:T(8,128)S(1)} collective-permute-done((f32[64,512]{1,0:T(8,128)S(1)}, f32[64,512]{1,0:T(8,128)S(1)}, u32[]{:S(2)}, u32[]{:S(2)}) %collective-permute-start.8) | collective-permute-done | bytes 131104 | tf_op jit(solution)/shard_map/ppermute | solution.py:357
  51.3 1.6 %collective-permute-start.9 = (f32[64,512]{1,0:T(8,128)S(1)}, f32[64,512]{1,0:T(8,128)S(1)}, u32[]{:S(2)}, u32[]{:S(2)}) collective-permute-start(f32[64,512]{1,0:T(8,128)S(1)} %add.33.refs_0_), channel_id=1, source_target_pairs={{0,2},{2,0},{1,3},{3,1},{4,6},{6,4},{5,7},{7,5},{8,10},{10,8},{9,1... | collective-permute-start | bytes 393224 | tf_op jit(solution)/shard_map/ppermute | solution.py:357
  54.2 1.8 %collective-permute-done.16 = f32[64,1024]{1,0:T(8,128)S(1)} collective-permute-done((f32[64,1024]{1,0:T(8,128)S(1)}, f32[64,1024]{1,0:T(8,128)S(1)}, u32[]{:S(2)}, u32[]{:S(2)}) %collective-permute-start.16) | collective-permute-done | bytes 262176 | tf_op jit(solution)/shard_map/ppermute | solution.py:357
  56.1 1.6 %collective-permute-start.17 = (f32[64,1024]{1,0:T(8,128)S(1)}, f32[64,1024]{1,0:T(8,128)S(1)}, u32[]{:S(2)}, u32[]{:S(2)}) collective-permute-start(f32[64,1024]{1,0:T(8,128)S(1)} %add.36), channel_id=1, source_target_pairs={{0,8},{4,12},{8,0},{12,4},{1,9},{5,13},{9,1},{13,5},{2,10},{6,14},... | collective-permute-start | bytes 786440 | tf_op jit(solution)/shard_map/ppermute | solution.py:357
  57.7 1.5 %adapter.1 = (bf16[512,1024]{1,0:T(8,128)(2,1)}, f32[64,1024]{1,0:T(8,128)S(1)}) custom-call(f32[64,512]{1,0:T(8,128)S(1)} %add.33.refs_0_, f32[64,512]{1,0:T(8,128)S(1)} %collective-permute-done.9.refs_1_, bf16[64,1024]{1,0:T(8,128)(2,1)S(1)} %copy-done.9, bf16[512,1024]{1,0:T(8,128)(2,1)S(1)} %copy-done.6), custom_call_target="tpu_custom_call" | custom-call | bytes 5535000 | tf_op jit(solution)/shard_map/adapter/pallas_call | solution.py:310
  61.7 12.9 %collective-permute-done.10.refs_7_ = f32[136,512]{1,0:T(8,128)S(1)} collective-permute-done((f32[136,512]{1,0:T(8,128)S(1)}, f32[136,512]{1,0:T(8,128)S(1)}, u32[]{:S(2)}, u32[]{:S(2)}) %collective-permute-start.10) | collective-permute-done | bytes 278560 | tf_op jit(solution)/shard_map/ppermute | solution.py:333
  74.7 1.3 %collective-permute-start.11 = (f32[128,512]{1,0:T(8,128)S(1)}, f32[128,512]{1,0:T(8,128)S(1)}, u32[]{:S(2)}, u32[]{:S(2)}) collective-permute-start(f32[128,512]{1,0:T(8,128)S(1)} %fusion.1), channel_id=1, source_target_pairs={{8,0},{9,1},{10,2},{11,3},{24,16},{25,17},{26,18},{27,19}} | collective-permute-start | bytes 786440 | tf_op jit(solution)/shard_map/ppermute | solution.py:337
  76.0 4.3 %collective-permute-done.18 = f32[64,1024]{1,0:T(8,128)S(1)} collective-permute-done((f32[64,1024]{1,0:T(8,128)S(1)}, f32[64,1024]{1,0:T(8,128)S(1)}, u32[]{:S(2)}, u32[]{:S(2)}) %collective-permute-start.18) | collective-permute-done | bytes 262176 | tf_op jit(solution)/shard_map/ppermute | solution.py:357
  81.2 2.2 %collective-permute-start.19 = (f32[64,1024]{1,0:T(8,128)S(1)}, f32[64,1024]{1,0:T(8,128)S(1)}, u32[]{:S(2)}, u32[]{:S(2)}) collective-permute-start(f32[64,1024]{1,0:T(8,128)S(1)} %add.38), channel_id=1, source_target_pairs={{0,8},{4,12},{8,0},{12,4},{1,9},{5,13},{9,1},{13,5},{2,10},{6,14},... | collective-permute-start | bytes 786440 | tf_op jit(solution)/shard_map/ppermute | solution.py:357
  83.4 1.6 %pair.2 = (bf16[512,256]{1,0:T(8,128)(2,1)}, f32[512,512]{1,0:T(8,128)S(1)}, f32[512,128]{1,0:T(8,128)S(1)}) custom-call(bf16[512,256]{1,0:T(8,128)(2,1)S(1)} %copy-done.3, bf16[512,256]{1,0:T(8,128)(2,1)S(1)} %copy-done.5, f32[8,512]{1,0:T(8,128)S(1)} %get-tuple-element.62.refs_2_.refs_4_, f32[512,8]{1,0:T(8,128)S(1)} %get-tuple-element.63.refs_3_, ...), custom_call_target="tpu_custom_call" | custom-call | bytes 7380000 | tf_op jit(solution)/shard_map/pair/pallas_call | solution.py:310
  85.0 2.0 %pair.3 = (bf16[512,256]{1,0:T(8,128)(2,1)}, f32[512,512]{1,0:T(8,128)S(1)}, f32[512,128]{1,0:T(8,128)S(1)}) custom-call(bf16[512,256]{1,0:T(8,128)(2,1)S(1)} %copy-done.3, bf16[512,256]{1,0:T(8,128)(2,1)S(1)} %copy-done.5, f32[8,512]{1,0:T(8,128)S(1)} %get-tuple-element.55.refs_2_.refs_4_, ...), custom_call_target="tpu_custom_call", output_to_operand_aliasing={{0}: (7, {})} | custom-call | bytes 7380000 | tf_op jit(solution)/shard_map/pair/pallas_call | solution.py:310
  87.8 2.5 %input.2 = (bf16[512,1024]{1,0:T(8,128)(2,1)}, bf16[512,256]{1,0:T(8,128)(2,1)}, f32[16,512]{1,0:T(8,128)}) custom-call(f32[512,512]{1,0:T(8,128)S(1)} %get-tuple-element.86.refs_0_, f32[512,128]{1,0:T(8,128)S(1)} %get-tuple-element.87.refs_1_, bf16[512,128]{1,0:T(8,128)(2,1)S(1)} %get-tuple-element.88.refs_2_, f32[512,8]{1,0:T(8,128)S(1)} %get-tuple-element.63.refs_3_, ...), custom_call_target="tpu_custom_call" | custom-call | bytes 9225000 | tf_op jit(solution)/shard_map/input/pallas_call | solution.py:310
  90.3 2.1 %collective-permute-done.11.refs_8_ = f32[128,512]{1,0:T(8,128)S(1)} collective-permute-done((f32[128,512]{1,0:T(8,128)S(1)}, f32[128,512]{1,0:T(8,128)S(1)}, u32[]{:S(2)}, u32[]{:S(2)}) %collective-permute-start.11) | collective-permute-done | bytes 262176 | tf_op jit(solution)/shard_map/ppermute | solution.py:337
  92.4 2.5 %input.3 = (bf16[512,1024]{1,0:T(8,128)(2,1)}, bf16[512,256]{1,0:T(8,128)(2,1)}, f32[16,512]{1,0:T(8,128)}) custom-call(f32[512,512]{1,0:T(8,128)S(1)} %get-tuple-element.81.refs_0_, f32[512,128]{1,0:T(8,128)S(1)} %get-tuple-element.82.refs_1_, ...), custom_call_target="tpu_custom_call", output_to_operand_aliasing={{0}: (17, {}), {1}: (18, {}), {2}: (19, {})} | custom-call | bytes 9225000 | tf_op jit(solution)/shard_map/input/pallas_call | solution.py:310
  94.9 8.0 %collective-permute-done.19 = f32[64,1024]{1,0:T(8,128)S(1)} collective-permute-done((f32[64,1024]{1,0:T(8,128)S(1)}, f32[64,1024]{1,0:T(8,128)S(1)}, u32[]{:S(2)}, u32[]{:S(2)}) %collective-permute-start.19) | collective-permute-done | bytes 262176 | tf_op jit(solution)/shard_map/ppermute | solution.py:357
  (76 shorter events, 19.7 us)
Async XLA Ops:
  6.2 7.4 %copy-start.6 = (bf16[512,1024]{1,0:T(8,128)(2,1)S(1)}, bf16[512,1024]{1,0:T(8,128)(2,1)}, u32[]{:S(2)}) copy-start(bf16[512,1024]{1,0:T(8,128)(2,1)} %refs_3_.5) | copy-start | bytes 3145732
  6.2 7.4 %copy-start.9 = (bf16[64,1024]{1,0:T(8,128)(2,1)S(1)}, bf16[64,1024]{1,0:T(8,128)(2,1)}, u32[]{:S(2)}) copy-start(bf16[64,1024]{1,0:T(8,128)(2,1)} %refs_2_.5) | copy-start | bytes 393220
  6.2 12.1 %collective-permute-start.5 = (f32[136,512]{1,0:T(8,128)S(1)}, f32[136,512]{1,0:T(8,128)S(1)}, u32[]{:S(2)}, u32[]{:S(2)}) collective-permute-start(f32[136,512]{1,0:T(8,128)S(1)} %get-tuple-element.66), channel_id=1, source_target_pairs={{0,4},{8,12},{1,5},{9,13},{2,6},{10,14},{3,7},{11,15},{16,20},{24,... | collective-permute-start | bytes 835592 | tf_op jit(solution)/shard_map/ppermute | solution.py:333
  12.3 10.8 %collective-permute-start = (f32[136,512]{1,0:T(8,128)S(1)}, f32[136,512]{1,0:T(8,128)S(1)}, u32[]{:S(2)}, u32[]{:S(2)}) collective-permute-start(f32[136,512]{1,0:T(8,128)S(1)} %get-tuple-element.59), channel_id=1, source_target_pairs={{0,4},{8,12},{1,5},{9,13},{2,6},{10,14},{3,7},{11,15},{16,20},{24,... | collective-permute-start | bytes 835592 | tf_op jit(solution)/shard_map/ppermute | solution.py:333
  14.1 10.6 %collective-permute-start.3 = (f32[64,512]{1,0:T(8,128)S(1)}, f32[64,512]{1,0:T(8,128)S(1)}, u32[]{:S(2)}, u32[]{:S(2)}) collective-permute-start(f32[64,512]{1,0:T(8,128)S(1)} %rank.1), channel_id=1, source_target_pairs={{0,1},{1,0},{2,3},{3,2},{4,5},{5,4},{6,7},{7,6},{8,9},{9,8},{10,11... | collective-permute-start | bytes 393224 | tf_op jit(solution)/shard_map/ppermute | solution.py:357
  18.4 11.5 %copy-start.8 = (bf16[512,1024]{1,0:T(8,128)(2,1)S(1)}, bf16[512,1024]{1,0:T(8,128)(2,1)}, u32[]{:S(2)}) copy-start(bf16[512,1024]{1,0:T(8,128)(2,1)} %refs_11_.3) | copy-start | bytes 3145732
  18.4 11.4 %collective-permute-start.6 = (f32[128,512]{1,0:T(8,128)S(1)}, f32[128,512]{1,0:T(8,128)S(1)}, u32[]{:S(2)}, u32[]{:S(2)}) collective-permute-start(f32[128,512]{1,0:T(8,128)S(1)} %fusion.2), channel_id=1, source_target_pairs={{4,12},{5,13},{6,14},{7,15},{20,28},{21,29},{22,30},{23,31}} | collective-permute-start | bytes 786440 | tf_op jit(solution)/shard_map/ppermute | solution.py:337
  19.2 10.6 %collective-permute-start.7 = (f32[128,512]{1,0:T(8,128)S(1)}, f32[128,512]{1,0:T(8,128)S(1)}, u32[]{:S(2)}, u32[]{:S(2)}) collective-permute-start(f32[128,512]{1,0:T(8,128)S(1)} %fusion.2), channel_id=1, source_target_pairs={{4,8},{5,9},{6,10},{7,11},{20,24},{21,25},{22,26},{23,27}} | collective-permute-start | bytes 786440 | tf_op jit(solution)/shard_map/ppermute | solution.py:338
  23.2 12.6 %collective-permute-start.1 = (f32[128,512]{1,0:T(8,128)S(1)}, f32[128,512]{1,0:T(8,128)S(1)}, u32[]{:S(2)}, u32[]{:S(2)}) collective-permute-start(f32[128,512]{1,0:T(8,128)S(1)} %fusion.3), channel_id=1, source_target_pairs={{4,12},{5,13},{6,14},{7,15},{20,28},{21,29},{22,30},{23,31}} | collective-permute-start | bytes 786440 | tf_op jit(solution)/shard_map/ppermute | solution.py:337
  24.1 11.8 %collective-permute-start.2 = (f32[128,512]{1,0:T(8,128)S(1)}, f32[128,512]{1,0:T(8,128)S(1)}, u32[]{:S(2)}, u32[]{:S(2)}) collective-permute-start(f32[128,512]{1,0:T(8,128)S(1)} %fusion.3), channel_id=1, source_target_pairs={{4,8},{5,9},{6,10},{7,11},{20,24},{21,25},{22,26},{23,27}} | collective-permute-start | bytes 786440 | tf_op jit(solution)/shard_map/ppermute | solution.py:338
  24.8 5.0 %collective-permute-start.4 = (f32[64,512]{1,0:T(8,128)S(1)}, f32[64,512]{1,0:T(8,128)S(1)}, u32[]{:S(2)}, u32[]{:S(2)}) collective-permute-start(f32[64,512]{1,0:T(8,128)S(1)} %add.31.refs_12_), channel_id=1, source_target_pairs={{0,2},{2,0},{1,3},{3,1},{4,6},{6,4},{5,7},{7,5},{8,10},{10,8},{9,1... | collective-permute-start | bytes 393224 | tf_op jit(solution)/shard_map/ppermute | solution.py:357
  26.4 3.5 %copy-start.10 = (bf16[1024,64]{0,1:T(8,128)(2,1)S(1)}, bf16[1024,64]{0,1:T(8,128)(2,1)}, u32[]{:S(2)}) copy-start(bf16[1024,64]{0,1:T(8,128)(2,1)} %param.24) | copy-start | bytes 393220
  33.9 25.8 %collective-permute-start.13 = (f32[136,512]{1,0:T(8,128)S(1)}, f32[136,512]{1,0:T(8,128)S(1)}, u32[]{:S(2)}, u32[]{:S(2)}) collective-permute-start(f32[136,512]{1,0:T(8,128)S(1)} %get-tuple-element.89.refs_10_), channel_id=1, source_target_pairs={{12,8},{4,0},{13,9},{5,1},{14,10},{6,2},{15,11},{7,3},{28,24},{20,... | collective-permute-start | bytes 835592 | tf_op jit(solution)/shard_map/ppermute | solution.py:333
  39.2 16.8 %collective-permute-start.16 = (f32[64,1024]{1,0:T(8,128)S(1)}, f32[64,1024]{1,0:T(8,128)S(1)}, u32[]{:S(2)}, u32[]{:S(2)}) collective-permute-start(f32[64,1024]{1,0:T(8,128)S(1)} %get-tuple-element.99), channel_id=1, source_target_pairs={{0,4},{4,0},{8,12},{12,8},{1,5},{5,1},{9,13},{13,9},{2,6},{6,2},{1... | collective-permute-start | bytes 786440 | tf_op jit(solution)/shard_map/ppermute | solution.py:357
  50.0 1.3 %collective-permute-start.8 = (f32[64,512]{1,0:T(8,128)S(1)}, f32[64,512]{1,0:T(8,128)S(1)}, u32[]{:S(2)}, u32[]{:S(2)}) collective-permute-start(f32[64,512]{1,0:T(8,128)S(1)} %get-tuple-element.74), channel_id=1, source_target_pairs={{0,1},{1,0},{2,3},{3,2},{4,5},{5,4},{6,7},{7,6},{8,9},{9,8},{10,11... | collective-permute-start | bytes 393224 | tf_op jit(solution)/shard_map/ppermute | solution.py:357
  51.3 6.4 %collective-permute-start.9 = (f32[64,512]{1,0:T(8,128)S(1)}, f32[64,512]{1,0:T(8,128)S(1)}, u32[]{:S(2)}, u32[]{:S(2)}) collective-permute-start(f32[64,512]{1,0:T(8,128)S(1)} %add.33.refs_0_), channel_id=1, source_target_pairs={{0,2},{2,0},{1,3},{3,1},{4,6},{6,4},{5,7},{7,5},{8,10},{10,8},{9,1... | collective-permute-start | bytes 393224 | tf_op jit(solution)/shard_map/ppermute | solution.py:357
  52.9 21.8 %collective-permute-start.10 = (f32[136,512]{1,0:T(8,128)S(1)}, f32[136,512]{1,0:T(8,128)S(1)}, u32[]{:S(2)}, u32[]{:S(2)}) collective-permute-start(f32[136,512]{1,0:T(8,128)S(1)} %get-tuple-element.84.refs_10_), channel_id=1, source_target_pairs={{12,8},{4,0},{13,9},{5,1},{14,10},{6,2},{15,11},{7,3},{28,24},{20,... | collective-permute-start | bytes 835592 | tf_op jit(solution)/shard_map/ppermute | solution.py:333
  56.1 25.2 %collective-permute-start.17 = (f32[64,1024]{1,0:T(8,128)S(1)}, f32[64,1024]{1,0:T(8,128)S(1)}, u32[]{:S(2)}, u32[]{:S(2)}) collective-permute-start(f32[64,1024]{1,0:T(8,128)S(1)} %add.36), channel_id=1, source_target_pairs={{0,8},{4,12},{8,0},{12,4},{1,9},{5,13},{9,1},{13,5},{2,10},{6,14},... | collective-permute-start | bytes 786440 | tf_op jit(solution)/shard_map/ppermute | solution.py:357
  59.1 21.2 %collective-permute-start.18 = (f32[64,1024]{1,0:T(8,128)S(1)}, f32[64,1024]{1,0:T(8,128)S(1)}, u32[]{:S(2)}, u32[]{:S(2)}) collective-permute-start(f32[64,1024]{1,0:T(8,128)S(1)} %get-tuple-element.100), channel_id=1, source_target_pairs={{0,4},{4,0},{8,12},{12,8},{1,5},{5,1},{9,13},{13,9},{2,6},{6,2},{1... | collective-permute-start | bytes 786440 | tf_op jit(solution)/shard_map/ppermute | solution.py:357
  59.7 28.1 %collective-permute-start.14 = (f32[128,512]{1,0:T(8,128)S(1)}, f32[128,512]{1,0:T(8,128)S(1)}, u32[]{:S(2)}, u32[]{:S(2)}) collective-permute-start(f32[128,512]{1,0:T(8,128)S(1)} %fusion), channel_id=1, source_target_pairs={{8,0},{9,1},{10,2},{11,3},{24,16},{25,17},{26,18},{27,19}} | collective-permute-start | bytes 786440 | tf_op jit(solution)/shard_map/ppermute | solution.py:337
  61.0 26.8 %collective-permute-start.15 = (f32[128,512]{1,0:T(8,128)S(1)}, f32[128,512]{1,0:T(8,128)S(1)}, u32[]{:S(2)}, u32[]{:S(2)}) collective-permute-start(f32[128,512]{1,0:T(8,128)S(1)} %fusion), channel_id=1, source_target_pairs={{8,4},{9,5},{10,6},{11,7},{24,20},{25,21},{26,22},{27,23}} | collective-permute-start | bytes 786440 | tf_op jit(solution)/shard_map/ppermute | solution.py:338
  74.7 17.7 %collective-permute-start.11 = (f32[128,512]{1,0:T(8,128)S(1)}, f32[128,512]{1,0:T(8,128)S(1)}, u32[]{:S(2)}, u32[]{:S(2)}) collective-permute-start(f32[128,512]{1,0:T(8,128)S(1)} %fusion.1), channel_id=1, source_target_pairs={{8,0},{9,1},{10,2},{11,3},{24,16},{25,17},{26,18},{27,19}} | collective-permute-start | bytes 786440 | tf_op jit(solution)/shard_map/ppermute | solution.py:337
  80.3 12.0 %collective-permute-start.12 = (f32[128,512]{1,0:T(8,128)S(1)}, f32[128,512]{1,0:T(8,128)S(1)}, u32[]{:S(2)}, u32[]{:S(2)}) collective-permute-start(f32[128,512]{1,0:T(8,128)S(1)} %fusion.1), channel_id=1, source_target_pairs={{8,4},{9,5},{10,6},{11,7},{24,20},{25,21},{26,22},{27,23}} | collective-permute-start | bytes 786440 | tf_op jit(solution)/shard_map/ppermute | solution.py:338
  81.2 21.6 %collective-permute-start.19 = (f32[64,1024]{1,0:T(8,128)S(1)}, f32[64,1024]{1,0:T(8,128)S(1)}, u32[]{:S(2)}, u32[]{:S(2)}) collective-permute-start(f32[64,1024]{1,0:T(8,128)S(1)} %add.38), channel_id=1, source_target_pairs={{0,8},{4,12},{8,0},{12,4},{1,9},{5,13},{9,1},{13,5},{2,10},{6,14},... | collective-permute-start | bytes 786440 | tf_op jit(solution)/shard_map/ppermute | solution.py:357
  (13 other events, 20.6 us)
where the time goes:
time: 104 us
  waiting for transfers between devices  40.7 us (39%)
  starting transfers between devices  34.3 us (33%)
  Pallas kernels  20.5 us (20%)
  local copies, waits for them, and re-layouts  5.24 us (5%)
  other arithmetic  1.77 us (2%)
    pallas_call x12, Pallas kernels, call(): pl.pallas_call(body, grid=(1,), in_specs=in_specs, out_specs=out_specs, o...  20.5 us
    ppermute x4, waiting for transfers between devices, passed_on(): near = lax.ppermute(part, axis, pairs)  20.4 us
    ppermute x8, starting transfers between devices, exchange_pair(): other = lax.ppermute(part, axis, [(i, i ^ span) for i in range(count)])  18.3 us
    ppermute x8, waiting for transfers between devices, exchange_pair(): other = lax.ppermute(part, axis, [(i, i ^ span) for i in range(count)])  18.3 us
    ppermute x4, starting transfers between devices, passed_on(): near = lax.ppermute(part, axis, pairs)  8.94 us
    unnamed x34, local copies, waits for them, and re-layouts  5.22 us
    ppermute x4, starting transfers between devices, passed_on(): lax.ppermute(joined, axis, [(source, far)])  4.2 us
    ppermute x4, starting transfers between devices, passed_on(): lax.ppermute(joined, axis, [(source, mid)])  2.88 us
  transfers between devices with their start and end apart: 20, of which 9 were waited for; matrix products, arithmetic and copies ran while one was open for 1% of the time, Pallas kernels for 19%

commit v1 on v0

--- a/solution.py
+++ b/solution.py
@@ -12,7 +12,8 @@
 ROWS = 32
 EPS = 1e-05
 SCALE = 2.0
-VMEM = 32 * 2**20
+VMEM = 18 * 2**20
+COST = 3.69e6
 
 f32 = jnp.float32
 bf16 = jnp.bfloat16
@@ -110,8 +111,7 @@
     from_start = id_cols[:, :1] == 0
     bend[...] = jnp.where(to_end, b[...].astype(f32), 0.0).astype(bf16)
     cstart[...] = jnp.where(from_start, c[...].astype(f32), 0.0).astype(bf16)
-    state[0:STATE] = dot(bend[...], xw[...], 0, 0) * half_row
-    state[STATE:] = jnp.broadcast_to(total, (8, channels))
+    state[...] = dot(bend[...], xw[...], 0, 0) * half_row
 
 
 def score_kernel(b, c, ids_row, ids_col, xw, y_loc):
@@ -135,7 +135,7 @@
 
 
 def gather_incoming(near, far, mid):
-    return near[0:STATE] + near[STATE : STATE + 1] * far[...] + mid[...]
+    return near[...] + far[...] + mid[...]
 
 
 def norm_kernel(*refs, first):
@@ -182,8 +182,7 @@
         return carry
 
     lax.fori_loop(0, length // ROWS, tile, 0, unroll=4)
-    state_grad[0:STATE] = dot(cstart[...], gye[...], 0, 0) * rows[1:2]
-    state_grad[STATE:] = jnp.broadcast_to(rows[0:1], (8, channels))
+    state_grad[...] = dot(cstart[...], gye[...], 0, 0) * rows[1:2]
     u_here = dot(down[...], mixed[...], 1, 1)
     u_part[...] = u_here if first == 0 else u_here + u_before[...]
     down_part[...] = dot(gu, mixed[...], 1, 0)
@@ -266,7 +265,7 @@
     ones = places.astype(bf16)
     x_dot = dot(ones, product[0], 1, 1) + dot(ones, product[1], 1, 1)
     crossing = jnp.sum(
-        (rows[0:1] * incoming + grad_dev[0:STATE]) * scaled_in[...].astype(f32), axis=0, keepdims=True
+        (rows[0:1] * incoming + grad_dev[...]) * scaled_in[...].astype(f32), axis=0, keepdims=True
     ) / rows[1:2]
     constant = jnp.sum(jnp.where(places, crossing, 0.0), axis=1, keepdims=True)
     g_log = running_sum(x_dot - y_dot[...], True) + constant
@@ -280,6 +279,25 @@
     up_part[...] = dot(u, lo[...], 1, 0)
 
 
+def adapter_halves_kernel(odd, u_here, u_there, up, lo, down_part, out, up_keep, up_send, down_keep, down_send):
+    u = (SCALE * (u_here[...] + u_there[...])).astype(bf16)
+    out[...] = dot(u, up[...], 0, 0).astype(bf16)
+    up_part = dot(u, lo[...], 1, 0)
+    rows = up_keep.shape[0]
+    is_odd = odd[0] == 1
+    for keep, send, part in ((up_keep, up_send, up_part), (down_keep, down_send, down_part[...])):
+        keep[...] = jnp.where(is_odd, part[rows:], part[:rows])
+        send[...] = jnp.where(is_odd, part[:rows], part[rows:])
+
+
+def join_kernel(odd, *refs):
+    is_odd = odd[0] == 1
+    for keep, other, out in (refs[0:2] + refs[4:5], refs[2:4] + refs[5:6]):
+        rows = keep.shape[0]
+        out[:rows] = jnp.where(is_odd, other[...], keep[...])
+        out[rows:] = jnp.where(is_odd, keep[...], other[...])
+
+
 def rank_kernel(up, lo, part):
     part[...] = dot(up[...], lo[...], 1, 1)
 
@@ -287,6 +305,10 @@
 def call(kernel, ins, outs, scratch=(), cost=1.0, name=None):
     in_specs, operands = [], []
     for array, block, index in ins:
+        if block == "scalar":
+            in_specs.append(pl.BlockSpec(memory_space=pltpu.SMEM))
+            operands.append(array)
+            continue
         if block is None:
             block, index = array.shape, (0,) * array.ndim
         in_specs.append(pl.BlockSpec(block, functools.partial(lambda at, i: at, index)))
@@ -317,34 +339,29 @@
         input_output_aliases=aliases,
         compiler_params=pltpu.CompilerParams(vmem_limit_bytes=VMEM),
         cost_estimate=pl.CostEstimate(
-            flops=0, bytes_accessed=int(cost * 3.69e6), transcendentals=0
+            flops=0, bytes_accessed=int(cost * COST), transcendentals=0
         ),
         name=name,
     )(*operands)
 
 
-def passed_on(part, axis, reverse):
+def after(value, *others):
+    return lax.optimization_barrier((value, *others))[0]
+
+
+def hop(part, axis, *pairs):
+    return lax.ppermute(part, axis, list(pairs))
+
+
+def chain(state, decay, axis, reverse):
     count = lax.axis_size(axis)
-    state = part[:STATE]
-    decay = part[STATE : STATE + 1]
-    if count == 4:
-        pairs = [(3, 2), (1, 0)] if reverse else [(0, 1), (2, 3)]
-        source, far, mid = (2, 0, 1) if reverse else (1, 3, 2)
-        near = lax.ppermute(part, axis, pairs)
-        joined = decay * near[:STATE] + state
-        return (
-            near,
-            lax.ppermute(joined, axis, [(source, far)]),
-            lax.ppermute(joined, axis, [(source, mid)]),
-        )
     incoming = jnp.zeros_like(state)
     out = state
-    for hop in range(count - 1):
-        pair = (count - 1 - hop, count - 2 - hop) if reverse else (hop, hop + 1)
-        got = lax.ppermute(out, axis, [pair])
+    for at in range(count - 1):
+        got = hop(out, axis, (count - 1 - at, count - 2 - at) if reverse else (at, at + 1))
         incoming = incoming + got
         out = state + decay * got
-    return jnp.concatenate([incoming, jnp.zeros_like(part[STATE:])]), incoming, jnp.zeros_like(state)
+    return incoming, jnp.zeros_like(state), jnp.zeros_like(state)
 
 
 def exchange_pair(part, axes):
@@ -404,62 +421,103 @@
     def fresh(shape, dtype):
         return (shape, dtype, None, None, None)
 
-    states = []
-    for g in range(groups):
-        states.append(
-            call(
-                functools.partial(state_kernel, first=g * heads),
-                [
-                    cols(mixer_input_channels, g),
-                    cols(input_group_maps, g),
-                    cols(output_group_maps, g),
-                    head_rows(step_size_input, g),
-                    whole(resets),
-                    whole(rates),
-                    whole(biases),
-                ],
-                [
-                    fresh((length, width), bf16),
-                    fresh((STATE + 8, width), f32),
-                    fresh((length, STATE), bf16),
-                    fresh((length, STATE), bf16),
-                    fresh((4 * heads, length), f32),
-                    fresh((8, width), f32),
-                    fresh((8, length), f32),
-                    fresh((length, 8), f32),
-                ],
-                cost=1.5,
-                name="state",
-            )
+    everything = range(groups)
+    short = lax.axis_size("ctx") == 4
+
+    def state_call(g, rates):
+        return call(
+            functools.partial(state_kernel, first=g * heads),
+            [
+                cols(mixer_input_channels, g),
+                cols(input_group_maps, g),
+                cols(output_group_maps, g),
+                head_rows(step_size_input, g),
+                whole(resets),
+                whole(rates),
+                whole(biases),
+            ],
+            [
+                fresh((length, width), bf16),
+                fresh((STATE, width), f32),
+                fresh((length, STATE), bf16),
+                fresh((length, STATE), bf16),
+                fresh((4 * heads, length), f32),
+                fresh((8, width), f32),
+                fresh((8, length), f32),
+                fresh((length, 8), f32),
+            ],
+            cost=1.5,
+            name="state",
         )
+
+    def score_call(g):
+        xw, _, _, _, _, _, ids_row, ids_col = states[g]
+        return call(
+            score_kernel,
+            [
+                cols(input_group_maps, g),
+                cols(output_group_maps, g),
+                whole(ids_row),
+                whole(ids_col),
+                whole(xw),
+            ],
+            [fresh((length, width), f32)],
+            cost=1.0,
+            name="score",
+        )[0]
+
+    states, y_locs = [], []
+    for g in everything:
+        states.append(state_call(g, after(rates, y_locs[-1]) if g else rates))
+        y_locs.append(score_call(g))
     (gu_part,) = call(
         rank_kernel,
-        [whole(adapter_up_map), whole(layer_output_gradient)],
+        [whole(after(adapter_up_map, states[0][5])), whole(layer_output_gradient)],
         [fresh((rank, length), f32)],
         cost=1.0,
         name="rank",
     )
     gu = exchange_pair(gu_part, ("fsdp", "head"))
-    y_locs = []
-    for g in range(groups):
-        xw, _, _, _, _, _, ids_row, ids_col = states[g]
-        y_locs += call(
-            score_kernel,
+    parts = [states[g][1] for g in everything]
+    decays = [states[g][5][0:1] for g in everything]
+    entering = []
+    if short:
+        first = [hop(parts[0], "ctx", (0, 1))]
+        for g in range(1, groups):
+            first.append(hop(after(parts[g], first[-1]), "ctx", (0, 1)))
+        for g in everything:
+            joined = after(decays[g], parts[-1], gu[0]) * first[g] + parts[g]
+            second = hop(joined, "ctx", (1, 2))
+            joined = after(decays[g], y_locs[-1], gu[1]) * second + parts[g]
+            entering.append((first[g], second, hop(joined, "ctx", (2, 3))))
+    else:
+        entering = [chain(parts[g], decays[g], "ctx", False) for g in everything]
+    mixed = gate_grad = down_part = u_part = c_grad = None
+    normed, pairs = [], []
+
+    def pair_call(g, held, *others):
+        xw, state, bend, cstart, small, rows, ids_row, ids_col = states[g]
+        return call(
+            pair_kernel,
             [
                 cols(input_group_maps, g),
                 cols(output_group_maps, g),
-                whole(ids_row),
+                whole(after(ids_row, *others) if others else ids_row),
                 whole(ids_col),
                 whole(xw),
-            ],
-            [fresh((length, width), f32)],
-            cost=1.0,
-            name="score",
+                whole(normed[g][0]),
+                whole(normed[g][1]),
+            ],
+            [
+                ((length, groups * STATE), bf16, (length, STATE), (0, g), held),
+                fresh((length, width), f32),
+                fresh((length, STATE), f32),
+            ],
+            cost=2.0,
+            name="pair",
         )
-    entering = [passed_on(states[g][1], "ctx", False) for g in range(groups)]
-    mixed = gate_grad = down_part = u_part = None
-    normed = []
-    for g in range(groups):
+
+    for g in everything:
         xw, state, bend, cstart, small, rows, ids_row, ids_col = states[g]
         results = call(
             functools.partial(norm_kernel, first=g * heads),
@@ -484,7 +542,7 @@
                 ((rank, channels), f32, (rank, width), (0, g), down_part),
                 fresh((length, width), bf16),
                 fresh((STATE, width), bf16),
-                fresh((STATE + 8, width), f32),
+                fresh((STATE, width), f32),
                 fresh((rank, length), f32),
                 fresh((heads, length), f32),
             ],
@@ -499,43 +557,67 @@
         )
         mixed, gate_grad, down_part, gye, scaled, state_grad, u_part, y_dot = results
         normed.append((gye, scaled, state_grad, y_dot))
-    leaving = [passed_on(normed[g][2], "ctx", True) for g in range(groups)]
+    leaving = []
+    if short:
+        last = [hop(normed[g][2], "ctx", (3, 2)) for g in everything]
+        joined = after(decays[0], u_part) * last[0] + normed[0][2]
+        then = [hop(joined, "ctx", (2, 1))]
     u = exchange_pair(u_part, ("fsdp", "head"))
-    c_grad = None
-    pairs = []
-    for g in range(groups):
-        xw, state, bend, cstart, small, rows, ids_row, ids_col = states[g]
-        c_grad, z_loc, b_loc = call(
-            pair_kernel,
-            [
-                cols(input_group_maps, g),
-                cols(output_group_maps, g),
-                whole(ids_row),
-                whole(ids_col),
-                whole(xw),
-                whole(normed[g][0]),
-                whole(normed[g][1]),
-            ],
-            [
-                ((length, groups * STATE), bf16, (length, STATE), (0, g), c_grad),
-                fresh((length, width), f32),
-                fresh((length, STATE), f32),
-            ],
-            cost=2.0,
-            name="pair",
+    half = fresh((rank // 2, channels), f32)
+    if short:
+        odd = (lax.axis_index("ctx") % 2).reshape(1)
+        adapter_output, *halves = call(
+            adapter_halves_kernel,
+            [
+                (odd, "scalar", None),
+                *map(whole, u),
+                whole(adapter_up_map),
+                whole(layer_output_gradient),
+                whole(down_part),
+            ],
+            [fresh((length, channels), bf16), half, half, half, half],
+            cost=1.5,
+            name="adapter",
         )
+    else:
+        adapter_output, up_part = call(
+            adapter_kernel,
+            [*map(whole, u), whole(adapter_up_map), whole(layer_output_gradient)],
+            [fresh((length, channels), bf16), fresh((rank, channels), f32)],
+            cost=1.5,
+            name="adapter",
+        )
+    if short:
+        for g in range(1, groups):
+            joined = after(decays[g], halves[0]) * last[g] + normed[g][2]
+            then.append(hop(joined, "ctx", (2, 1)))
+    for g in everything:
+        c_grad, z_loc, b_loc = pair_call(g, c_grad, *([joined] if short else []))
         pairs.append((z_loc, b_loc))
-    down_sum = exchange_sum(down_part, ("ctx",))
-    adapter_output, up_part = call(
-        adapter_kernel,
-        [*map(whole, u), whole(adapter_up_map), whole(layer_output_gradient)],
-        [fresh((length, channels), bf16), fresh((rank, channels), f32)],
-        cost=1.5,
-        name="adapter",
-    )
-    up_sum = exchange_sum(up_part, ("ctx",))
+    if short:
+        for g in everything:
+            joined = after(decays[g], pairs[-1][1]) * then[g] + normed[g][2]
+            leaving.append((last[g], then[g], hop(joined, "ctx", (1, 0))))
+        neighbours = [(0, 1), (1, 0), (2, 3), (3, 2)]
+        across = [(0, 2), (2, 0), (1, 3), (3, 1)]
+        ends = []
+        for keep, send in (halves[:2], halves[2:]):
+            keep = keep + hop(send, "ctx", *neighbours)
+            got = hop(keep, "ctx", *across)
+            keep = after(keep, joined) + got
+            ends += [keep, hop(keep, "ctx", *neighbours)]
+        up_sum, down_sum = call(
+            join_kernel,
+            [(odd, "scalar", None), *map(whole, ends)],
+            [fresh((rank, channels), f32), fresh((rank, channels), f32)],
+            name="join",
+        )
+    else:
+        up_sum = exchange_sum(up_part, ("ctx",))
+        down_sum = exchange_sum(down_part, ("ctx",))
+        leaving = [chain(normed[g][2], decays[g], "ctx", True) for g in everything]
     x_grad = b_grad = step_grad = None
-    for g in range(groups):
+    for g in everything:
         xw, state, bend, cstart, small, rows, ids_row, ids_col = states[g]
         x_grad, b_grad, step_grad = call(
             functools.partial(input_kernel, first=g * heads),

time: 104 us -> 97 us (0.933)
  waiting for transfers between devices: 40.7 us -> 20.1 us
  local copies, waits for them, and re-layouts: 5.24 us -> 11.2 us
  Pallas kernels: 20.5 us -> 23.3 us
  other arithmetic: 1.77 us -> 4.48 us
  starting transfers between devices: 34.3 us -> 35.8 us
    ppermute x12 -> x18, starting transfers between devices: 16 us -> 32.6 us  [hop(): return lax.ppermute(part, axis, list(pairs))]
    ppermute x8 -> x4, waiting for transfers between devices: 18.3 us -> 2.6 us  [exchange_pair(): other = lax.ppermute(part, axis, [(i, i ^ span) for i in range(count)])]
    ppermute x8 -> x4, starting transfers between devices: 18.3 us -> 3.2 us  [exchange_pair(): other = lax.ppermute(part, axis, [(i, i ^ span) for i in range(count)])]
    unnamed x34 -> x102, local copies, waits for them, and re-layouts: 5.22 us -> 11.2 us
    ppermute x12 -> x18, waiting for transfers between devices: 22.5 us -> 17.5 us  [hop(): return lax.ppermute(part, axis, list(pairs))]
    pallas_call x12 -> x13, Pallas kernels: 20.5 us -> 23.3 us  [call(): pl.pallas_call(body, grid=(1,), in_specs=in_specs, out_specs=out_specs, o...]
    add x5 -> x12, other arithmetic: 0.93 us -> 3.46 us  [the longest x1 1.11 us: per_device(): joined = after(decays[0], u_part) * last[0] + normed[0][2]]
  transfers between devices with their start and end apart: 20 -> 22, of which waited for: 9 -> 8; matrix products, arithmetic and copies ran while one was open for 1% -> 5% of each run, Pallas kernels for 19% -> 20%
where the time goes in v1:
time: 97 us; the launch traced here: 96.2 us
  starting transfers between devices  35.8 us (37%)
  Pallas kernels  23.3 us (24%)
  waiting for transfers between devices  20.1 us (21%)
  local copies, waits for them, and re-layouts  11.2 us (12%)
  other arithmetic  4.48 us (5%)
  between operations  1.25 us (1%)
    ppermute x18, starting transfers between devices, hop(): return lax.ppermute(part, axis, list(pairs))  32.6 us
    pallas_call x13, Pallas kernels, call(): pl.pallas_call(body, grid=(1,), in_specs=in_specs, out_specs=out_specs, o...  23.3 us
    ppermute x18, waiting for transfers between devices, hop(): return lax.ppermute(part, axis, list(pairs))  17.5 us
    unnamed x102, local copies, waits for them, and re-layouts  11.2 us
    ppermute x4, starting transfers between devices, exchange_pair(): other = lax.ppermute(part, axis, [(i, i ^ span) for i in range(count)])  3.2 us
    ppermute x4, waiting for transfers between devices, exchange_pair(): other = lax.ppermute(part, axis, [(i, i ^ span) for i in range(count)])  2.6 us
  transfers between devices with their start and end apart: 22, of which 8 were waited for; matrix products, arithmetic and copies ran while one was open for 5% of the time, Pallas kernels for 20%

profile of v1, /device:TPU:0, one launch (start us, length us, event | category | flops | bytes accessed | tf_op | source)
XLA Modules:
  0.0 96.2 jit_solution(5650394250945192291)
XLA Ops:
  6.3 4.9 %collective-permute-start = (f32[128,512]{1,0:T(8,128)S(1)}, f32[128,512]{1,0:T(8,128)S(1)}, u32[]{:S(2)}, u32[]{:S(2)}) collective-permute-start(f32[128,512]{1,0:T(8,128)S(1)} %get-tuple-element.84), channel_id=1, source_target_pairs={{0,4},{1,5},{2,6},{3,7},{16,20},{17,21},{18,22},{19,23}} | collective-permute-start | bytes 786440 | tf_op jit(solution)/shard_map/ppermute | solution.py:353
  14.5 2.2 %collective-permute-done.refs_2_ = f32[128,512]{1,0:T(8,128)S(1)} collective-permute-done((f32[128,512]{1,0:T(8,128)S(1)}, f32[128,512]{1,0:T(8,128)S(1)}, u32[]{:S(2)}, u32[]{:S(2)}) %collective-permute-start) | collective-permute-done | bytes 262176 | tf_op jit(solution)/shard_map/ppermute | solution.py:353
  16.7 4.4 %collective-permute-start.1 = (f32[128,512]{1,0:T(8,128)S(1)}, f32[128,512]{1,0:T(8,128)S(1)}, u32[]{:S(2)}, u32[]{:S(2)}) collective-permute-start(f32[128,512]{1,0:T(8,128)S(1)} %get-tuple-element.85), channel_id=1, source_target_pairs={{0,4},{1,5},{2,6},{3,7},{16,20},{17,21},{18,22},{19,23}} | collective-permute-start | bytes 786440 | tf_op jit(solution)/shard_map/ppermute | solution.py:353
  21.2 1.6 %collective-permute-start.4 = (f32[64,512]{1,0:T(8,128)S(1)}, f32[64,512]{1,0:T(8,128)S(1)}, u32[]{:S(2)}, u32[]{:S(2)}) collective-permute-start(f32[64,512]{1,0:T(8,128)S(1)} %add.46.refs_12_), channel_id=1, source_target_pairs={{0,2},{2,0},{1,3},{3,1},{4,6},{6,4},{5,7},{7,5},{8,10},{10,8},{9,1... | collective-permute-start | bytes 393224 | tf_op jit(solution)/shard_map/ppermute | solution.py:374
  23.5 2.3 %collective-permute-done.1.refs_2_ = f32[128,512]{1,0:T(8,128)S(1)} collective-permute-done((f32[128,512]{1,0:T(8,128)S(1)}, f32[128,512]{1,0:T(8,128)S(1)}, u32[]{:S(2)}, u32[]{:S(2)}) %collective-permute-start.1) | collective-permute-done | bytes 262176 | tf_op jit(solution)/shard_map/ppermute | solution.py:353
  29.6 3.4 %norm.2 = (bf16[512,1024]{1,0:T(8,128)(2,1)}, bf16[512,1024]{1,0:T(8,128)(2,1)}, f32[64,1024]{1,0:T(8,128)S(1)}, bf16[512,512]{1,0:T(8,128)(2,1)S(1)}, bf16[128,...) custom-call(f32[512,512]{1,0:T(8,128)S(1)} %score.2.refs_0_, ...), custom_call_target="tpu_custom_call" | custom-call | bytes 14760000 | tf_op jit(solution)/shard_map/norm/pallas_call | solution.py:332
  34.5 1.4 %collective-permute-start.13 = (f32[128,512]{1,0:T(8,128)}, f32[128,512]{1,0:T(8,128)}, u32[]{:S(2)}, u32[]{:S(2)}) collective-permute-start(f32[128,512]{1,0:T(8,128)} %get-tuple-element.122.refs_10_), channel_id=1, source_target_pairs={{12,8},{13,9},{14,10},{15,11},{28,24},{29,25},{30,26},{31,27}} | collective-permute-start | bytes 786440 | tf_op jit(solution)/shard_map/ppermute | solution.py:353
  35.9 3.4 %norm.3 = (bf16[512,1024]{1,0:T(8,128)(2,1)}, bf16[512,1024]{1,0:T(8,128)(2,1)}, f32[64,1024]{1,0:T(8,128)S(1)}, bf16[512,512]{1,0:T(8,128)(2,1)S(1)}, bf16[128,...) custom-call(f32[512,512]{1,0:T(8,128)S(1)} %score.3.refs_0_, ...), custom_call_target="tpu_custom_call", output_to_operand_aliasing={{0}: (16, {}), {1}: (17, {}), {2}: (18, {})} | custom-call | bytes 14760000 | tf_op jit(solution)/shard_map/norm/pallas_call | solution.py:332
  42.0 1.4 %collective-permute-start.10 = (f32[128,512]{1,0:T(8,128)S(1)}, f32[128,512]{1,0:T(8,128)}, u32[]{:S(2)}, u32[]{:S(2)}) collective-permute-start(f32[128,512]{1,0:T(8,128)S(1)} %get-tuple-element.106.refs_10_), channel_id=1, source_target_pairs={{12,8},{13,9},{14,10},{15,11},{28,24},{29,25},{30,26},{31,27}} | collective-permute-start | bytes 786440 | tf_op jit(solution)/shard_map/ppermute | solution.py:353
  44.7 1.6 %collective-permute-start.9 = (f32[64,512]{1,0:T(8,128)S(1)}, f32[64,512]{1,0:T(8,128)S(1)}, u32[]{:S(2)}, u32[]{:S(2)}) collective-permute-start(f32[64,512]{1,0:T(8,128)S(1)} %add.52.refs_1_), channel_id=1, source_target_pairs={{0,2},{2,0},{1,3},{3,1},{4,6},{6,4},{5,7},{7,5},{8,10},{10,8},{9,1... | collective-permute-start | bytes 393224 | tf_op jit(solution)/shard_map/ppermute | solution.py:374
  48.1 2.3 %collective-permute-done.9.refs_2_ = f32[64,512]{1,0:T(8,128)S(1)} collective-permute-done((f32[64,512]{1,0:T(8,128)S(1)}, f32[64,512]{1,0:T(8,128)S(1)}, u32[]{:S(2)}, u32[]{:S(2)}) %collective-permute-start.9) | collective-permute-done | bytes 131104 | tf_op jit(solution)/shard_map/ppermute | solution.py:374
  50.4 1.5 %adapter.1 = (bf16[512,1024]{1,0:T(8,128)(2,1)}, f32[32,1024]{1,0:T(8,128)S(1)}, f32[32,1024]{1,0:T(8,128)S(1)}, f32[32,1024]{1,0:T(8,128)S(1)}, f32[32,1024]{1,0:T(8,128)S(1)}) custom-call(s32[1]{0:T(128)} %bitcast.10.refs_0_, f32[64,512]{1,0:T(8,128)S(1)} %add.52.refs_1_, f32[64,512]{1,0:T(8,128)S(1)} %collective-permute-done.9.refs_2_, ...), custom_call_target="tpu_custom_call" | custom-call | bytes 5535000 | tf_op jit(solution)/shard_map/adapter/pallas_call | solution.py:332
  53.6 6.5 %collective-permute-start.16 = (f32[32,1024]{1,0:T(8,128)S(1)}, f32[32,1024]{1,0:T(8,128)S(1)}, u32[]{:S(2)}, u32[]{:S(2)}) collective-permute-start(f32[32,1024]{1,0:T(8,128)S(1)} %get-tuple-element.134), channel_id=1, source_target_pairs={{0,4},{4,0},{8,12},{12,8},{1,5},{5,1},{9,13},{13,9},{2,6},{6,2},{1... | collective-permute-start | bytes 393224 | tf_op jit(solution)/shard_map/ppermute | solution.py:353
  60.2 1.6 %pair.2 = (bf16[512,256]{1,0:T(8,128)(2,1)}, f32[512,512]{1,0:T(8,128)S(1)}, f32[512,128]{1,0:T(8,128)S(1)}) custom-call(bf16[512,256]{1,0:T(8,128)(2,1)S(1)} %copy-done.3, bf16[512,256]{1,0:T(8,128)(2,1)S(1)} %copy-done.5, f32[8,512]{1,0:T(8,128)S(1)} %copy-done.26, f32[512,8]{1,0:T(8,128)S(1)} %get-tuple-element.76.refs_3_, ...), custom_call_target="tpu_custom_call" | custom-call | bytes 7380000 | tf_op jit(solution)/shard_map/pair/pallas_call | solution.py:332
  61.8 2.0 %pair.3 = (bf16[512,256]{1,0:T(8,128)(2,1)}, f32[512,512]{1,0:T(8,128)S(1)}, f32[512,128]{1,0:T(8,128)S(1)}) custom-call(bf16[512,256]{1,0:T(8,128)(2,1)S(1)} %copy-done.3, bf16[512,256]{1,0:T(8,128)(2,1)S(1)} %copy-done.5, f32[8,512]{1,0:T(8,128)S(1)} %get-tuple-element.107.refs_2_.refs_4_, ...), custom_call_target="tpu_custom_call", output_to_operand_aliasing={{0}: (7, {})} | custom-call | bytes 7380000 | tf_op jit(solution)/shard_map/pair/pallas_call | solution.py:332
  64.8 1.3 %collective-permute-start.15 = (f32[128,512]{1,0:T(8,128)S(1)}, f32[128,512]{1,0:T(8,128)S(1)}, u32[]{:S(2)}, u32[]{:S(2)}) collective-permute-start(f32[128,512]{1,0:T(8,128)S(1)} %multiply_add_fusion), channel_id=1, source_target_pairs={{4,0},{5,1},{6,2},{7,3},{20,16},{21,17},{22,18},{23,19}} | collective-permute-start | bytes 786440 | tf_op jit(solution)/shard_map/ppermute | solution.py:353
  66.2 5.7 %collective-permute-start.17 = (f32[32,1024]{1,0:T(8,128)S(1)}, f32[32,1024]{1,0:T(8,128)S(1)}, u32[]{:S(2)}, u32[]{:S(2)}) collective-permute-start(f32[32,1024]{1,0:T(8,128)S(1)} %add.57), channel_id=1, source_target_pairs={{0,8},{8,0},{4,12},{12,4},{1,9},{9,1},{5,13},{13,5},{2,10},{10,2},... | collective-permute-start | bytes 393224 | tf_op jit(solution)/shard_map/ppermute | solution.py:353
  72.7 1.5 %collective-permute-start.12 = (f32[128,512]{1,0:T(8,128)S(1)}, f32[128,512]{1,0:T(8,128)S(1)}, u32[]{:S(2)}, u32[]{:S(2)}) collective-permute-start(f32[128,512]{1,0:T(8,128)S(1)} %multiply_add_fusion.2), channel_id=1, source_target_pairs={{4,0},{5,1},{6,2},{7,3},{20,16},{21,17},{22,18},{23,19}} | collective-permute-start | bytes 786440 | tf_op jit(solution)/shard_map/ppermute | solution.py:353
  74.1 7.4 %collective-permute-done.17 = f32[32,1024]{1,0:T(8,128)S(1)} collective-permute-done((f32[32,1024]{1,0:T(8,128)S(1)}, f32[32,1024]{1,0:T(8,128)S(1)}, u32[]{:S(2)}, u32[]{:S(2)}) %collective-permute-start.17) | collective-permute-done | bytes 131104 | tf_op jit(solution)/shard_map/ppermute | solution.py:353
  81.6 1.8 %collective-permute-done.20 = f32[32,1024]{1,0:T(8,128)S(1)} collective-permute-done((f32[32,1024]{1,0:T(8,128)S(1)}, f32[32,1024]{1,0:T(8,128)S(1)}, u32[]{:S(2)}, u32[]{:S(2)}) %collective-permute-start.20) | collective-permute-done | bytes 131104 | tf_op jit(solution)/shard_map/ppermute | solution.py:353
  84.7 3.5 %input.2 = (bf16[512,1024]{1,0:T(8,128)(2,1)}, bf16[512,256]{1,0:T(8,128)(2,1)}, f32[16,512]{1,0:T(8,128)}) custom-call(f32[512,512]{1,0:T(8,128)S(1)} %get-tuple-element.119.refs_0_, f32[512,128]{1,0:T(8,128)S(1)} %get-tuple-element.120.refs_1_, bf16[512,128]{1,0:T(8,128)(2,1)S(1)} %copy-done.30, f32[512,8]{1,0:T(8,128)S(1)} %get-tuple-element.76.refs_3_, ...), custom_call_target="tpu_custom_call" | custom-call | bytes 9225000 | tf_op jit(solution)/shard_map/input/pallas_call | solution.py:332
  88.2 2.4 %collective-permute-done.18.refs_2_ = f32[32,1024]{1,0:T(8,128)S(1)} collective-permute-done((f32[32,1024]{1,0:T(8,128)S(1)}, f32[32,1024]{1,0:T(8,128)S(1)}, u32[]{:S(2)}, u32[]{:S(2)}) %collective-permute-start.18) | collective-permute-done | bytes 131104 | tf_op jit(solution)/shard_map/ppermute | solution.py:353
  90.5 1.4 %collective-permute-done.21.refs_4_ = f32[32,1024]{1,0:T(8,128)S(1)} collective-permute-done((f32[32,1024]{1,0:T(8,128)S(1)}, f32[32,1024]{1,0:T(8,128)S(1)}, u32[]{:S(2)}, u32[]{:S(2)}) %collective-permute-start.21) | collective-permute-done | bytes 131104 | tf_op jit(solution)/shard_map/ppermute | solution.py:353
  92.8 3.4 %input.3 = (bf16[512,1024]{1,0:T(8,128)(2,1)}, bf16[512,256]{1,0:T(8,128)(2,1)}, f32[16,512]{1,0:T(8,128)}) custom-call(f32[512,512]{1,0:T(8,128)S(1)} %get-tuple-element.114.refs_0_, f32[512,128]{1,0:T(8,128)S(1)} %get-tuple-element.115.refs_1_, bf16[512,128]{1,0:T(8,128)(2,1)S(1)} %copy-done.28, ...), custom_call_target="tpu_custom_call", output_to_operand_aliasing={{0}: (17, {}), {1}: (18, {}), {2}: (19, {})} | custom-call | bytes 9225000 | tf_op jit(solution)/shard_map/input/pallas_call | solution.py:332
  (151 shorter events, 26.3 us)
Async XLA Ops:
  6.2 22.7 %copy-start.21 = (f32[32,512]{1,0:T(8,128)}, f32[32,512]{1,0:T(8,128)S(1)}, u32[]{:S(2)}) copy-start(f32[32,512]{1,0:T(8,128)S(1)} %get-tuple-element.95.refs_5_.refs_13_) | copy-start | bytes 196612
  6.2 22.7 %copy-start.34 = (f32[8,512]{1,0:T(8,128)}, f32[8,512]{1,0:T(8,128)S(1)}, u32[]{:S(2)}) copy-start(f32[8,512]{1,0:T(8,128)S(1)} %get-tuple-element.87.refs_6_.refs_12_) | copy-start | bytes 49156
  6.3 10.5 %collective-permute-start = (f32[128,512]{1,0:T(8,128)S(1)}, f32[128,512]{1,0:T(8,128)S(1)}, u32[]{:S(2)}, u32[]{:S(2)}) collective-permute-start(f32[128,512]{1,0:T(8,128)S(1)} %get-tuple-element.84), channel_id=1, source_target_pairs={{0,4},{1,5},{2,6},{3,7},{16,20},{17,21},{18,22},{19,23}} | collective-permute-start | bytes 786440 | tf_op jit(solution)/shard_map/ppermute | solution.py:353
  11.7 9.5 %collective-permute-start.2 = (f32[64,512]{1,0:T(8,128)S(1)}, f32[64,512]{1,0:T(8,128)S(1)}, u32[]{:S(2)}, u32[]{:S(2)}) collective-permute-start(f32[64,512]{1,0:T(8,128)S(1)} %rank.1), channel_id=1, source_target_pairs={{0,1},{1,0},{2,3},{3,2},{4,5},{5,4},{6,7},{7,6},{8,9},{9,8},{10,11... | collective-permute-start | bytes 393224 | tf_op jit(solution)/shard_map/ppermute | solution.py:374
  16.7 9.1 %collective-permute-start.1 = (f32[128,512]{1,0:T(8,128)S(1)}, f32[128,512]{1,0:T(8,128)S(1)}, u32[]{:S(2)}, u32[]{:S(2)}) collective-permute-start(f32[128,512]{1,0:T(8,128)S(1)} %get-tuple-element.85), channel_id=1, source_target_pairs={{0,4},{1,5},{2,6},{3,7},{16,20},{17,21},{18,22},{19,23}} | collective-permute-start | bytes 786440 | tf_op jit(solution)/shard_map/ppermute | solution.py:353
  21.2 6.0 %collective-permute-start.4 = (f32[64,512]{1,0:T(8,128)S(1)}, f32[64,512]{1,0:T(8,128)S(1)}, u32[]{:S(2)}, u32[]{:S(2)}) collective-permute-start(f32[64,512]{1,0:T(8,128)S(1)} %add.46.refs_12_), channel_id=1, source_target_pairs={{0,2},{2,0},{1,3},{3,1},{4,6},{6,4},{5,7},{7,5},{8,10},{10,8},{9,1... | collective-permute-start | bytes 393224 | tf_op jit(solution)/shard_map/ppermute | solution.py:374
  22.8 4.4 %collective-permute-start.6 = (f32[128,512]{1,0:T(8,128)S(1)}, f32[128,512]{1,0:T(8,128)S(1)}, u32[]{:S(2)}, u32[]{:S(2)}) collective-permute-start(f32[128,512]{1,0:T(8,128)S(1)} %multiply_add_fusion.5), channel_id=1, source_target_pairs={{4,8},{5,9},{6,10},{7,11},{20,24},{21,25},{22,26},{23,27}} | collective-permute-start | bytes 786440 | tf_op jit(solution)/shard_map/ppermute | solution.py:353
  25.8 2.3 %collective-permute-start.3 = (f32[128,512]{1,0:T(8,128)S(1)}, f32[128,512]{1,0:T(8,128)S(1)}, u32[]{:S(2)}, u32[]{:S(2)}) collective-permute-start(f32[128,512]{1,0:T(8,128)S(1)} %multiply_add_fusion.7), channel_id=1, source_target_pairs={{4,8},{5,9},{6,10},{7,11},{20,24},{21,25},{22,26},{23,27}} | collective-permute-start | bytes 786440 | tf_op jit(solution)/shard_map/ppermute | solution.py:353
  27.3 1.6 %collective-permute-start.7 = (f32[128,512]{1,0:T(8,128)S(1)}, f32[128,512]{1,0:T(8,128)S(1)}, u32[]{:S(2)}, u32[]{:S(2)}) collective-permute-start(f32[128,512]{1,0:T(8,128)S(1)} %multiply_add_fusion.4), channel_id=1, source_target_pairs={{8,12},{9,13},{10,14},{11,15},{24,28},{25,29},{26,30},{27,31}} | collective-permute-start | bytes 786440 | tf_op jit(solution)/shard_map/ppermute | solution.py:353
  28.2 7.7 %collective-permute-start.5 = (f32[128,512]{1,0:T(8,128)S(1)}, f32[128,512]{1,0:T(8,128)S(1)}, u32[]{:S(2)}, u32[]{:S(2)}) collective-permute-start(f32[128,512]{1,0:T(8,128)S(1)} %multiply_add_fusion.6), channel_id=1, source_target_pairs={{8,12},{9,13},{10,14},{11,15},{24,28},{25,29},{26,30},{27,31}} | collective-permute-start | bytes 786440 | tf_op jit(solution)/shard_map/ppermute | solution.py:353
  34.5 11.8 %collective-permute-start.13 = (f32[128,512]{1,0:T(8,128)}, f32[128,512]{1,0:T(8,128)}, u32[]{:S(2)}, u32[]{:S(2)}) collective-permute-start(f32[128,512]{1,0:T(8,128)} %get-tuple-element.122.refs_10_), channel_id=1, source_target_pairs={{12,8},{13,9},{14,10},{15,11},{28,24},{29,25},{30,26},{31,27}} | collective-permute-start | bytes 786440 | tf_op jit(solution)/shard_map/ppermute | solution.py:353
  42.0 1.7 %collective-permute-start.8 = (f32[64,512]{1,0:T(8,128)}, f32[64,512]{1,0:T(8,128)}, u32[]{:S(2)}, u32[]{:S(2)}) collective-permute-start(f32[64,512]{1,0:T(8,128)} %get-tuple-element.101), channel_id=1, source_target_pairs={{0,1},{1,0},{2,3},{3,2},{4,5},{5,4},{6,7},{7,6},{8,9},{9,8},{10,11... | collective-permute-start | bytes 393224 | tf_op jit(solution)/shard_map/ppermute | solution.py:374
  42.0 9.8 %collective-permute-start.10 = (f32[128,512]{1,0:T(8,128)S(1)}, f32[128,512]{1,0:T(8,128)}, u32[]{:S(2)}, u32[]{:S(2)}) collective-permute-start(f32[128,512]{1,0:T(8,128)S(1)} %get-tuple-element.106.refs_10_), channel_id=1, source_target_pairs={{12,8},{13,9},{14,10},{15,11},{28,24},{29,25},{30,26},{31,27}} | collective-permute-start | bytes 786440 | tf_op jit(solution)/shard_map/ppermute | solution.py:353
  44.7 5.6 %collective-permute-start.9 = (f32[64,512]{1,0:T(8,128)S(1)}, f32[64,512]{1,0:T(8,128)S(1)}, u32[]{:S(2)}, u32[]{:S(2)}) collective-permute-start(f32[64,512]{1,0:T(8,128)S(1)} %add.52.refs_1_), channel_id=1, source_target_pairs={{0,2},{2,0},{1,3},{3,1},{4,6},{6,4},{5,7},{7,5},{8,10},{10,8},{9,1... | collective-permute-start | bytes 393224 | tf_op jit(solution)/shard_map/ppermute | solution.py:374
  47.4 16.4 %collective-permute-start.14 = (f32[128,512]{1,0:T(8,128)S(1)}, f32[128,512]{1,0:T(8,128)S(1)}, u32[]{:S(2)}, u32[]{:S(2)}) collective-permute-start(f32[128,512]{1,0:T(8,128)S(1)} %multiply_add_fusion.1), channel_id=1, source_target_pairs={{8,4},{9,5},{10,6},{11,7},{24,20},{25,21},{26,22},{27,23}} | collective-permute-start | bytes 786440 | tf_op jit(solution)/shard_map/ppermute | solution.py:353
  52.9 19.7 %collective-permute-start.11 = (f32[128,512]{1,0:T(8,128)S(1)}, f32[128,512]{1,0:T(8,128)S(1)}, u32[]{:S(2)}, u32[]{:S(2)}) collective-permute-start(f32[128,512]{1,0:T(8,128)S(1)} %multiply_add_fusion.3), channel_id=1, source_target_pairs={{8,4},{9,5},{10,6},{11,7},{24,20},{25,21},{26,22},{27,23}} | collective-permute-start | bytes 786440 | tf_op jit(solution)/shard_map/ppermute | solution.py:353
  53.6 12.6 %collective-permute-start.16 = (f32[32,1024]{1,0:T(8,128)S(1)}, f32[32,1024]{1,0:T(8,128)S(1)}, u32[]{:S(2)}, u32[]{:S(2)}) collective-permute-start(f32[32,1024]{1,0:T(8,128)S(1)} %get-tuple-element.134), channel_id=1, source_target_pairs={{0,4},{4,0},{8,12},{12,8},{1,5},{5,1},{9,13},{13,9},{2,6},{6,2},{1... | collective-permute-start | bytes 393224 | tf_op jit(solution)/shard_map/ppermute | solution.py:353
  60.1 11.8 %collective-permute-start.19 = (f32[32,1024]{1,0:T(8,128)S(1)}, f32[32,1024]{1,0:T(8,128)S(1)}, u32[]{:S(2)}, u32[]{:S(2)}) collective-permute-start(f32[32,1024]{1,0:T(8,128)S(1)} %get-tuple-element.137), channel_id=1, source_target_pairs={{0,4},{4,0},{8,12},{12,8},{1,5},{5,1},{9,13},{13,9},{2,6},{6,2},{1... | collective-permute-start | bytes 393224 | tf_op jit(solution)/shard_map/ppermute | solution.py:353
  64.8 19.2 %collective-permute-start.15 = (f32[128,512]{1,0:T(8,128)S(1)}, f32[128,512]{1,0:T(8,128)S(1)}, u32[]{:S(2)}, u32[]{:S(2)}) collective-permute-start(f32[128,512]{1,0:T(8,128)S(1)} %multiply_add_fusion), channel_id=1, source_target_pairs={{4,0},{5,1},{6,2},{7,3},{20,16},{21,17},{22,18},{23,19}} | collective-permute-start | bytes 786440 | tf_op jit(solution)/shard_map/ppermute | solution.py:353
  66.2 15.3 %collective-permute-start.17 = (f32[32,1024]{1,0:T(8,128)S(1)}, f32[32,1024]{1,0:T(8,128)S(1)}, u32[]{:S(2)}, u32[]{:S(2)}) collective-permute-start(f32[32,1024]{1,0:T(8,128)S(1)} %add.57), channel_id=1, source_target_pairs={{0,8},{8,0},{4,12},{12,4},{1,9},{9,1},{5,13},{13,5},{2,10},{10,2},... | collective-permute-start | bytes 393224 | tf_op jit(solution)/shard_map/ppermute | solution.py:353
  71.9 11.6 %collective-permute-start.20 = (f32[32,1024]{1,0:T(8,128)S(1)}, f32[32,1024]{1,0:T(8,128)S(1)}, u32[]{:S(2)}, u32[]{:S(2)}) collective-permute-start(f32[32,1024]{1,0:T(8,128)S(1)} %add.59), channel_id=1, source_target_pairs={{0,8},{8,0},{4,12},{12,4},{1,9},{9,1},{5,13},{13,5},{2,10},{10,2},... | collective-permute-start | bytes 393224 | tf_op jit(solution)/shard_map/ppermute | solution.py:353
  72.7 20.1 %collective-permute-start.12 = (f32[128,512]{1,0:T(8,128)S(1)}, f32[128,512]{1,0:T(8,128)S(1)}, u32[]{:S(2)}, u32[]{:S(2)}) collective-permute-start(f32[128,512]{1,0:T(8,128)S(1)} %multiply_add_fusion.2), channel_id=1, source_target_pairs={{4,0},{5,1},{6,2},{7,3},{20,16},{21,17},{22,18},{23,19}} | collective-permute-start | bytes 786440 | tf_op jit(solution)/shard_map/ppermute | solution.py:353
  81.5 9.0 %collective-permute-start.18 = (f32[32,1024]{1,0:T(8,128)S(1)}, f32[32,1024]{1,0:T(8,128)S(1)}, u32[]{:S(2)}, u32[]{:S(2)}) collective-permute-start(f32[32,1024]{1,0:T(8,128)S(1)} %add.58.refs_1_), channel_id=1, source_target_pairs={{0,4},{4,0},{8,12},{12,8},{1,5},{5,1},{9,13},{13,9},{2,6},{6,2},{1... | collective-permute-start | bytes 393224 | tf_op jit(solution)/shard_map/ppermute | solution.py:353
  83.5 8.5 %collective-permute-start.21 = (f32[32,1024]{1,0:T(8,128)S(1)}, f32[32,1024]{1,0:T(8,128)S(1)}, u32[]{:S(2)}, u32[]{:S(2)}) collective-permute-start(f32[32,1024]{1,0:T(8,128)S(1)} %add.60.refs_3_), channel_id=1, source_target_pairs={{0,4},{4,0},{8,12},{12,8},{1,5},{5,1},{9,13},{13,9},{2,6},{6,2},{1... | collective-permute-start | bytes 393224 | tf_op jit(solution)/shard_map/ppermute | solution.py:353
  (49 other events, 165.2 us)

commit v2 on v1

--- a/solution.py
+++ b/solution.py
@@ -154,7 +154,7 @@
     scaled[...] = (gather_incoming(near, far, mid) * rows[1:2]).astype(bf16)
     inner[...] = y_loc[...] + dot(cstart[...], scaled[...], 1, 0)
     falls[...] = spread(small[heads : 2 * heads], places)
-    g_mixed[...] = frozen[...].astype(f32) + dot(gu, down[...], 0, 0)
+    g_mixed[...] = dot(gu, down[...], 0, 0)
     skip_row = spread_row(skip, places)
     gain_row = gain[...]
 
@@ -170,7 +170,7 @@
         inv = lax.rsqrt(jnp.sum(grouped * grouped, axis=1, keepdims=True) * (1.0 / channels) + EPS)
         normed = grouped * inv
         mixed[at] = (normed * gain_row).astype(bf16)
-        g_norm = g_mixed[at] * gain_row
+        g_norm = (frozen[at].astype(f32) + g_mixed[at]) * gain_row
         mean = jnp.sum(g_norm * normed, axis=1, keepdims=True) * (1.0 / channels)
         g_grouped = inv * (g_norm - normed * mean)
         gate_grad[at] = (g_grouped * y * (sig + act * (1.0 - sig))).astype(bf16)
@@ -230,8 +230,8 @@
 
 def input_kernel(
     z_loc, b_loc, bend, ids_col, ids_row, xw, gye, near, far, mid, grad_dev, scaled_in, rows, small, skips,
-    rates, y_dot,
-    x_grad, b_grad, step_grad,
+    rates, y_dot, passing,
+    x_grad, b_grad, step_grad, passed,
     inner, weights, rises, product,
     first,
 ):
@@ -244,6 +244,7 @@
     rise = small[2 * heads : 3 * heads]
     raw = small[3 * heads :]
     incoming = gather_incoming(near, far, mid)
+    passed[...] = passing[...]
     scaled = (incoming * rows[1:2]).astype(bf16)
     inner[...] = z_loc[...] + dot(bend[...], scaled, 1, 0)
     weights[...] = spread(dt * rise, places)
@@ -279,23 +280,29 @@
     up_part[...] = dot(u, lo[...], 1, 0)
 
 
-def adapter_halves_kernel(odd, u_here, u_there, up, lo, down_part, out, up_keep, up_send, down_keep, down_send):
+def output_kernel(u, up, out):
+    out[...] = dot(u[...], up[...], 0, 0).astype(bf16)
+
+
+def halves_kernel(odd, u_here, u_there, lo, down_part, u_out, keep, send):
     u = (SCALE * (u_here[...] + u_there[...])).astype(bf16)
-    out[...] = dot(u, up[...], 0, 0).astype(bf16)
+    u_out[...] = u
+    rows = keep.shape[0] // 2
+    is_odd = odd[0] == 1
+    down = down_part[...]
+    keep[rows:] = jnp.where(is_odd, down[rows:], down[:rows])
+    send[rows:] = jnp.where(is_odd, down[:rows], down[rows:])
     up_part = dot(u, lo[...], 1, 0)
-    rows = up_keep.shape[0]
+    keep[:rows] = jnp.where(is_odd, up_part[rows:], up_part[:rows])
+    send[:rows] = jnp.where(is_odd, up_part[:rows], up_part[rows:])
+
+
+def join_kernel(odd, keep, other, up_out, down_out):
     is_odd = odd[0] == 1
-    for keep, send, part in ((up_keep, up_send, up_part), (down_keep, down_send, down_part[...])):
-        keep[...] = jnp.where(is_odd, part[rows:], part[:rows])
-        send[...] = jnp.where(is_odd, part[:rows], part[rows:])
-
-
-def join_kernel(odd, *refs):
-    is_odd = odd[0] == 1
-    for keep, other, out in (refs[0:2] + refs[4:5], refs[2:4] + refs[5:6]):
-        rows = keep.shape[0]
-        out[:rows] = jnp.where(is_odd, other[...], keep[...])
-        out[rows:] = jnp.where(is_odd, keep[...], other[...])
+    rows = keep.shape[0] // 2
+    for at, out in ((pl.ds(0, rows), up_out), (pl.ds(rows, rows), down_out)):
+        out[:rows] = jnp.where(is_odd, other[at], keep[at])
+        out[rows:] = jnp.where(is_odd, keep[at], other[at])
 
 
 def rank_kernel(up, lo, part):
@@ -304,9 +311,12 @@
 
 def call(kernel, ins, outs, scratch=(), cost=1.0, name=None):
     in_specs, operands = [], []
-    for array, block, index in ins:
-        if block == "scalar":
-            in_specs.append(pl.BlockSpec(memory_space=pltpu.SMEM))
+    for array, block, index, *pinned in ins:
+        if pinned:
+            array = pltpu.with_memory_space_constraint(array, pltpu.HBM)
+        if block in ("scalar", "far"):
+            space = pltpu.SMEM if block == "scalar" else pltpu.HBM
+            in_specs.append(pl.BlockSpec(memory_space=space))
             operands.append(array)
             continue
         if block is None:
@@ -314,11 +324,11 @@
         in_specs.append(pl.BlockSpec(block, functools.partial(lambda at, i: at, index)))
         operands.append(array)
     out_specs, out_shapes, aliases = [], [], {}
-    for at, (shape, dtype, block, index, held) in enumerate(outs):
+    for at, (shape, dtype, block, index, held, *pinned) in enumerate(outs):
         if block is None:
             block, index = shape, (0,) * len(shape)
         out_specs.append(pl.BlockSpec(block, functools.partial(lambda at, i: at, index)))
-        out_shapes.append(jax.ShapeDtypeStruct(shape, dtype))
+        out_shapes.append((pltpu.HBM if pinned else jax.ShapeDtypeStruct)(shape, dtype))
         if held is not None:
             aliases[len(operands)] = at
             operands.append(held)
@@ -364,13 +374,13 @@
     return incoming, jnp.zeros_like(state), jnp.zeros_like(state)
 
 
-def exchange_pair(part, axes):
+def exchange_pair(part, axes, *before):
     other = None
     for axis in axes:
         count = lax.axis_size(axis)
         span = 1
         while span < count:
-            part = part if other is None else part + other
+            part = part if other is None else after(part, *before) + other
             other = lax.ppermute(part, axis, [(i, i ^ span) for i in range(count)])
             span *= 2
     return part, other
@@ -421,6 +431,12 @@
     def fresh(shape, dtype):
         return (shape, dtype, None, None, None)
 
+    def far(array):
+        return (array, "far", None, True)
+
+    def slow(item):
+        return (*item, True)
+
     everything = range(groups)
     short = lax.axis_size("ctx") == 4
 
@@ -428,13 +444,13 @@
         return call(
             functools.partial(state_kernel, first=g * heads),
             [
-                cols(mixer_input_channels, g),
-                cols(input_group_maps, g),
-                cols(output_group_maps, g),
-                head_rows(step_size_input, g),
-                whole(resets),
-                whole(rates),
-                whole(biases),
+                slow(cols(mixer_input_channels, g)),
+                slow(cols(input_group_maps, g)),
+                slow(cols(output_group_maps, g)),
+                slow(head_rows(step_size_input, g)),
+                slow(whole(resets)),
+                slow(whole(rates)),
+                slow(whole(biases)),
             ],
             [
                 fresh((length, width), bf16),
@@ -477,20 +493,19 @@
         cost=1.0,
         name="rank",
     )
-    gu = exchange_pair(gu_part, ("fsdp", "head"))
     parts = [states[g][1] for g in everything]
     decays = [states[g][5][0:1] for g in everything]
     entering = []
     if short:
-        first = [hop(parts[0], "ctx", (0, 1))]
-        for g in range(1, groups):
-            first.append(hop(after(parts[g], first[-1]), "ctx", (0, 1)))
+        first = [hop(parts[g], "ctx", (0, 1)) for g in everything]
+        joined = [after(decays[g], parts[-1], gu_part) * first[g] + parts[g] for g in everything]
+        gu = exchange_pair(gu_part, ("fsdp", "head"), joined[0])
         for g in everything:
-            joined = after(decays[g], parts[-1], gu[0]) * first[g] + parts[g]
-            second = hop(joined, "ctx", (1, 2))
-            joined = after(decays[g], y_locs[-1], gu[1]) * second + parts[g]
-            entering.append((first[g], second, hop(joined, "ctx", (2, 3))))
+            second = hop(joined[g], "ctx", (1, 2))
+            third = after(decays[g], y_locs[-1], gu[1]) * second + parts[g]
+            entering.append((first[g], second, hop(third, "ctx", (2, 3))))
     else:
+        gu = exchange_pair(gu_part, ("fsdp", "head"))
         entering = [chain(parts[g], decays[g], "ctx", False) for g in everything]
     mixed = gate_grad = down_part = u_part = c_grad = None
     normed, pairs = [], []
@@ -539,12 +554,12 @@
             [
                 ((length, channels), bf16, (length, width), (0, g), mixed),
                 ((length, channels), bf16, (length, width), (0, g), gate_grad),
-                ((rank, channels), f32, (rank, width), (0, g), down_part),
+                slow(((rank, channels), f32, (rank, width), (0, g), down_part)),
                 fresh((length, width), bf16),
                 fresh((STATE, width), bf16),
                 fresh((STATE, width), f32),
                 fresh((rank, length), f32),
-                fresh((heads, length), f32),
+                slow(fresh((heads, length), f32)),
             ],
             [
                 pltpu.VMEM((length, width), f32),
@@ -557,29 +572,99 @@
         )
         mixed, gate_grad, down_part, gye, scaled, state_grad, u_part, y_dot = results
         normed.append((gye, scaled, state_grad, y_dot))
-    leaving = []
-    if short:
-        last = [hop(normed[g][2], "ctx", (3, 2)) for g in everything]
-        joined = after(decays[0], u_part) * last[0] + normed[0][2]
-        then = [hop(joined, "ctx", (2, 1))]
-    u = exchange_pair(u_part, ("fsdp", "head"))
-    half = fresh((rank // 2, channels), f32)
-    if short:
+    def input_call(g, leaving, held, passing, *before):
+        xw, state, bend, cstart, small, rows, ids_row, ids_col = states[g]
+        x_grad, b_grad, step_grad = held
+        return call(
+            functools.partial(input_kernel, first=g * heads),
+            [
+                whole(pairs[g][0]),
+                whole(pairs[g][1]),
+                whole(bend),
+                whole(ids_col),
+                whole(ids_row),
+                whole(xw),
+                whole(normed[g][0]),
+                *map(whole, leaving),
+                whole(normed[g][2]),
+                whole(normed[g][1]),
+                whole(rows),
+                whole(small),
+                whole(skips),
+                whole(after(rates, *before) if before else rates),
+                slow(whole(normed[g][3])),
+                whole(passing),
+            ],
+            [
+                ((length, channels), bf16, (length, width), (0, g), x_grad),
+                ((length, groups * STATE), bf16, (length, STATE), (0, g), b_grad),
+                ((groups * heads, length), f32, (heads, length), (g, 0), step_grad),
+                fresh(passing.shape, f32),
+            ],
+            [
+                pltpu.VMEM((length, width), f32),
+                pltpu.VMEM((length, width), f32),
+                pltpu.VMEM((length, width), f32),
+                pltpu.VMEM((2, length, width), bf16),
+            ],
+            cost=2.5,
+            name="input",
+        )
+
+    state_grads = [normed[g][2] for g in everything]
+    held = (None, None, None)
+    if short and groups == 2:
+        neighbours = [(0, 1), (1, 0), (2, 3), (3, 2)]
+        across = [(0, 2), (2, 0), (1, 3), (3, 1)]
+        last = [hop(state_grads[g], "ctx", (3, 2)) for g in everything]
+        sent = after(decays[0], u_part) * last[0] + state_grads[0]
+        then = [hop(sent, "ctx", (2, 1))]
+        u = exchange_pair(u_part, ("fsdp", "head"), sent)
         odd = (lax.axis_index("ctx") % 2).reshape(1)
-        adapter_output, *halves = call(
-            adapter_halves_kernel,
+        half = fresh((rank, channels), f32)
+        u, keep, send = call(
+            halves_kernel,
             [
                 (odd, "scalar", None),
                 *map(whole, u),
-                whole(adapter_up_map),
                 whole(layer_output_gradient),
-                whole(down_part),
-            ],
-            [fresh((length, channels), bf16), half, half, half, half],
+                slow(whole(down_part)),
+            ],
+            [fresh((rank, length), bf16), half, half],
             cost=1.5,
-            name="adapter",
+            name="halves",
+        )
+        sent = after(decays[1], keep) * last[1] + state_grads[1]
+        then.append(hop(sent, "ctx", (2, 1)))
+        got = hop(send, "ctx", *neighbours)
+        sent = after(decays[0], sent) * then[0] + state_grads[0]
+        ahead = [hop(sent, "ctx", (1, 0))]
+        c_grad, *pair = pair_call(0, c_grad, sent)
+        pairs.append(pair)
+        keep = after(keep, pair[1]) + got
+        got = hop(keep, "ctx", *across)
+        *held, decay = input_call(0, (last[0], then[0], ahead[0]), held, decays[1], keep)
+        sent = decay * then[1] + state_grads[1]
+        ahead.append(hop(sent, "ctx", (1, 0)))
+        c_grad, *pair = pair_call(1, c_grad, sent)
+        pairs.append(pair)
+        (adapter_output,) = call(
+            output_kernel,
+            [whole(after(u, sent)), whole(adapter_up_map)],
+            [fresh((length, channels), bf16)],
+            name="output",
+        )
+        keep = after(keep, sent, pair[1]) + got
+        got = hop(keep, "ctx", *neighbours)
+        *held, _ = input_call(1, (last[1], then[1], ahead[1]), held, decays[1])
+        up_sum, down_sum = call(
+            join_kernel,
+            [(odd, "scalar", None), whole(after(keep, held[2])), whole(got)],
+            [fresh((rank, channels), f32), fresh((rank, channels), f32)],
+            name="join",
         )
     else:
+        u = exchange_pair(u_part, ("fsdp", "head"))
         adapter_output, up_part = call(
             adapter_kernel,
             [*map(whole, u), whole(adapter_up_map), whole(layer_output_gradient)],
@@ -587,71 +672,14 @@
             cost=1.5,
             name="adapter",
         )
-    if short:
-        for g in range(1, groups):
-            joined = after(decays[g], halves[0]) * last[g] + normed[g][2]
-            then.append(hop(joined, "ctx", (2, 1)))
-    for g in everything:
-        c_grad, z_loc, b_loc = pair_call(g, c_grad, *([joined] if short else []))
-        pairs.append((z_loc, b_loc))
-    if short:
         for g in everything:
-            joined = after(decays[g], pairs[-1][1]) * then[g] + normed[g][2]
-            leaving.append((last[g], then[g], hop(joined, "ctx", (1, 0))))
-        neighbours = [(0, 1), (1, 0), (2, 3), (3, 2)]
-        across = [(0, 2), (2, 0), (1, 3), (3, 1)]
-        ends = []
-        for keep, send in (halves[:2], halves[2:]):
-            keep = keep + hop(send, "ctx", *neighbours)
-            got = hop(keep, "ctx", *across)
-            keep = after(keep, joined) + got
-            ends += [keep, hop(keep, "ctx", *neighbours)]
-        up_sum, down_sum = call(
-            join_kernel,
-            [(odd, "scalar", None), *map(whole, ends)],
-            [fresh((rank, channels), f32), fresh((rank, channels), f32)],
-            name="join",
-        )
-    else:
+            c_grad, *pair = pair_call(g, c_grad)
+            pairs.append(pair)
+            leaving = chain(state_grads[g], decays[g], "ctx", True)
+            *held, _ = input_call(g, leaving, held, decays[g])
         up_sum = exchange_sum(up_part, ("ctx",))
         down_sum = exchange_sum(down_part, ("ctx",))
-        leaving = [chain(normed[g][2], decays[g], "ctx", True) for g in everything]
-    x_grad = b_grad = step_grad = None
-    for g in everything:
-        xw, state, bend, cstart, small, rows, ids_row, ids_col = states[g]
-        x_grad, b_grad, step_grad = call(
-            functools.partial(input_kernel, first=g * heads),
-            [
-                whole(pairs[g][0]),
-                whole(pairs[g][1]),
-                whole(bend),
-                whole(ids_col),
-                whole(ids_row),
-                whole(xw),
-                whole(normed[g][0]),
-                *map(whole, leaving[g]),
-                whole(normed[g][2]),
-                whole(normed[g][1]),
-                whole(rows),
-                whole(small),
-                whole(skips),
-                whole(rates),
-                whole(normed[g][3]),
-            ],
-            [
-                ((length, channels), bf16, (length, width), (0, g), x_grad),
-                ((length, groups * STATE), bf16, (length, STATE), (0, g), b_grad),
-                ((groups * heads, length), f32, (heads, length), (g, 0), step_grad),
-            ],
-            [
-                pltpu.VMEM((length, width), f32),
-                pltpu.VMEM((length, width), f32),
-                pltpu.VMEM((length, width), f32),
-                pltpu.VMEM((2, length, width), bf16),
-            ],
-            cost=2.5,
-            name="input",
-        )
+    x_grad, b_grad, step_grad = held
     return (
         mixed,
         adapter_output,

time: 97 us -> 90.7 us (0.935)
  local copies, waits for them, and re-layouts: 11.2 us -> 4.15 us
  Pallas kernels: 23.3 us -> 27.2 us
  starting transfers between devices: 35.8 us -> 32.6 us
  waiting for transfers between devices: 20.1 us -> 21.1 us
    unnamed x102 -> x88, local copies, waits for them, and re-layouts: 11.2 us -> 4.14 us
    pallas_call x13 -> x14, Pallas kernels: 23.3 us -> 27.2 us  [call(): pl.pallas_call(body, grid=(1,), in_specs=in_specs, out_specs=out_specs, o...]
    ppermute x18 -> x15, starting transfers between devices: 32.6 us -> 29.5 us  [hop(): return lax.ppermute(part, axis, list(pairs))]
    ppermute x4, waiting for transfers between devices: 2.6 us -> 3.77 us  [exchange_pair(): other = lax.ppermute(part, axis, [(i, i ^ span) for i in range(count)])]
    add x14 -> x12, other arithmetic: 4.48 us -> 3.81 us  [the longest x1 1.03 us: per_device(): sent = after(decays[0], sent) * then[0] + state_grads[0]]
    ppermute x18 -> x15, waiting for transfers between devices: 17.5 us -> 17.3 us  [hop(): return lax.ppermute(part, axis, list(pairs))]
  transfers between devices with their start and end apart: 22 -> 19, of which waited for: 8 -> 8; matrix products, arithmetic and copies ran while one was open for 5% -> 4% of each run, Pallas kernels for 20% -> 27%
where the time goes in v2:
time: 90.7 us; the launch traced here: 90.2 us
  starting transfers between devices  32.6 us (36%)
  Pallas kernels  27.2 us (30%)
  waiting for transfers between devices  21.1 us (23%)
  local copies, waits for them, and re-layouts  4.15 us (5%)
  other arithmetic  3.81 us (4%)
  between operations  1.25 us (1%)
    ppermute x15, starting transfers between devices, hop(): return lax.ppermute(part, axis, list(pairs))  29.5 us
    pallas_call x14, Pallas kernels, call(): pl.pallas_call(body, grid=(1,), in_specs=in_specs, out_specs=out_specs, o...  27.2 us
    ppermute x15, waiting for transfers between devices, hop(): return lax.ppermute(part, axis, list(pairs))  17.3 us
    unnamed x88, local copies, waits for them, and re-layouts  4.14 us
    ppermute x4, waiting for transfers between devices, exchange_pair(): other = lax.ppermute(part, axis, [(i, i ^ span) for i in range(count)])  3.77 us
    ppermute x4, starting transfers between devices, exchange_pair(): other = lax.ppermute(part, axis, [(i, i ^ span) for i in range(count)])  3.13 us
  transfers between devices with their start and end apart: 19, of which 8 were waited for; matrix products, arithmetic and copies ran while one was open for 4% of the time, Pallas kernels for 27%

profile of v2, /device:TPU:0, one launch (start us, length us, event | category | flops | bytes accessed | tf_op | source)
XLA Modules:
  0.0 90.2 jit_solution(17986857859149034262)
XLA Ops:
  0.7 2.3 %state.2 = (bf16[512,512]{1,0:T(8,128)(2,1)S(1)}, f32[128,512]{1,0:T(8,128)S(1)}, bf16[512,128]{1,0:T(8,128)(2,1)S(1)}, bf16[512,128]{1,0:T(8,128)(2,1)S(1)}, f3...) custom-call(bf16[512,1024]{1,0:T(8,128)(2,1)} %refs_7_.3, ...), custom_call_target="tpu_custom_call" | custom-call | bytes 5535000 | tf_op jit(solution)/shard_map/state/pallas_call | solution.py:342
  3.0 4.9 %collective-permute-start.2 = (f32[128,512]{1,0:T(8,128)S(1)}, f32[128,512]{1,0:T(8,128)S(1)}, u32[]{:S(2)}, u32[]{:S(2)}) collective-permute-start(f32[128,512]{1,0:T(8,128)S(1)} %get-tuple-element.91), channel_id=1, source_target_pairs={{0,4},{1,5},{2,6},{3,7},{16,20},{17,21},{18,22},{19,23}} | collective-permute-start | bytes 786440 | tf_op jit(solution)/shard_map/ppermute | solution.py:363
  9.6 2.2 %state.3 = (bf16[512,512]{1,0:T(8,128)(2,1)S(1)}, f32[128,512]{1,0:T(8,128)S(1)}, bf16[512,128]{1,0:T(8,128)(2,1)S(1)}, bf16[512,128]{1,0:T(8,128)(2,1)S(1)}, f3...) custom-call(bf16[512,1024]{1,0:T(8,128)(2,1)} %refs_7_.3, ...), custom_call_target="tpu_custom_call" | custom-call | bytes 5535000 | tf_op jit(solution)/shard_map/state/pallas_call | solution.py:342
  15.2 1.6 %collective-permute-start.4 = (f32[64,512]{1,0:T(8,128)S(1)}, f32[64,512]{1,0:T(8,128)S(1)}, u32[]{:S(2)}, u32[]{:S(2)}) collective-permute-start(f32[64,512]{1,0:T(8,128)S(1)} %add.42.refs_12_), channel_id=1, source_target_pairs={{0,2},{2,0},{1,3},{3,1},{4,6},{6,4},{5,7},{7,5},{8,10},{10,8},{9,1... | collective-permute-start | bytes 393224 | tf_op jit(solution)/shard_map/ppermute | solution.py:384
  16.7 2.4 %collective-permute-done.refs_2_ = f32[128,512]{1,0:T(8,128)S(1)} collective-permute-done((f32[128,512]{1,0:T(8,128)S(1)}, f32[128,512]{1,0:T(8,128)S(1)}, u32[]{:S(2)}, u32[]{:S(2)}) %collective-permute-start) | collective-permute-done | bytes 262176 | tf_op jit(solution)/shard_map/ppermute | solution.py:363
  22.6 3.4 %norm.2 = (bf16[512,1024]{1,0:T(8,128)(2,1)}, bf16[512,1024]{1,0:T(8,128)(2,1)}, f32[64,1024]{1,0:T(8,128)}, bf16[512,512]{1,0:T(8,128)(2,1)S(1)}, bf16[128,512]...) custom-call(f32[512,512]{1,0:T(8,128)S(1)} %score.2.refs_0_, ...), custom_call_target="tpu_custom_call" | custom-call | bytes 14760000 | tf_op jit(solution)/shard_map/norm/pallas_call | solution.py:342
  27.5 3.5 %norm.3 = (bf16[512,1024]{1,0:T(8,128)(2,1)}, bf16[512,1024]{1,0:T(8,128)(2,1)}, f32[64,1024]{1,0:T(8,128)}, bf16[512,512]{1,0:T(8,128)(2,1)S(1)}, bf16[128,512]...) custom-call(f32[512,512]{1,0:T(8,128)S(1)} %score.3.refs_0_, ...), custom_call_target="tpu_custom_call", output_to_operand_aliasing={{0}: (16, {}), {1}: (17, {}), {2}: (18, {})} | custom-call | bytes 14760000 | tf_op jit(solution)/shard_map/norm/pallas_call | solution.py:342
  31.7 1.4 %collective-permute-start.11 = (f32[128,512]{1,0:T(8,128)S(1)}, f32[128,512]{1,0:T(8,128)}, u32[]{:S(2)}, u32[]{:S(2)}) collective-permute-start(f32[128,512]{1,0:T(8,128)S(1)} %get-tuple-element.111.refs_10_), channel_id=1, source_target_pairs={{12,8},{13,9},{14,10},{15,11},{28,24},{29,25},{30,26},{31,27}} | collective-permute-start | bytes 786440 | tf_op jit(solution)/shard_map/ppermute | solution.py:363
  34.5 1.5 %collective-permute-start.10 = (f32[64,512]{1,0:T(8,128)}, f32[64,512]{1,0:T(8,128)}, u32[]{:S(2)}, u32[]{:S(2)}) collective-permute-start(f32[64,512]{1,0:T(8,128)} %add.47.refs_1_), channel_id=1, source_target_pairs={{0,2},{2,0},{1,3},{3,1},{4,6},{6,4},{5,7},{7,5},{8,10},{10,8},{9,1... | collective-permute-start | bytes 393224 | tf_op jit(solution)/shard_map/ppermute | solution.py:384
  36.0 1.4 %collective-permute-start.12 = (f32[128,512]{1,0:T(8,128)}, f32[128,512]{1,0:T(8,128)}, u32[]{:S(2)}, u32[]{:S(2)}) collective-permute-start(f32[128,512]{1,0:T(8,128)} %multiply_add_fusion.3), channel_id=1, source_target_pairs={{8,4},{9,5},{10,6},{11,7},{24,20},{25,21},{26,22},{27,23}} | collective-permute-start | bytes 786440 | tf_op jit(solution)/shard_map/ppermute | solution.py:363
  37.4 3.4 %collective-permute-done.10.refs_2_ = f32[64,512]{1,0:T(8,128)} collective-permute-done((f32[64,512]{1,0:T(8,128)}, f32[64,512]{1,0:T(8,128)}, u32[]{:S(2)}, u32[]{:S(2)}) %collective-permute-start.10) | collective-permute-done | bytes 131104 | tf_op jit(solution)/shard_map/ppermute | solution.py:384
  40.7 1.4 %halves.1 = (bf16[64,512]{1,0:T(8,128)(2,1)S(1)}, f32[64,1024]{1,0:T(8,128)S(1)}, f32[64,1024]{1,0:T(8,128)S(1)}) custom-call(s32[1]{0:T(128)} %bitcast.10.refs_0_, f32[64,512]{1,0:T(8,128)} %add.47.refs_1_, f32[64,512]{1,0:T(8,128)} %collective-permute-done.10.refs_2_, bf16[512,1024]{1,0:T(8,128)(2,1)S(1)} %copy-done.5, f32[64,1024]{1,0:T(8,128)} %get-tuple-element.107.refs_4_), custom_call_target="tpu_custom_call" | custom-call | bytes 5535000 | tf_op jit(solution)/shard_map/halves/pallas_call | solution.py:342
  43.9 7.6 %collective-permute-start.14 = (f32[64,1024]{1,0:T(8,128)S(1)}, f32[64,1024]{1,0:T(8,128)S(1)}, u32[]{:S(2)}, u32[]{:S(2)}) collective-permute-start(f32[64,1024]{1,0:T(8,128)S(1)} %get-tuple-element.120), channel_id=1, source_target_pairs={{0,4},{4,0},{8,12},{12,8},{1,5},{5,1},{9,13},{13,9},{2,6},{6,2},{1... | collective-permute-start | bytes 786440 | tf_op jit(solution)/shard_map/ppermute | solution.py:363
  54.6 1.6 %pair.2 = (bf16[512,256]{1,0:T(8,128)(2,1)}, f32[512,512]{1,0:T(8,128)S(1)}, f32[512,128]{1,0:T(8,128)S(1)}) custom-call(bf16[512,256]{1,0:T(8,128)(2,1)S(1)} %copy-done.2, bf16[512,256]{1,0:T(8,128)(2,1)S(1)} %copy-done.4, f32[8,512]{1,0:T(8,128)S(1)} %copy-done.27, f32[512,8]{1,0:T(8,128)S(1)} %get-tuple-element.78.refs_3_, ...), custom_call_target="tpu_custom_call" | custom-call | bytes 7380000 | tf_op jit(solution)/shard_map/pair/pallas_call | solution.py:342
  56.3 2.4 %collective-permute-done.14 = f32[64,1024]{1,0:T(8,128)S(1)} collective-permute-done((f32[64,1024]{1,0:T(8,128)S(1)}, f32[64,1024]{1,0:T(8,128)S(1)}, u32[]{:S(2)}, u32[]{:S(2)}) %collective-permute-start.14) | collective-permute-done | bytes 262176 | tf_op jit(solution)/shard_map/ppermute | solution.py:363
  58.7 5.6 %collective-permute-start.17 = (f32[64,1024]{1,0:T(8,128)S(1)}, f32[64,1024]{1,0:T(8,128)S(1)}, u32[]{:S(2)}, u32[]{:S(2)}) collective-permute-start(f32[64,1024]{1,0:T(8,128)S(1)} %add.50), channel_id=1, source_target_pairs={{0,8},{8,0},{4,12},{12,4},{1,9},{9,1},{5,13},{13,5},{2,10},{10,2},... | collective-permute-start | bytes 786440 | tf_op jit(solution)/shard_map/ppermute | solution.py:363
  64.9 3.4 %input.2 = (bf16[512,1024]{1,0:T(8,128)(2,1)}, bf16[512,256]{1,0:T(8,128)(2,1)}, f32[16,512]{1,0:T(8,128)}, f32[1,512]{1,0:T(1,128)S(1)}) custom-call(f32[512,512]{1,0:T(8,128)S(1)} %get-tuple-element.116.refs_0_, f32[512,128]{1,0:T(8,128)S(1)} %get-tuple-element.117.refs_1_, bf16[512,128]{1,0:T(8,128)(2,1)S(1)} %copy-done.31, ...), custom_call_target="tpu_custom_call" | custom-call | bytes 9225000 | tf_op jit(solution)/shard_map/input/pallas_call | solution.py:342
  68.4 1.6 %collective-permute-start.16 = (f32[128,512]{1,0:T(8,128)S(1)}, f32[128,512]{1,0:T(8,128)S(1)}, u32[]{:S(2)}, u32[]{:S(2)}) collective-permute-start(f32[128,512]{1,0:T(8,128)S(1)} %multiply_add_fusion), channel_id=1, source_target_pairs={{4,0},{5,1},{6,2},{7,3},{20,16},{21,17},{22,18},{23,19}} | collective-permute-start | bytes 786440 | tf_op jit(solution)/shard_map/ppermute | solution.py:363
  70.0 2.0 %pair.3 = (bf16[512,256]{1,0:T(8,128)(2,1)}, f32[512,512]{1,0:T(8,128)S(1)}, f32[512,128]{1,0:T(8,128)S(1)}) custom-call(bf16[512,256]{1,0:T(8,128)(2,1)S(1)} %copy-done.2, bf16[512,256]{1,0:T(8,128)(2,1)S(1)} %copy-done.4, f32[8,512]{1,0:T(8,128)S(1)} %get-tuple-element.125.refs_2_.refs_4_, ...), custom_call_target="tpu_custom_call", output_to_operand_aliasing={{0}: (7, {})} | custom-call | bytes 7380000 | tf_op jit(solution)/shard_map/pair/pallas_call | solution.py:342
  72.0 6.2 %collective-permute-done.17 = f32[64,1024]{1,0:T(8,128)S(1)} collective-permute-done((f32[64,1024]{1,0:T(8,128)S(1)}, f32[64,1024]{1,0:T(8,128)S(1)}, u32[]{:S(2)}, u32[]{:S(2)}) %collective-permute-start.17) | collective-permute-done | bytes 262176 | tf_op jit(solution)/shard_map/ppermute | solution.py:363
  78.4 1.4 %output.1 = bf16[512,1024]{1,0:T(8,128)(2,1)} custom-call(bf16[64,512]{1,0:T(8,128)(2,1)S(1)} %get-tuple-element.124.refs_0_, bf16[64,1024]{1,0:T(8,128)(2,1)S(1)} %copy-done.16), custom_call_target="tpu_custom_call" | custom-call | bytes 3690000 | tf_op jit(solution)/shard_map/output/pallas_call | solution.py:342
  79.8 4.0 %collective-permute-done.16.refs_9_ = f32[128,512]{1,0:T(8,128)S(1)} collective-permute-done((f32[128,512]{1,0:T(8,128)S(1)}, f32[128,512]{1,0:T(8,128)S(1)}, u32[]{:S(2)}, u32[]{:S(2)}) %collective-permute-start.16) | collective-permute-done | bytes 262176 | tf_op jit(solution)/shard_map/ppermute | solution.py:363
  83.9 3.4 %input.3 = (bf16[512,1024]{1,0:T(8,128)(2,1)}, bf16[512,256]{1,0:T(8,128)(2,1)}, f32[16,512]{1,0:T(8,128)}, f32[1,512]{1,0:T(1,128)}) custom-call(f32[512,512]{1,0:T(8,128)S(1)} %get-tuple-element.129.refs_0_, f32[512,128]{1,0:T(8,128)S(1)} %get-tuple-element.130.refs_1_, ...), custom_call_target="tpu_custom_call", output_to_operand_aliasing={{0}: (18, {}), {1}: (19, {}), {2}: (20, {})} | custom-call | bytes 9225000 | tf_op jit(solution)/shard_map/input/pallas_call | solution.py:342
  87.3 2.0 %collective-permute-done.18.refs_2_ = f32[64,1024]{1,0:T(8,128)S(1)} collective-permute-done((f32[64,1024]{1,0:T(8,128)S(1)}, f32[64,1024]{1,0:T(8,128)S(1)}, u32[]{:S(2)}, u32[]{:S(2)}) %collective-permute-start.18) | collective-permute-done | bytes 262176 | tf_op jit(solution)/shard_map/ppermute | solution.py:363
  (130 shorter events, 18.4 us)
Async XLA Ops:
  2.9 19.0 %copy-start.22 = (f32[32,512]{1,0:T(8,128)}, f32[32,512]{1,0:T(8,128)S(1)}, u32[]{:S(2)}) copy-start(f32[32,512]{1,0:T(8,128)S(1)} %get-tuple-element.97.refs_5_.refs_13_) | copy-start | bytes 196612
  2.9 19.0 %copy-start.34 = (f32[8,512]{1,0:T(8,128)}, f32[8,512]{1,0:T(8,128)S(1)}, u32[]{:S(2)}) copy-start(f32[8,512]{1,0:T(8,128)S(1)} %get-tuple-element.87.refs_6_.refs_12_) | copy-start | bytes 49156
  3.0 10.5 %collective-permute-start.2 = (f32[128,512]{1,0:T(8,128)S(1)}, f32[128,512]{1,0:T(8,128)S(1)}, u32[]{:S(2)}, u32[]{:S(2)}) collective-permute-start(f32[128,512]{1,0:T(8,128)S(1)} %get-tuple-element.91), channel_id=1, source_target_pairs={{0,4},{1,5},{2,6},{3,7},{16,20},{17,21},{18,22},{19,23}} | collective-permute-start | bytes 786440 | tf_op jit(solution)/shard_map/ppermute | solution.py:363
  8.4 6.7 %collective-permute-start.3 = (f32[64,512]{1,0:T(8,128)S(1)}, f32[64,512]{1,0:T(8,128)S(1)}, u32[]{:S(2)}, u32[]{:S(2)}) collective-permute-start(f32[64,512]{1,0:T(8,128)S(1)} %rank.1), channel_id=1, source_target_pairs={{0,1},{1,0},{2,3},{3,2},{4,5},{5,4},{6,7},{7,6},{8,9},{9,8},{10,11... | collective-permute-start | bytes 393224 | tf_op jit(solution)/shard_map/ppermute | solution.py:384
  11.8 15.7 %copy-start.24 = (f32[32,512]{1,0:T(8,128)}, f32[32,512]{1,0:T(8,128)S(1)}, u32[]{:S(2)}) copy-start(f32[32,512]{1,0:T(8,128)S(1)} %get-tuple-element.94.refs_5_.refs_13_) | copy-start | bytes 196612
  11.8 15.7 %copy-start.32 = (f32[8,512]{1,0:T(8,128)}, f32[8,512]{1,0:T(8,128)S(1)}, u32[]{:S(2)}) copy-start(f32[8,512]{1,0:T(8,128)S(1)} %get-tuple-element.86.refs_6_.refs_12_) | copy-start | bytes 49156
  11.8 7.3 %collective-permute-start = (f32[128,512]{1,0:T(8,128)S(1)}, f32[128,512]{1,0:T(8,128)S(1)}, u32[]{:S(2)}, u32[]{:S(2)}) collective-permute-start(f32[128,512]{1,0:T(8,128)S(1)} %get-tuple-element.85), channel_id=1, source_target_pairs={{0,4},{1,5},{2,6},{3,7},{16,20},{17,21},{18,22},{19,23}} | collective-permute-start | bytes 786440 | tf_op jit(solution)/shard_map/ppermute | solution.py:363
  13.1 19.9 %copy-start.42 = (f32[1,512]{1,0:T(1,128)}, f32[1,512]{1,0:T(1,128)S(1)}, u32[]{:S(2)}) copy-start(f32[1,512]{1,0:T(1,128)S(1)} %slice.7) | copy-start | bytes 6148
  13.5 6.9 %collective-permute-start.6 = (f32[128,512]{1,0:T(8,128)S(1)}, f32[128,512]{1,0:T(8,128)S(1)}, u32[]{:S(2)}, u32[]{:S(2)}) collective-permute-start(f32[128,512]{1,0:T(8,128)S(1)} %multiply_add_fusion.6), channel_id=1, source_target_pairs={{4,8},{5,9},{6,10},{7,11},{20,24},{21,25},{22,26},{23,27}} | collective-permute-start | bytes 786440 | tf_op jit(solution)/shard_map/ppermute | solution.py:363
  15.2 5.2 %collective-permute-start.4 = (f32[64,512]{1,0:T(8,128)S(1)}, f32[64,512]{1,0:T(8,128)S(1)}, u32[]{:S(2)}, u32[]{:S(2)}) collective-permute-start(f32[64,512]{1,0:T(8,128)S(1)} %add.42.refs_12_), channel_id=1, source_target_pairs={{0,2},{2,0},{1,3},{3,1},{4,6},{6,4},{5,7},{7,5},{8,10},{10,8},{9,1... | collective-permute-start | bytes 393224 | tf_op jit(solution)/shard_map/ppermute | solution.py:384
  19.2 2.0 %collective-permute-start.1 = (f32[128,512]{1,0:T(8,128)S(1)}, f32[128,512]{1,0:T(8,128)S(1)}, u32[]{:S(2)}, u32[]{:S(2)}) collective-permute-start(f32[128,512]{1,0:T(8,128)S(1)} %multiply_add_fusion.7), channel_id=1, source_target_pairs={{4,8},{5,9},{6,10},{7,11},{20,24},{21,25},{22,26},{23,27}} | collective-permute-start | bytes 786440 | tf_op jit(solution)/shard_map/ppermute | solution.py:363
  20.4 1.5 %collective-permute-start.7 = (f32[128,512]{1,0:T(8,128)S(1)}, f32[128,512]{1,0:T(8,128)S(1)}, u32[]{:S(2)}, u32[]{:S(2)}) collective-permute-start(f32[128,512]{1,0:T(8,128)S(1)} %multiply_add_fusion.4), channel_id=1, source_target_pairs={{8,12},{9,13},{10,14},{11,15},{24,28},{25,29},{26,30},{27,31}} | collective-permute-start | bytes 786440 | tf_op jit(solution)/shard_map/ppermute | solution.py:363
  21.2 6.3 %collective-permute-start.5 = (f32[128,512]{1,0:T(8,128)S(1)}, f32[128,512]{1,0:T(8,128)S(1)}, u32[]{:S(2)}, u32[]{:S(2)}) collective-permute-start(f32[128,512]{1,0:T(8,128)S(1)} %multiply_add_fusion.5), channel_id=1, source_target_pairs={{8,12},{9,13},{10,14},{11,15},{24,28},{25,29},{26,30},{27,31}} | collective-permute-start | bytes 786440 | tf_op jit(solution)/shard_map/ppermute | solution.py:363
  26.8 6.2 %collective-permute-start.8 = (f32[128,512]{1,0:T(8,128)S(1)}, f32[128,512]{1,0:T(8,128)S(1)}, u32[]{:S(2)}, u32[]{:S(2)}) collective-permute-start(f32[128,512]{1,0:T(8,128)S(1)} %get-tuple-element.105.refs_10_), channel_id=1, source_target_pairs={{12,8},{13,9},{14,10},{15,11},{28,24},{29,25},{30,26},{31,27}} | collective-permute-start | bytes 786440 | tf_op jit(solution)/shard_map/ppermute | solution.py:363
  31.7 2.2 %collective-permute-start.9 = (f32[64,512]{1,0:T(8,128)S(1)}, f32[64,512]{1,0:T(8,128)S(1)}, u32[]{:S(2)}, u32[]{:S(2)}) collective-permute-start(f32[64,512]{1,0:T(8,128)S(1)} %get-tuple-element.106), channel_id=1, source_target_pairs={{0,1},{1,0},{2,3},{3,2},{4,5},{5,4},{6,7},{7,6},{8,9},{9,8},{10,11... | collective-permute-start | bytes 393224 | tf_op jit(solution)/shard_map/ppermute | solution.py:384
  31.7 10.5 %collective-permute-start.11 = (f32[128,512]{1,0:T(8,128)S(1)}, f32[128,512]{1,0:T(8,128)}, u32[]{:S(2)}, u32[]{:S(2)}) collective-permute-start(f32[128,512]{1,0:T(8,128)S(1)} %get-tuple-element.111.refs_10_), channel_id=1, source_target_pairs={{12,8},{13,9},{14,10},{15,11},{28,24},{29,25},{30,26},{31,27}} | collective-permute-start | bytes 786440 | tf_op jit(solution)/shard_map/ppermute | solution.py:363
  34.5 6.2 %collective-permute-start.10 = (f32[64,512]{1,0:T(8,128)}, f32[64,512]{1,0:T(8,128)}, u32[]{:S(2)}, u32[]{:S(2)}) collective-permute-start(f32[64,512]{1,0:T(8,128)} %add.47.refs_1_), channel_id=1, source_target_pairs={{0,2},{2,0},{1,3},{3,1},{4,6},{6,4},{5,7},{7,5},{8,10},{10,8},{9,1... | collective-permute-start | bytes 393224 | tf_op jit(solution)/shard_map/ppermute | solution.py:384
  36.0 15.5 %collective-permute-start.12 = (f32[128,512]{1,0:T(8,128)}, f32[128,512]{1,0:T(8,128)}, u32[]{:S(2)}, u32[]{:S(2)}) collective-permute-start(f32[128,512]{1,0:T(8,128)} %multiply_add_fusion.3), channel_id=1, source_target_pairs={{8,4},{9,5},{10,6},{11,7},{24,20},{25,21},{26,22},{27,23}} | collective-permute-start | bytes 786440 | tf_op jit(solution)/shard_map/ppermute | solution.py:363
  43.9 14.8 %collective-permute-start.14 = (f32[64,1024]{1,0:T(8,128)S(1)}, f32[64,1024]{1,0:T(8,128)S(1)}, u32[]{:S(2)}, u32[]{:S(2)}) collective-permute-start(f32[64,1024]{1,0:T(8,128)S(1)} %get-tuple-element.120), channel_id=1, source_target_pairs={{0,4},{4,0},{8,12},{12,8},{1,5},{5,1},{9,13},{13,9},{2,6},{6,2},{1... | collective-permute-start | bytes 786440 | tf_op jit(solution)/shard_map/ppermute | solution.py:363
  52.6 11.7 %collective-permute-start.13 = (f32[128,512]{1,0:T(8,128)S(1)}, f32[128,512]{1,0:T(8,128)S(1)}, u32[]{:S(2)}, u32[]{:S(2)}) collective-permute-start(f32[128,512]{1,0:T(8,128)S(1)} %multiply_add_fusion.1), channel_id=1, source_target_pairs={{4,0},{5,1},{6,2},{7,3},{20,16},{21,17},{22,18},{23,19}} | collective-permute-start | bytes 786440 | tf_op jit(solution)/shard_map/ppermute | solution.py:363
  53.9 14.5 %collective-permute-start.15 = (f32[128,512]{1,0:T(8,128)S(1)}, f32[128,512]{1,0:T(8,128)S(1)}, u32[]{:S(2)}, u32[]{:S(2)}) collective-permute-start(f32[128,512]{1,0:T(8,128)S(1)} %multiply_add_fusion.2), channel_id=1, source_target_pairs={{8,4},{9,5},{10,6},{11,7},{24,20},{25,21},{26,22},{27,23}} | collective-permute-start | bytes 786440 | tf_op jit(solution)/shard_map/ppermute | solution.py:363
  58.7 19.5 %collective-permute-start.17 = (f32[64,1024]{1,0:T(8,128)S(1)}, f32[64,1024]{1,0:T(8,128)S(1)}, u32[]{:S(2)}, u32[]{:S(2)}) collective-permute-start(f32[64,1024]{1,0:T(8,128)S(1)} %add.50), channel_id=1, source_target_pairs={{0,8},{8,0},{4,12},{12,4},{1,9},{9,1},{5,13},{13,5},{2,10},{10,2},... | collective-permute-start | bytes 786440 | tf_op jit(solution)/shard_map/ppermute | solution.py:363
  68.4 15.4 %collective-permute-start.16 = (f32[128,512]{1,0:T(8,128)S(1)}, f32[128,512]{1,0:T(8,128)S(1)}, u32[]{:S(2)}, u32[]{:S(2)}) collective-permute-start(f32[128,512]{1,0:T(8,128)S(1)} %multiply_add_fusion), channel_id=1, source_target_pairs={{4,0},{5,1},{6,2},{7,3},{20,16},{21,17},{22,18},{23,19}} | collective-permute-start | bytes 786440 | tf_op jit(solution)/shard_map/ppermute | solution.py:363
  78.3 11.0 %collective-permute-start.18 = (f32[64,1024]{1,0:T(8,128)S(1)}, f32[64,1024]{1,0:T(8,128)S(1)}, u32[]{:S(2)}, u32[]{:S(2)}) collective-permute-start(f32[64,1024]{1,0:T(8,128)S(1)} %add.52.refs_1_), channel_id=1, source_target_pairs={{0,4},{4,0},{8,12},{12,8},{1,5},{5,1},{9,13},{13,9},{2,6},{6,2},{1... | collective-permute-start | bytes 786440 | tf_op jit(solution)/shard_map/ppermute | solution.py:363
  (39 other events, 154.5 us)

commit v3 on v2

--- a/solution.py
+++ b/solution.py
@@ -144,8 +144,9 @@
     (gu_here, gu_there, down) = refs[12:15]
     refs = refs[15:]
     u_before = None if first == 0 else refs.pop(0)
-    (mixed, gate_grad, down_part, gye, scaled, state_grad, u_part, y_dot) = refs[:8]
-    (inner, falls, g_mixed, product) = refs[8:]
+    (mixed, gate_grad, down_part, gye, scaled, state_grad, u_part, y_dot, decay) = refs[:9]
+    (inner, falls, g_mixed, product) = refs[9:]
+    decay[...] = rows[0:1]
     length, channels = x.shape
     heads = channels // HEAD
     skip = head_column(skips[...], heads, first)
@@ -181,7 +182,7 @@
         product[1, at] = low
         return carry
 
-    lax.fori_loop(0, length // ROWS, tile, 0, unroll=4)
+    lax.fori_loop(0, length // ROWS, tile, 0, unroll=length // ROWS)
     state_grad[...] = dot(cstart[...], gye[...], 0, 0) * rows[1:2]
     u_here = dot(down[...], mixed[...], 1, 1)
     u_part[...] = u_here if first == 0 else u_here + u_before[...]
@@ -259,7 +260,7 @@
         product[1, at] = low
         return carry
 
-    lax.fori_loop(0, length // ROWS, tile, 0, unroll=4)
+    lax.fori_loop(0, length // ROWS, tile, 0, unroll=length // ROWS)
     carried = dot(xw[...], scaled, 1, 1)
     to_end = ids_col[:, 0:1] == ids_row[0:1, length - 1 :]
     b_grad[...] = (b_loc[...] + jnp.where(to_end, carried, 0.0)).astype(bf16)
@@ -455,7 +456,7 @@
             [
                 fresh((length, width), bf16),
                 fresh((STATE, width), f32),
-                fresh((length, STATE), bf16),
+                slow(fresh((length, STATE), bf16)),
                 fresh((length, STATE), bf16),
                 fresh((4 * heads, length), f32),
                 fresh((8, width), f32),
@@ -466,8 +467,9 @@
             name="state",
         )
 
-    def score_call(g):
+    def score_call(g, *before):
         xw, _, _, _, _, _, ids_row, ids_col = states[g]
+        ids_row = after(ids_row, *before) if before else ids_row
         return call(
             score_kernel,
             [
@@ -482,29 +484,41 @@
             name="score",
         )[0]
 
-    states, y_locs = [], []
-    for g in everything:
-        states.append(state_call(g, after(rates, y_locs[-1]) if g else rates))
-        y_locs.append(score_call(g))
-    (gu_part,) = call(
-        rank_kernel,
-        [whole(after(adapter_up_map, states[0][5])), whole(layer_output_gradient)],
-        [fresh((rank, length), f32)],
-        cost=1.0,
-        name="rank",
-    )
+    def rank_call(*before):
+        return call(
+            rank_kernel,
+            [
+                whole(after(adapter_up_map, *before) if before else adapter_up_map),
+                whole(layer_output_gradient),
+            ],
+            [fresh((rank, length), f32)],
+            cost=1.0,
+            name="rank",
+        )[0]
+
+    states, y_locs = [state_call(0, rates)], []
+    gu_part = rank_call(states[0][5])
+    for g in range(1, groups):
+        states.append(state_call(g, after(rates, gu_part)))
+
     parts = [states[g][1] for g in everything]
     decays = [states[g][5][0:1] for g in everything]
     entering = []
     if short:
         first = [hop(parts[g], "ctx", (0, 1)) for g in everything]
-        joined = [after(decays[g], parts[-1], gu_part) * first[g] + parts[g] for g in everything]
-        gu = exchange_pair(gu_part, ("fsdp", "head"), joined[0])
-        for g in everything:
-            second = hop(joined[g], "ctx", (1, 2))
-            third = after(decays[g], y_locs[-1], gu[1]) * second + parts[g]
-            entering.append((first[g], second, hop(third, "ctx", (2, 3))))
+        gu = exchange_pair(gu_part, ("fsdp", "head"), states[-1][5])
+        y_locs.append(score_call(0, gu[0]))
+        joined = [after(decays[g], y_locs[0]) * first[g] + parts[g] for g in everything]
+        second = [hop(joined[g], "ctx", (1, 2)) for g in everything]
+        joined = decays[0] * second[0] + parts[0]
+        third = [hop(joined, "ctx", (2, 3))]
+        for g in range(1, groups):
+            y_locs.append(score_call(g, joined))
+            joined = after(decays[g], y_locs[-1], gu[1]) * second[g] + parts[g]
+            third.append(hop(joined, "ctx", (2, 3)))
+        entering = list(zip(first, second, third))
     else:
+        y_locs = [score_call(g) for g in everything]
         gu = exchange_pair(gu_part, ("fsdp", "head"))
         entering = [chain(parts[g], decays[g], "ctx", False) for g in everything]
     mixed = gate_grad = down_part = u_part = c_grad = None
@@ -555,11 +569,12 @@
                 ((length, channels), bf16, (length, width), (0, g), mixed),
                 ((length, channels), bf16, (length, width), (0, g), gate_grad),
                 slow(((rank, channels), f32, (rank, width), (0, g), down_part)),
-                fresh((length, width), bf16),
-                fresh((STATE, width), bf16),
+                (slow if g < groups - 1 else tuple)(fresh((length, width), bf16)),
+                slow(fresh((STATE, width), bf16)),
                 fresh((STATE, width), f32),
                 fresh((rank, length), f32),
                 slow(fresh((heads, length), f32)),
+                fresh((1, width), f32),
             ],
             [
                 pltpu.VMEM((length, width), f32),
@@ -570,8 +585,8 @@
             cost=4.0,
             name="norm",
         )
-        mixed, gate_grad, down_part, gye, scaled, state_grad, u_part, y_dot = results
-        normed.append((gye, scaled, state_grad, y_dot))
+        mixed, gate_grad, down_part, gye, scaled, state_grad, u_part, y_dot, decay = results
+        normed.append((gye, scaled, state_grad, y_dot, decay))
     def input_call(g, leaving, held, passing, *before):
         xw, state, bend, cstart, small, rows, ids_row, ids_col = states[g]
         x_grad, b_grad, step_grad = held
@@ -612,6 +627,7 @@
         )
 
     state_grads = [normed[g][2] for g in everything]
+    decays = [normed[g][4] for g in everything]
     held = (None, None, None)
     if short and groups == 2:
         neighbours = [(0, 1), (1, 0), (2, 3), (3, 2)]
@@ -641,20 +657,20 @@
         ahead = [hop(sent, "ctx", (1, 0))]
         c_grad, *pair = pair_call(0, c_grad, sent)
         pairs.append(pair)
-        keep = after(keep, pair[1]) + got
+        sent = after(decays[1], pair[1]) * then[1] + state_grads[1]
+        ahead.append(hop(sent, "ctx", (1, 0)))
+        keep = after(keep, sent) + got
         got = hop(keep, "ctx", *across)
-        *held, decay = input_call(0, (last[0], then[0], ahead[0]), held, decays[1], keep)
-        sent = decay * then[1] + state_grads[1]
-        ahead.append(hop(sent, "ctx", (1, 0)))
-        c_grad, *pair = pair_call(1, c_grad, sent)
+        c_grad, *pair = pair_call(1, c_grad, keep)
         pairs.append(pair)
+        *held, _ = input_call(0, (last[0], then[0], ahead[0]), held, decays[1], pair[1])
         (adapter_output,) = call(
             output_kernel,
-            [whole(after(u, sent)), whole(adapter_up_map)],
+            [whole(after(u, pair[1])), whole(adapter_up_map)],
             [fresh((length, channels), bf16)],
             name="output",
         )
-        keep = after(keep, sent, pair[1]) + got
+        keep = after(keep, held[2]) + got
         got = hop(keep, "ctx", *neighbours)
         *held, _ = input_call(1, (last[1], then[1], ahead[1]), held, decays[1])
         up_sum, down_sum = call(

time: 90.7 us -> 82.5 us (0.910)
  starting transfers between devices: 32.6 us -> 29.4 us
  waiting for transfers between devices: 21.1 us -> 19.2 us
  Pallas kernels: 27.2 us -> 25.6 us
  local copies, waits for them, and re-layouts: 4.15 us -> 2.65 us
    ppermute x15, waiting for transfers between devices: 17.3 us -> 13.5 us  [hop(): return lax.ppermute(part, axis, list(pairs))]
    ppermute x15, starting transfers between devices: 29.5 us -> 26.3 us  [hop(): return lax.ppermute(part, axis, list(pairs))]
    ppermute x4, waiting for transfers between devices: 3.77 us -> 5.71 us  [exchange_pair(): other = lax.ppermute(part, axis, [(i, i ^ span) for i in range(count)])]
    pallas_call x14, Pallas kernels: 27.2 us -> 25.6 us  [call(): pl.pallas_call(body, grid=(1,), in_specs=in_specs, out_specs=out_specs, o...]
    unnamed x88 -> x74, local copies, waits for them, and re-layouts: 4.14 us -> 2.65 us
  transfers between devices with their start and end apart: 19 -> 19, of which waited for: 8 -> 7; matrix products, arithmetic and copies ran while one was open for 4% -> 5% of each run, Pallas kernels for 27% -> 27%
where the time goes in v3:
time: 82.5 us; the launch traced here: 82 us
  starting transfers between devices  29.4 us (36%)
  Pallas kernels  25.6 us (31%)
  waiting for transfers between devices  19.2 us (23%)
  other arithmetic  3.82 us (5%)
  local copies, waits for them, and re-layouts  2.65 us (3%)
  between operations  1.22 us (1%)
    ppermute x15, starting transfers between devices, hop(): return lax.ppermute(part, axis, list(pairs))  26.3 us
    pallas_call x14, Pallas kernels, call(): pl.pallas_call(body, grid=(1,), in_specs=in_specs, out_specs=out_specs, o...  25.6 us
    ppermute x15, waiting for transfers between devices, hop(): return lax.ppermute(part, axis, list(pairs))  13.5 us
    ppermute x4, waiting for transfers between devices, exchange_pair(): other = lax.ppermute(part, axis, [(i, i ^ span) for i in range(count)])  5.71 us
    ppermute x4, starting transfers between devices, exchange_pair(): other = lax.ppermute(part, axis, [(i, i ^ span) for i in range(count)])  3.12 us
    unnamed x74, local copies, waits for them, and re-layouts  2.65 us
  transfers between devices with their start and end apart: 19, of which 7 were waited for; matrix products, arithmetic and copies ran while one was open for 5% of the time, Pallas kernels for 27%

profile of v3, /device:TPU:0, one launch (start us, length us, event | category | flops | bytes accessed | tf_op | source)
XLA Modules:
  0.0 82.0 jit_solution(4743422569247927578)
XLA Ops:
  0.7 2.6 %state.2 = (bf16[512,512]{1,0:T(8,128)(2,1)S(1)}, f32[128,512]{1,0:T(8,128)S(1)}, bf16[512,128]{1,0:T(8,128)(2,1)}, bf16[512,128]{1,0:T(8,128)(2,1)S(1)}, f32[32...) custom-call(bf16[512,1024]{1,0:T(8,128)(2,1)} %refs_7_.3, ...), custom_call_target="tpu_custom_call" | custom-call | bytes 5535000 | tf_op jit(solution)/shard_map/state/pallas_call | solution.py:343
  3.2 4.9 %collective-permute-start.1 = (f32[128,512]{1,0:T(8,128)S(1)}, f32[128,512]{1,0:T(8,128)S(1)}, u32[]{:S(2)}, u32[]{:S(2)}) collective-permute-start(f32[128,512]{1,0:T(8,128)S(1)} %get-tuple-element.91), channel_id=1, source_target_pairs={{0,4},{1,5},{2,6},{3,7},{16,20},{17,21},{18,22},{19,23}} | collective-permute-start | bytes 786440 | tf_op jit(solution)/shard_map/ppermute | solution.py:364
  8.7 2.5 %state.3 = (bf16[512,512]{1,0:T(8,128)(2,1)S(1)}, f32[128,512]{1,0:T(8,128)S(1)}, bf16[512,128]{1,0:T(8,128)(2,1)}, bf16[512,128]{1,0:T(8,128)(2,1)S(1)}, f32[32...) custom-call(bf16[512,1024]{1,0:T(8,128)(2,1)} %refs_7_.3, ...), custom_call_target="tpu_custom_call" | custom-call | bytes 5535000 | tf_op jit(solution)/shard_map/state/pallas_call | solution.py:343
  11.2 1.4 %collective-permute-start.3 = (f32[128,512]{1,0:T(8,128)S(1)}, f32[128,512]{1,0:T(8,128)S(1)}, u32[]{:S(2)}, u32[]{:S(2)}) collective-permute-start(f32[128,512]{1,0:T(8,128)S(1)} %get-tuple-element.96), channel_id=1, source_target_pairs={{0,4},{1,5},{2,6},{3,7},{16,20},{17,21},{18,22},{19,23}} | collective-permute-start | bytes 786440 | tf_op jit(solution)/shard_map/ppermute | solution.py:364
  14.6 4.8 %collective-permute-done.3.refs_2_ = f32[128,512]{1,0:T(8,128)S(1)} collective-permute-done((f32[128,512]{1,0:T(8,128)S(1)}, f32[128,512]{1,0:T(8,128)S(1)}, u32[]{:S(2)}, u32[]{:S(2)}) %collective-permute-start.3) | collective-permute-done | bytes 262176 | tf_op jit(solution)/shard_map/ppermute | solution.py:364
  20.1 1.6 %collective-permute-start.5 = (f32[64,512]{1,0:T(8,128)S(1)}, f32[64,512]{1,0:T(8,128)S(1)}, u32[]{:S(2)}, u32[]{:S(2)}) collective-permute-start(f32[64,512]{1,0:T(8,128)S(1)} %add.40.refs_12_), channel_id=1, source_target_pairs={{0,2},{2,0},{1,3},{3,1},{4,6},{6,4},{5,7},{7,5},{8,10},{10,8},{9,1... | collective-permute-start | bytes 393224 | tf_op jit(solution)/shard_map/ppermute | solution.py:385
  23.2 2.3 %collective-permute-done.5.refs_13_ = f32[64,512]{1,0:T(8,128)S(1)} collective-permute-done((f32[64,512]{1,0:T(8,128)S(1)}, f32[64,512]{1,0:T(8,128)S(1)}, u32[]{:S(2)}, u32[]{:S(2)}) %collective-permute-start.5) | collective-permute-done | bytes 131104 | tf_op jit(solution)/shard_map/ppermute | solution.py:385
  27.0 2.8 %norm.2 = (bf16[512,1024]{1,0:T(8,128)(2,1)}, bf16[512,1024]{1,0:T(8,128)(2,1)}, f32[64,1024]{1,0:T(8,128)}, bf16[512,512]{1,0:T(8,128)(2,1)}, bf16[128,512]{1,0...) custom-call(f32[512,512]{1,0:T(8,128)S(1)} %score.2.refs_0_, ...), custom_call_target="tpu_custom_call" | custom-call | bytes 14760000 | tf_op jit(solution)/shard_map/norm/pallas_call | solution.py:343
  30.5 2.8 %norm.3 = (bf16[512,1024]{1,0:T(8,128)(2,1)}, bf16[512,1024]{1,0:T(8,128)(2,1)}, f32[64,1024]{1,0:T(8,128)}, bf16[512,512]{1,0:T(8,128)(2,1)S(1)}, bf16[128,512]...) custom-call(f32[512,512]{1,0:T(8,128)S(1)} %score.3.refs_0_, ...), custom_call_target="tpu_custom_call", output_to_operand_aliasing={{0}: (16, {}), {1}: (17, {}), {2}: (18, {})} | custom-call | bytes 14760000 | tf_op jit(solution)/shard_map/norm/pallas_call | solution.py:343
  33.9 1.4 %collective-permute-start.11 = (f32[128,512]{1,0:T(8,128)S(1)}, f32[128,512]{1,0:T(8,128)}, u32[]{:S(2)}, u32[]{:S(2)}) collective-permute-start(f32[128,512]{1,0:T(8,128)S(1)} %get-tuple-element.117.refs_10_), channel_id=1, source_target_pairs={{12,8},{13,9},{14,10},{15,11},{28,24},{29,25},{30,26},{31,27}} | collective-permute-start | bytes 786440 | tf_op jit(solution)/shard_map/ppermute | solution.py:364
  36.7 1.5 %collective-permute-start.10 = (f32[64,512]{1,0:T(8,128)}, f32[64,512]{1,0:T(8,128)}, u32[]{:S(2)}, u32[]{:S(2)}) collective-permute-start(f32[64,512]{1,0:T(8,128)} %add.47.refs_1_), channel_id=1, source_target_pairs={{0,2},{2,0},{1,3},{3,1},{4,6},{6,4},{5,7},{7,5},{8,10},{10,8},{9,1... | collective-permute-start | bytes 393224 | tf_op jit(solution)/shard_map/ppermute | solution.py:385
  39.6 3.4 %collective-permute-done.10.refs_2_ = f32[64,512]{1,0:T(8,128)} collective-permute-done((f32[64,512]{1,0:T(8,128)}, f32[64,512]{1,0:T(8,128)}, u32[]{:S(2)}, u32[]{:S(2)}) %collective-permute-start.10) | collective-permute-done | bytes 131104 | tf_op jit(solution)/shard_map/ppermute | solution.py:385
  42.9 1.4 %halves.1 = (bf16[64,512]{1,0:T(8,128)(2,1)S(1)}, f32[64,1024]{1,0:T(8,128)S(1)}, f32[64,1024]{1,0:T(8,128)S(1)}) custom-call(s32[1]{0:T(128)} %bitcast.10.refs_0_, f32[64,512]{1,0:T(8,128)} %add.47.refs_1_, f32[64,512]{1,0:T(8,128)} %collective-permute-done.10.refs_2_, bf16[512,1024]{1,0:T(8,128)(2,1)S(1)} %copy-done.3, f32[64,1024]{1,0:T(8,128)} %get-tuple-element.112.refs_4_), custom_call_target="tpu_custom_call" | custom-call | bytes 5535000 | tf_op jit(solution)/shard_map/halves/pallas_call | solution.py:343
  46.9 4.3 %collective-permute-start.14 = (f32[64,1024]{1,0:T(8,128)S(1)}, f32[64,1024]{1,0:T(8,128)S(1)}, u32[]{:S(2)}, u32[]{:S(2)}) collective-permute-start(f32[64,1024]{1,0:T(8,128)S(1)} %get-tuple-element.125), channel_id=1, source_target_pairs={{0,4},{4,0},{8,12},{12,8},{1,5},{5,1},{9,13},{13,9},{2,6},{6,2},{1... | collective-permute-start | bytes 786440 | tf_op jit(solution)/shard_map/ppermute | solution.py:364
  53.6 1.6 %pair.2 = (bf16[512,256]{1,0:T(8,128)(2,1)}, f32[512,512]{1,0:T(8,128)S(1)}, f32[512,128]{1,0:T(8,128)S(1)}) custom-call(bf16[512,256]{1,0:T(8,128)(2,1)S(1)} %copy-done.1, bf16[512,256]{1,0:T(8,128)(2,1)S(1)} %copy-done.2, f32[8,512]{1,0:T(8,128)S(1)} %copy-done.22, f32[512,8]{1,0:T(8,128)S(1)} %get-tuple-element.88.refs_3_, ...), custom_call_target="tpu_custom_call" | custom-call | bytes 7380000 | tf_op jit(solution)/shard_map/pair/pallas_call | solution.py:343
  55.3 3.1 %collective-permute-done.14 = f32[64,1024]{1,0:T(8,128)S(1)} collective-permute-done((f32[64,1024]{1,0:T(8,128)S(1)}, f32[64,1024]{1,0:T(8,128)S(1)}, u32[]{:S(2)}, u32[]{:S(2)}) %collective-permute-start.14) | collective-permute-done | bytes 262176 | tf_op jit(solution)/shard_map/ppermute | solution.py:364
  58.4 5.2 %collective-permute-start.17 = (f32[64,1024]{1,0:T(8,128)S(1)}, f32[64,1024]{1,0:T(8,128)S(1)}, u32[]{:S(2)}, u32[]{:S(2)}) collective-permute-start(f32[64,1024]{1,0:T(8,128)S(1)} %add.51), channel_id=1, source_target_pairs={{0,8},{8,0},{4,12},{12,4},{1,9},{9,1},{5,13},{13,5},{2,10},{10,2},... | collective-permute-start | bytes 786440 | tf_op jit(solution)/shard_map/ppermute | solution.py:364
  63.6 1.5 %collective-permute-start.15 = (f32[128,512]{1,0:T(8,128)S(1)}, f32[128,512]{1,0:T(8,128)S(1)}, u32[]{:S(2)}, u32[]{:S(2)}) collective-permute-start(f32[128,512]{1,0:T(8,128)S(1)} %multiply_add_fusion), channel_id=1, source_target_pairs={{4,0},{5,1},{6,2},{7,3},{20,16},{21,17},{22,18},{23,19}} | collective-permute-start | bytes 786440 | tf_op jit(solution)/shard_map/ppermute | solution.py:364
  65.1 2.0 %pair.3 = (bf16[512,256]{1,0:T(8,128)(2,1)}, f32[512,512]{1,0:T(8,128)S(1)}, f32[512,128]{1,0:T(8,128)S(1)}) custom-call(bf16[512,256]{1,0:T(8,128)(2,1)S(1)} %copy-done.1, bf16[512,256]{1,0:T(8,128)(2,1)S(1)} %copy-done.2, f32[8,512]{1,0:T(8,128)S(1)} %get-tuple-element.126.refs_2_.refs_4_, ...), custom_call_target="tpu_custom_call", output_to_operand_aliasing={{0}: (7, {})} | custom-call | bytes 7380000 | tf_op jit(solution)/shard_map/pair/pallas_call | solution.py:343
  67.8 2.9 %input.2 = (bf16[512,1024]{1,0:T(8,128)(2,1)}, bf16[512,256]{1,0:T(8,128)(2,1)}, f32[16,512]{1,0:T(8,128)}, f32[1,512]{1,0:T(1,128)}) custom-call(f32[512,512]{1,0:T(8,128)S(1)} %get-tuple-element.135.refs_0_, f32[512,128]{1,0:T(8,128)S(1)} %get-tuple-element.122.refs_1_, bf16[512,128]{1,0:T(8,128)(2,1)S(1)} %copy-done.24, ...), custom_call_target="tpu_custom_call" | custom-call | bytes 9225000 | tf_op jit(solution)/shard_map/input/pallas_call | solution.py:343
  70.7 3.0 %collective-permute-done.17 = f32[64,1024]{1,0:T(8,128)S(1)} collective-permute-done((f32[64,1024]{1,0:T(8,128)S(1)}, f32[64,1024]{1,0:T(8,128)S(1)}, u32[]{:S(2)}, u32[]{:S(2)}) %collective-permute-start.17) | collective-permute-done | bytes 262176 | tf_op jit(solution)/shard_map/ppermute | solution.py:364
  74.4 1.4 %output.1 = bf16[512,1024]{1,0:T(8,128)(2,1)} custom-call(bf16[64,512]{1,0:T(8,128)(2,1)S(1)} %get-tuple-element.131.refs_0_, bf16[64,1024]{1,0:T(8,128)(2,1)S(1)} %copy-done.13), custom_call_target="tpu_custom_call" | custom-call | bytes 3690000 | tf_op jit(solution)/shard_map/output/pallas_call | solution.py:343
  75.8 3.0 %input.3 = (bf16[512,1024]{1,0:T(8,128)(2,1)}, bf16[512,256]{1,0:T(8,128)(2,1)}, f32[16,512]{1,0:T(8,128)}, f32[1,512]{1,0:T(1,128)}) custom-call(f32[512,512]{1,0:T(8,128)S(1)} %get-tuple-element.132.refs_0_, f32[512,128]{1,0:T(8,128)S(1)} %get-tuple-element.130.refs_1_, ...), custom_call_target="tpu_custom_call", output_to_operand_aliasing={{0}: (18, {}), {1}: (19, {}), {2}: (20, {})} | custom-call | bytes 9225000 | tf_op jit(solution)/shard_map/input/pallas_call | solution.py:343
  78.8 2.3 %collective-permute-done.18.refs_2_ = f32[64,1024]{1,0:T(8,128)S(1)} collective-permute-done((f32[64,1024]{1,0:T(8,128)S(1)}, f32[64,1024]{1,0:T(8,128)S(1)}, u32[]{:S(2)}, u32[]{:S(2)}) %collective-permute-start.18) | collective-permute-done | bytes 262176 | tf_op jit(solution)/shard_map/ppermute | solution.py:364
  (116 shorter events, 17.2 us)
Async XLA Ops:
  3.2 23.1 %copy-start.17 = (f32[32,512]{1,0:T(8,128)}, f32[32,512]{1,0:T(8,128)S(1)}, u32[]{:S(2)}) copy-start(f32[32,512]{1,0:T(8,128)S(1)} %get-tuple-element.101.refs_5_.refs_13_) | copy-start | bytes 196612
  3.2 23.1 %copy-start.27 = (f32[8,512]{1,0:T(8,128)}, f32[8,512]{1,0:T(8,128)S(1)}, u32[]{:S(2)}) copy-start(f32[8,512]{1,0:T(8,128)S(1)} %get-tuple-element.80.refs_6_.refs_12_) | copy-start | bytes 49156
  3.2 10.6 %collective-permute-start.1 = (f32[128,512]{1,0:T(8,128)S(1)}, f32[128,512]{1,0:T(8,128)S(1)}, u32[]{:S(2)}, u32[]{:S(2)}) collective-permute-start(f32[128,512]{1,0:T(8,128)S(1)} %get-tuple-element.91), channel_id=1, source_target_pairs={{0,4},{1,5},{2,6},{3,7},{16,20},{17,21},{18,22},{19,23}} | collective-permute-start | bytes 786440 | tf_op jit(solution)/shard_map/ppermute | solution.py:364
  8.6 4.1 %collective-permute-start = (f32[64,512]{1,0:T(8,128)S(1)}, f32[64,512]{1,0:T(8,128)S(1)}, u32[]{:S(2)}, u32[]{:S(2)}) collective-permute-start(f32[64,512]{1,0:T(8,128)S(1)} %rank.1), channel_id=1, source_target_pairs={{0,1},{1,0},{2,3},{3,2},{4,5},{5,4},{6,7},{7,6},{8,9},{9,8},{10,11... | collective-permute-start | bytes 393224 | tf_op jit(solution)/shard_map/ppermute | solution.py:385
  11.2 19.2 %copy-start.19 = (f32[32,512]{1,0:T(8,128)}, f32[32,512]{1,0:T(8,128)S(1)}, u32[]{:S(2)}) copy-start(f32[32,512]{1,0:T(8,128)S(1)} %get-tuple-element.99.refs_5_.refs_13_) | copy-start | bytes 196612
  11.2 19.2 %copy-start.25 = (f32[8,512]{1,0:T(8,128)}, f32[8,512]{1,0:T(8,128)S(1)}, u32[]{:S(2)}) copy-start(f32[8,512]{1,0:T(8,128)S(1)} %get-tuple-element.85.refs_6_.refs_12_) | copy-start | bytes 49156
  11.2 8.1 %collective-permute-start.3 = (f32[128,512]{1,0:T(8,128)S(1)}, f32[128,512]{1,0:T(8,128)S(1)}, u32[]{:S(2)}, u32[]{:S(2)}) collective-permute-start(f32[128,512]{1,0:T(8,128)S(1)} %get-tuple-element.96), channel_id=1, source_target_pairs={{0,4},{1,5},{2,6},{3,7},{16,20},{17,21},{18,22},{19,23}} | collective-permute-start | bytes 786440 | tf_op jit(solution)/shard_map/ppermute | solution.py:364
  13.9 7.7 %collective-permute-start.2 = (f32[128,512]{1,0:T(8,128)S(1)}, f32[128,512]{1,0:T(8,128)S(1)}, u32[]{:S(2)}, u32[]{:S(2)}) collective-permute-start(f32[128,512]{1,0:T(8,128)S(1)} %multiply_add_fusion.7), channel_id=1, source_target_pairs={{4,8},{5,9},{6,10},{7,11},{20,24},{21,25},{22,26},{23,27}} | collective-permute-start | bytes 786440 | tf_op jit(solution)/shard_map/ppermute | solution.py:364
  19.4 6.2 %collective-permute-start.4 = (f32[128,512]{1,0:T(8,128)S(1)}, f32[128,512]{1,0:T(8,128)S(1)}, u32[]{:S(2)}, u32[]{:S(2)}) collective-permute-start(f32[128,512]{1,0:T(8,128)S(1)} %multiply_add_fusion.5), channel_id=1, source_target_pairs={{4,8},{5,9},{6,10},{7,11},{20,24},{21,25},{22,26},{23,27}} | collective-permute-start | bytes 786440 | tf_op jit(solution)/shard_map/ppermute | solution.py:364
  20.1 5.5 %collective-permute-start.5 = (f32[64,512]{1,0:T(8,128)S(1)}, f32[64,512]{1,0:T(8,128)S(1)}, u32[]{:S(2)}, u32[]{:S(2)}) collective-permute-start(f32[64,512]{1,0:T(8,128)S(1)} %add.40.refs_12_), channel_id=1, source_target_pairs={{0,2},{2,0},{1,3},{3,1},{4,6},{6,4},{5,7},{7,5},{8,10},{10,8},{9,1... | collective-permute-start | bytes 393224 | tf_op jit(solution)/shard_map/ppermute | solution.py:385
  21.7 4.6 %collective-permute-start.7 = (f32[128,512]{1,0:T(8,128)S(1)}, f32[128,512]{1,0:T(8,128)S(1)}, u32[]{:S(2)}, u32[]{:S(2)}) collective-permute-start(f32[128,512]{1,0:T(8,128)S(1)} %multiply_add_fusion.6), channel_id=1, source_target_pairs={{8,12},{9,13},{10,14},{11,15},{24,28},{25,29},{26,30},{27,31}} | collective-permute-start | bytes 786440 | tf_op jit(solution)/shard_map/ppermute | solution.py:364
  25.6 4.9 %collective-permute-start.6 = (f32[128,512]{1,0:T(8,128)S(1)}, f32[128,512]{1,0:T(8,128)S(1)}, u32[]{:S(2)}, u32[]{:S(2)}) collective-permute-start(f32[128,512]{1,0:T(8,128)S(1)} %multiply_add_fusion.4), channel_id=1, source_target_pairs={{8,12},{9,13},{10,14},{11,15},{24,28},{25,29},{26,30},{27,31}} | collective-permute-start | bytes 786440 | tf_op jit(solution)/shard_map/ppermute | solution.py:364
  29.8 5.5 %collective-permute-start.8 = (f32[128,512]{1,0:T(8,128)S(1)}, f32[128,512]{1,0:T(8,128)S(1)}, u32[]{:S(2)}, u32[]{:S(2)}) collective-permute-start(f32[128,512]{1,0:T(8,128)S(1)} %get-tuple-element.110.refs_10_), channel_id=1, source_target_pairs={{12,8},{13,9},{14,10},{15,11},{28,24},{29,25},{30,26},{31,27}} | collective-permute-start | bytes 786440 | tf_op jit(solution)/shard_map/ppermute | solution.py:364
  33.9 2.2 %collective-permute-start.9 = (f32[64,512]{1,0:T(8,128)S(1)}, f32[64,512]{1,0:T(8,128)S(1)}, u32[]{:S(2)}, u32[]{:S(2)}) collective-permute-start(f32[64,512]{1,0:T(8,128)S(1)} %get-tuple-element.111), channel_id=1, source_target_pairs={{0,1},{1,0},{2,3},{3,2},{4,5},{5,4},{6,7},{7,6},{8,9},{9,8},{10,11... | collective-permute-start | bytes 393224 | tf_op jit(solution)/shard_map/ppermute | solution.py:385
  33.9 10.5 %collective-permute-start.11 = (f32[128,512]{1,0:T(8,128)S(1)}, f32[128,512]{1,0:T(8,128)}, u32[]{:S(2)}, u32[]{:S(2)}) collective-permute-start(f32[128,512]{1,0:T(8,128)S(1)} %get-tuple-element.117.refs_10_), channel_id=1, source_target_pairs={{12,8},{13,9},{14,10},{15,11},{28,24},{29,25},{30,26},{31,27}} | collective-permute-start | bytes 786440 | tf_op jit(solution)/shard_map/ppermute | solution.py:364
  36.7 6.2 %collective-permute-start.10 = (f32[64,512]{1,0:T(8,128)}, f32[64,512]{1,0:T(8,128)}, u32[]{:S(2)}, u32[]{:S(2)}) collective-permute-start(f32[64,512]{1,0:T(8,128)} %add.47.refs_1_), channel_id=1, source_target_pairs={{0,2},{2,0},{1,3},{3,1},{4,6},{6,4},{5,7},{7,5},{8,10},{10,8},{9,1... | collective-permute-start | bytes 393224 | tf_op jit(solution)/shard_map/ppermute | solution.py:385
  38.2 13.0 %collective-permute-start.12 = (f32[128,512]{1,0:T(8,128)}, f32[128,512]{1,0:T(8,128)}, u32[]{:S(2)}, u32[]{:S(2)}) collective-permute-start(f32[128,512]{1,0:T(8,128)} %multiply_add_fusion.3), channel_id=1, source_target_pairs={{8,4},{9,5},{10,6},{11,7},{24,20},{25,21},{26,22},{27,23}} | collective-permute-start | bytes 786440 | tf_op jit(solution)/shard_map/ppermute | solution.py:364
  46.1 9.1 %collective-permute-start.13 = (f32[128,512]{1,0:T(8,128)S(1)}, f32[128,512]{1,0:T(8,128)S(1)}, u32[]{:S(2)}, u32[]{:S(2)}) collective-permute-start(f32[128,512]{1,0:T(8,128)S(1)} %multiply_add_fusion.2), channel_id=1, source_target_pairs={{8,4},{9,5},{10,6},{11,7},{24,20},{25,21},{26,22},{27,23}} | collective-permute-start | bytes 786440 | tf_op jit(solution)/shard_map/ppermute | solution.py:364
  46.9 11.4 %collective-permute-start.14 = (f32[64,1024]{1,0:T(8,128)S(1)}, f32[64,1024]{1,0:T(8,128)S(1)}, u32[]{:S(2)}, u32[]{:S(2)}) collective-permute-start(f32[64,1024]{1,0:T(8,128)S(1)} %get-tuple-element.125), channel_id=1, source_target_pairs={{0,4},{4,0},{8,12},{12,8},{1,5},{5,1},{9,13},{13,9},{2,6},{6,2},{1... | collective-permute-start | bytes 786440 | tf_op jit(solution)/shard_map/ppermute | solution.py:364
  52.3 14.9 %collective-permute-start.16 = (f32[128,512]{1,0:T(8,128)S(1)}, f32[128,512]{1,0:T(8,128)S(1)}, u32[]{:S(2)}, u32[]{:S(2)}) collective-permute-start(f32[128,512]{1,0:T(8,128)S(1)} %multiply_add_fusion.1), channel_id=1, source_target_pairs={{4,0},{5,1},{6,2},{7,3},{20,16},{21,17},{22,18},{23,19}} | collective-permute-start | bytes 786440 | tf_op jit(solution)/shard_map/ppermute | solution.py:364
  55.3 9.8 %copy-start.9 = (bf16[512,512]{1,0:T(8,128)(2,1)S(1)}, bf16[512,512]{1,0:T(8,128)(2,1)}, u32[]{:S(2)}) copy-start(bf16[512,512]{1,0:T(8,128)(2,1)} %copy-done.8) | copy-start | bytes 1572868
  58.4 15.3 %collective-permute-start.17 = (f32[64,1024]{1,0:T(8,128)S(1)}, f32[64,1024]{1,0:T(8,128)S(1)}, u32[]{:S(2)}, u32[]{:S(2)}) collective-permute-start(f32[64,1024]{1,0:T(8,128)S(1)} %add.51), channel_id=1, source_target_pairs={{0,8},{8,0},{4,12},{12,4},{1,9},{9,1},{5,13},{13,5},{2,10},{10,2},... | collective-permute-start | bytes 786440 | tf_op jit(solution)/shard_map/ppermute | solution.py:364
  63.6 12.2 %collective-permute-start.15 = (f32[128,512]{1,0:T(8,128)S(1)}, f32[128,512]{1,0:T(8,128)S(1)}, u32[]{:S(2)}, u32[]{:S(2)}) collective-permute-start(f32[128,512]{1,0:T(8,128)S(1)} %multiply_add_fusion), channel_id=1, source_target_pairs={{4,0},{5,1},{6,2},{7,3},{20,16},{21,17},{22,18},{23,19}} | collective-permute-start | bytes 786440 | tf_op jit(solution)/shard_map/ppermute | solution.py:364
  73.7 7.4 %collective-permute-start.18 = (f32[64,1024]{1,0:T(8,128)S(1)}, f32[64,1024]{1,0:T(8,128)S(1)}, u32[]{:S(2)}, u32[]{:S(2)}) collective-permute-start(f32[64,1024]{1,0:T(8,128)S(1)} %add.52.refs_1_), channel_id=1, source_target_pairs={{0,4},{4,0},{8,12},{12,8},{1,5},{5,1},{9,13},{13,9},{2,6},{6,2},{1... | collective-permute-start | bytes 786440 | tf_op jit(solution)/shard_map/ppermute | solution.py:364
  (32 other events, 112.0 us)

commit v4 on v3

--- a/solution.py
+++ b/solution.py
@@ -138,14 +138,21 @@
     return near[...] + far[...] + mid[...]
 
 
-def norm_kernel(*refs, first):
+def split_rows(odd, part, keep, send):
+    rows = keep.shape[0]
+    is_odd = odd[0:1, 0:1] == 1
+    keep[...] = jnp.where(is_odd, part[rows:], part[:rows])
+    send[...] = jnp.where(is_odd, part[:rows], part[rows:])
+
+
+def norm_kernel(odd, *refs, first):
     refs = list(refs)
     (y_loc, cstart, near, far, mid, small, rows, x, gate, skips, gain, frozen) = refs[:12]
     (gu_here, gu_there, down) = refs[12:15]
     refs = refs[15:]
     u_before = None if first == 0 else refs.pop(0)
-    (mixed, gate_grad, down_part, gye, scaled, state_grad, u_part, y_dot, decay) = refs[:9]
-    (inner, falls, g_mixed, product) = refs[9:]
+    (mixed, gate_grad, keep, send, gye, scaled, state_grad, u_part, y_dot, decay) = refs[:10]
+    (inner, falls, g_mixed, product) = refs[10:]
     decay[...] = rows[0:1]
     length, channels = x.shape
     heads = channels // HEAD
@@ -186,7 +193,8 @@
     state_grad[...] = dot(cstart[...], gye[...], 0, 0) * rows[1:2]
     u_here = dot(down[...], mixed[...], 1, 1)
     u_part[...] = u_here if first == 0 else u_here + u_before[...]
-    down_part[...] = dot(gu, mixed[...], 1, 0)
+    down_part = dot(gu, mixed[...], 1, 0)
+    split_rows(odd, down_part, keep, send)
     ones = places.astype(bf16)
     y_dot[...] = dot(ones, product[0], 1, 1) + dot(ones, product[1], 1, 1)
 
@@ -285,28 +293,28 @@
     out[...] = dot(u[...], up[...], 0, 0).astype(bf16)
 
 
-def halves_kernel(odd, u_here, u_there, lo, down_part, u_out, keep, send):
+def halves_kernel(
+    odd, u_here, u_there, lo, keep_down, send_down, decay_in, u_out, keep, send, decay
+):
     u = (SCALE * (u_here[...] + u_there[...])).astype(bf16)
     u_out[...] = u
-    rows = keep.shape[0] // 2
-    is_odd = odd[0] == 1
-    down = down_part[...]
-    keep[rows:] = jnp.where(is_odd, down[rows:], down[:rows])
-    send[rows:] = jnp.where(is_odd, down[:rows], down[rows:])
-    up_part = dot(u, lo[...], 1, 0)
-    keep[:rows] = jnp.where(is_odd, up_part[rows:], up_part[:rows])
-    send[:rows] = jnp.where(is_odd, up_part[:rows], up_part[rows:])
-
-
-def join_kernel(odd, keep, other, up_out, down_out):
-    is_odd = odd[0] == 1
+    rows = keep_down.shape[0]
+    split_rows(odd, dot(u, lo[...], 1, 0), keep.at[:rows], send.at[:rows])
+    keep[rows:] = keep_down[...]
+    send[rows:] = send_down[...]
+    decay[...] = decay_in[...]
+
+
+def join_kernel(odd, keep, got, up_out, down_out):
+    is_odd = odd[0:1, 0:1] == 1
     rows = keep.shape[0] // 2
     for at, out in ((pl.ds(0, rows), up_out), (pl.ds(rows, rows), down_out)):
-        out[:rows] = jnp.where(is_odd, other[at], keep[at])
-        out[rows:] = jnp.where(is_odd, keep[at], other[at])
-
-
-def rank_kernel(up, lo, part):
+        out[:rows] = jnp.where(is_odd, got[at], keep[at])
+        out[rows:] = jnp.where(is_odd, keep[at], got[at])
+
+
+def rank_kernel(up, lo, odd, part, marks):
+    marks[...] = odd[...]
     part[...] = dot(up[...], lo[...], 1, 1)
 
 
@@ -484,20 +492,24 @@
             name="score",
         )[0]
 
+    paired = short and groups == 2
+    odd = jnp.full((8, 128), lax.axis_index("ctx") % 2 if paired else 0, jnp.int32)
+
     def rank_call(*before):
         return call(
             rank_kernel,
             [
                 whole(after(adapter_up_map, *before) if before else adapter_up_map),
                 whole(layer_output_gradient),
-            ],
-            [fresh((rank, length), f32)],
+                whole(odd),
+            ],
+            [fresh((rank, length), f32), fresh((8, 128), jnp.int32)],
             cost=1.0,
             name="rank",
-        )[0]
+        )
 
     states, y_locs = [state_call(0, rates)], []
-    gu_part = rank_call(states[0][5])
+    gu_part, marks = rank_call(states[0][5])
     for g in range(1, groups):
         states.append(state_call(g, after(rates, gu_part)))
 
@@ -521,7 +533,7 @@
         y_locs = [score_call(g) for g in everything]
         gu = exchange_pair(gu_part, ("fsdp", "head"))
         entering = [chain(parts[g], decays[g], "ctx", False) for g in everything]
-    mixed = gate_grad = down_part = u_part = c_grad = None
+    mixed = gate_grad = keep_down = send_down = u_part = c_grad = None
     normed, pairs = [], []
 
     def pair_call(g, held, *others):
@@ -551,6 +563,7 @@
         results = call(
             functools.partial(norm_kernel, first=g * heads),
             [
+                whole(marks),
                 whole(y_locs[g]),
                 whole(cstart),
                 *map(whole, entering[g]),
@@ -568,13 +581,14 @@
             [
                 ((length, channels), bf16, (length, width), (0, g), mixed),
                 ((length, channels), bf16, (length, width), (0, g), gate_grad),
-                slow(((rank, channels), f32, (rank, width), (0, g), down_part)),
+                slow(((rank // 2, channels), f32, (rank // 2, width), (0, g), keep_down)),
+                slow(((rank // 2, channels), f32, (rank // 2, width), (0, g), send_down)),
                 (slow if g < groups - 1 else tuple)(fresh((length, width), bf16)),
                 slow(fresh((STATE, width), bf16)),
                 fresh((STATE, width), f32),
                 fresh((rank, length), f32),
                 slow(fresh((heads, length), f32)),
-                fresh((1, width), f32),
+                (slow if g == groups - 1 else tuple)(fresh((1, width), f32)),
             ],
             [
                 pltpu.VMEM((length, width), f32),
@@ -585,7 +599,7 @@
             cost=4.0,
             name="norm",
         )
-        mixed, gate_grad, down_part, gye, scaled, state_grad, u_part, y_dot, decay = results
+        mixed, gate_grad, keep_down, send_down, gye, scaled, state_grad, u_part, y_dot, decay = results
         normed.append((gye, scaled, state_grad, y_dot, decay))
     def input_call(g, leaving, held, passing, *before):
         xw, state, bend, cstart, small, rows, ids_row, ids_col = states[g]
@@ -629,41 +643,42 @@
     state_grads = [normed[g][2] for g in everything]
     decays = [normed[g][4] for g in everything]
     held = (None, None, None)
-    if short and groups == 2:
+    if paired:
         neighbours = [(0, 1), (1, 0), (2, 3), (3, 2)]
         across = [(0, 2), (2, 0), (1, 3), (3, 1)]
         last = [hop(state_grads[g], "ctx", (3, 2)) for g in everything]
         sent = after(decays[0], u_part) * last[0] + state_grads[0]
         then = [hop(sent, "ctx", (2, 1))]
         u = exchange_pair(u_part, ("fsdp", "head"), sent)
-        odd = (lax.axis_index("ctx") % 2).reshape(1)
         half = fresh((rank, channels), f32)
-        u, keep, send = call(
+        u, keep, send, decay = call(
             halves_kernel,
             [
-                (odd, "scalar", None),
+                whole(odd),
                 *map(whole, u),
                 whole(layer_output_gradient),
-                slow(whole(down_part)),
-            ],
-            [fresh((rank, length), bf16), half, half],
+                slow(whole(keep_down)),
+                slow(whole(send_down)),
+                slow(whole(decays[1])),
+            ],
+            [fresh((rank, length), bf16), half, half, fresh((1, width), f32)],
             cost=1.5,
             name="halves",
         )
-        sent = after(decays[1], keep) * last[1] + state_grads[1]
+        sent = decay * last[1] + state_grads[1]
         then.append(hop(sent, "ctx", (2, 1)))
         got = hop(send, "ctx", *neighbours)
         sent = after(decays[0], sent) * then[0] + state_grads[0]
         ahead = [hop(sent, "ctx", (1, 0))]
         c_grad, *pair = pair_call(0, c_grad, sent)
         pairs.append(pair)
-        sent = after(decays[1], pair[1]) * then[1] + state_grads[1]
+        sent = after(decay, pair[1]) * then[1] + state_grads[1]
         ahead.append(hop(sent, "ctx", (1, 0)))
         keep = after(keep, sent) + got
         got = hop(keep, "ctx", *across)
         c_grad, *pair = pair_call(1, c_grad, keep)
         pairs.append(pair)
-        *held, _ = input_call(0, (last[0], then[0], ahead[0]), held, decays[1], pair[1])
+        *held, _ = input_call(0, (last[0], then[0], ahead[0]), held, decay, pair[1])
         (adapter_output,) = call(
             output_kernel,
             [whole(after(u, pair[1])), whole(adapter_up_map)],
@@ -672,10 +687,10 @@
         )
         keep = after(keep, held[2]) + got
         got = hop(keep, "ctx", *neighbours)
-        *held, _ = input_call(1, (last[1], then[1], ahead[1]), held, decays[1])
+        *held, _ = input_call(1, (last[1], then[1], ahead[1]), held, decay)
         up_sum, down_sum = call(
             join_kernel,
-            [(odd, "scalar", None), whole(after(keep, held[2])), whole(got)],
+            [whole(odd), whole(after(keep, held[2])), whole(got)],
             [fresh((rank, channels), f32), fresh((rank, channels), f32)],
             name="join",
         )
@@ -694,7 +709,7 @@
             leaving = chain(state_grads[g], decays[g], "ctx", True)
             *held, _ = input_call(g, leaving, held, decays[g])
         up_sum = exchange_sum(up_part, ("ctx",))
-        down_sum = exchange_sum(down_part, ("ctx",))
+        down_sum = exchange_sum(jnp.concatenate([keep_down, send_down], axis=0), ("ctx",))
     x_grad, b_grad, step_grad = held
     return (
         mixed,

time: 82.5 us -> 80.7 us (0.978)
  other arithmetic: 3.82 us -> 0.46 us
  waiting for transfers between devices: 19.2 us -> 21.2 us
  local copies, waits for them, and re-layouts: 2.65 us -> 1.37 us
  starting transfers between devices: 29.4 us -> 30.5 us
    unnamed x74 -> x32, local copies, waits for them, and re-layouts: 2.65 us -> 1.36 us
    ppermute x15, waiting for transfers between devices: 13.5 us -> 14.7 us  [hop(): return lax.ppermute(part, axis, list(pairs))]
    add x1, other arithmetic: 1.03 us -> 0.04 us  [per_device(): sent = after(decays[0], sent) * then[0] + state_grads[0]]
    add x2, other arithmetic: 1.08 us -> 0.1 us  [the longest x1 0.05 us: per_device(): sent = after(decay, pair[1]) * then[1] + state_grads[1]]
    ppermute x15, starting transfers between devices: 26.3 us -> 27.3 us  [hop(): return lax.ppermute(part, axis, list(pairs))]
  transfers between devices with their start and end apart: 19 -> 19, of which waited for: 7 -> 9; matrix products, arithmetic and copies ran while one was open for 5% -> 1% of each run, Pallas kernels for 27% -> 28%
where the time goes in v4:
time: 80.7 us; the launch traced here: 80.2 us
  starting transfers between devices  30.5 us (38%)
  Pallas kernels  25.6 us (32%)
  waiting for transfers between devices  21.2 us (26%)
  local copies, waits for them, and re-layouts  1.37 us (2%)
  between operations  1.12 us (1%)
    ppermute x15, starting transfers between devices, hop(): return lax.ppermute(part, axis, list(pairs))  27.3 us
    pallas_call x14, Pallas kernels, call(): pl.pallas_call(body, grid=(1,), in_specs=in_specs, out_specs=out_specs, o...  25.6 us
    ppermute x15, waiting for transfers between devices, hop(): return lax.ppermute(part, axis, list(pairs))  14.7 us
    ppermute x4, waiting for transfers between devices, exchange_pair(): other = lax.ppermute(part, axis, [(i, i ^ span) for i in range(count)])  6.48 us
    ppermute x4, starting transfers between devices, exchange_pair(): other = lax.ppermute(part, axis, [(i, i ^ span) for i in range(count)])  3.18 us
  transfers between devices with their start and end apart: 19, of which 9 were waited for; matrix products, arithmetic and copies ran while one was open for 1% of the time, Pallas kernels for 28%

profile of v4, /device:TPU:0, one launch (start us, length us, event | category | flops | bytes accessed | tf_op | source)
XLA Modules:
  0.0 80.2 jit_solution(17517588316447692346)
XLA Ops:
  0.7 2.6 %state.2 = (bf16[512,512]{1,0:T(8,128)(2,1)S(1)}, f32[128,512]{1,0:T(8,128)S(1)}, bf16[512,128]{1,0:T(8,128)(2,1)}, bf16[512,128]{1,0:T(8,128)(2,1)S(1)}, f32[32...) custom-call(bf16[512,1024]{1,0:T(8,128)(2,1)} %refs_8_.3, ...), custom_call_target="tpu_custom_call" | custom-call | bytes 5535000 | tf_op jit(solution)/shard_map/state/pallas_call | solution.py:351
  3.2 4.9 %collective-permute-start.1 = (f32[128,512]{1,0:T(8,128)S(1)}, f32[128,512]{1,0:T(8,128)S(1)}, u32[]{:S(2)}, u32[]{:S(2)}) collective-permute-start(f32[128,512]{1,0:T(8,128)S(1)} %get-tuple-element.97), channel_id=1, source_target_pairs={{0,4},{1,5},{2,6},{3,7},{16,20},{17,21},{18,22},{19,23}} | collective-permute-start | bytes 786440 | tf_op jit(solution)/shard_map/ppermute | solution.py:372
  8.7 2.5 %state.3 = (bf16[512,512]{1,0:T(8,128)(2,1)S(1)}, f32[128,512]{1,0:T(8,128)S(1)}, bf16[512,128]{1,0:T(8,128)(2,1)}, bf16[512,128]{1,0:T(8,128)(2,1)S(1)}, f32[32...) custom-call(bf16[512,1024]{1,0:T(8,128)(2,1)} %refs_8_.3, ...), custom_call_target="tpu_custom_call" | custom-call | bytes 5535000 | tf_op jit(solution)/shard_map/state/pallas_call | solution.py:351
  11.2 1.4 %collective-permute-start.3 = (f32[128,512]{1,0:T(8,128)S(1)}, f32[128,512]{1,0:T(8,128)S(1)}, u32[]{:S(2)}, u32[]{:S(2)}) collective-permute-start(f32[128,512]{1,0:T(8,128)S(1)} %get-tuple-element.102), channel_id=1, source_target_pairs={{0,4},{1,5},{2,6},{3,7},{16,20},{17,21},{18,22},{19,23}} | collective-permute-start | bytes 786440 | tf_op jit(solution)/shard_map/ppermute | solution.py:372
  14.5 4.8 %collective-permute-done.3.refs_3_ = f32[128,512]{1,0:T(8,128)S(1)} collective-permute-done((f32[128,512]{1,0:T(8,128)S(1)}, f32[128,512]{1,0:T(8,128)S(1)}, u32[]{:S(2)}, u32[]{:S(2)}) %collective-permute-start.3) | collective-permute-done | bytes 262176 | tf_op jit(solution)/shard_map/ppermute | solution.py:372
  20.0 1.6 %collective-permute-start.5 = (f32[64,512]{1,0:T(8,128)S(1)}, f32[64,512]{1,0:T(8,128)S(1)}, u32[]{:S(2)}, u32[]{:S(2)}) collective-permute-start(f32[64,512]{1,0:T(8,128)S(1)} %add.41.refs_13_), channel_id=1, source_target_pairs={{0,2},{2,0},{1,3},{3,1},{4,6},{6,4},{5,7},{7,5},{8,10},{10,8},{9,1... | collective-permute-start | bytes 393224 | tf_op jit(solution)/shard_map/ppermute | solution.py:393
  23.0 2.5 %collective-permute-done.5.refs_14_ = f32[64,512]{1,0:T(8,128)S(1)} collective-permute-done((f32[64,512]{1,0:T(8,128)S(1)}, f32[64,512]{1,0:T(8,128)S(1)}, u32[]{:S(2)}, u32[]{:S(2)}) %collective-permute-start.5) | collective-permute-done | bytes 131104 | tf_op jit(solution)/shard_map/ppermute | solution.py:393
  27.0 3.1 %norm.2 = (bf16[512,1024]{1,0:T(8,128)(2,1)}, bf16[512,1024]{1,0:T(8,128)(2,1)}, f32[32,1024]{1,0:T(8,128)}, f32[32,1024]{1,0:T(8,128)}, bf16[512,512]{1,0:T(8,1...) custom-call(s32[8,128]{1,0:T(8,128)S(1)} %get-tuple-element.86.refs_, ...), custom_call_target="tpu_custom_call" | custom-call | bytes 14760000 | tf_op jit(solution)/shard_map/norm/pallas_call | solution.py:351
  30.8 2.9 %norm.3 = (bf16[512,1024]{1,0:T(8,128)(2,1)}, bf16[512,1024]{1,0:T(8,128)(2,1)}, f32[32,1024]{1,0:T(8,128)}, f32[32,1024]{1,0:T(8,128)}, bf16[512,512]{1,0:T(8,1...) custom-call(s32[8,128]{1,0:T(8,128)S(1)} %get-tuple-element.86.refs_, ...), custom_call_target="tpu_custom_call", output_to_operand_aliasing={{0}: (17, {}), {1}: (18, {}), {2}: (19, {}), {3}: (20, {})} | custom-call | bytes 14760000 | tf_op jit(solution)/shard_map/norm/pallas_call | solution.py:351
  35.1 1.6 %collective-permute-start.10 = (f32[64,512]{1,0:T(8,128)S(1)}, f32[64,512]{1,0:T(8,128)S(1)}, u32[]{:S(2)}, u32[]{:S(2)}) collective-permute-start(f32[64,512]{1,0:T(8,128)S(1)} %add.47.refs_1_), channel_id=1, source_target_pairs={{0,2},{2,0},{1,3},{3,1},{4,6},{6,4},{5,7},{7,5},{8,10},{10,8},{9,1... | collective-permute-start | bytes 393224 | tf_op jit(solution)/shard_map/ppermute | solution.py:393
  37.3 3.4 %collective-permute-done.10.refs_2_ = f32[64,512]{1,0:T(8,128)S(1)} collective-permute-done((f32[64,512]{1,0:T(8,128)S(1)}, f32[64,512]{1,0:T(8,128)S(1)}, u32[]{:S(2)}, u32[]{:S(2)}) %collective-permute-start.10) | collective-permute-done | bytes 131104 | tf_op jit(solution)/shard_map/ppermute | solution.py:393
  42.9 4.3 %collective-permute-start.14 = (f32[64,1024]{1,0:T(8,128)S(1)}, f32[64,1024]{1,0:T(8,128)S(1)}, u32[]{:S(2)}, u32[]{:S(2)}) collective-permute-start(f32[64,1024]{1,0:T(8,128)S(1)} %get-tuple-element.133), channel_id=1, source_target_pairs={{0,4},{4,0},{8,12},{12,8},{1,5},{5,1},{9,13},{13,9},{2,6},{6,2},{1... | collective-permute-start | bytes 786440 | tf_op jit(solution)/shard_map/ppermute | solution.py:372
  47.2 1.4 %collective-permute-start.16 = (f32[128,512]{1,0:T(8,128)S(1)}, f32[128,512]{1,0:T(8,128)S(1)}, u32[]{:S(2)}, u32[]{:S(2)}) collective-permute-start(f32[128,512]{1,0:T(8,128)S(1)} %multiply_add_fusion.1), channel_id=1, source_target_pairs={{4,0},{5,1},{6,2},{7,3},{20,16},{21,17},{22,18},{23,19}} | collective-permute-start | bytes 786440 | tf_op jit(solution)/shard_map/ppermute | solution.py:372
  48.6 1.6 %pair.2 = (bf16[512,256]{1,0:T(8,128)(2,1)}, f32[512,512]{1,0:T(8,128)S(1)}, f32[512,128]{1,0:T(8,128)S(1)}) custom-call(bf16[512,256]{1,0:T(8,128)(2,1)S(1)} %copy-done.1, bf16[512,256]{1,0:T(8,128)(2,1)S(1)} %copy-done.2, f32[8,512]{1,0:T(8,128)S(1)} %get-tuple-element.127.refs_2_.refs_4_, f32[512,8]{1,0:T(8,128)S(1)} %get-tuple-element.94.refs_3_, ...), custom_call_target="tpu_custom_call" | custom-call | bytes 7380000 | tf_op jit(solution)/shard_map/pair/pallas_call | solution.py:351
  50.3 2.6 %collective-permute-done.14 = f32[64,1024]{1,0:T(8,128)S(1)} collective-permute-done((f32[64,1024]{1,0:T(8,128)S(1)}, f32[64,1024]{1,0:T(8,128)S(1)}, u32[]{:S(2)}, u32[]{:S(2)}) %collective-permute-start.14) | collective-permute-done | bytes 262176 | tf_op jit(solution)/shard_map/ppermute | solution.py:372
  53.0 8.2 %collective-permute-start.17 = (f32[64,1024]{1,0:T(8,128)S(1)}, f32[64,1024]{1,0:T(8,128)S(1)}, u32[]{:S(2)}, u32[]{:S(2)}) collective-permute-start(f32[64,1024]{1,0:T(8,128)S(1)} %add.51), channel_id=1, source_target_pairs={{0,8},{8,0},{4,12},{12,4},{1,9},{9,1},{5,13},{13,5},{2,10},{10,2},... | collective-permute-start | bytes 786440 | tf_op jit(solution)/shard_map/ppermute | solution.py:372
  61.1 1.5 %collective-permute-start.15 = (f32[128,512]{1,0:T(8,128)S(1)}, f32[128,512]{1,0:T(8,128)S(1)}, u32[]{:S(2)}, u32[]{:S(2)}) collective-permute-start(f32[128,512]{1,0:T(8,128)S(1)} %multiply_add_fusion), channel_id=1, source_target_pairs={{4,0},{5,1},{6,2},{7,3},{20,16},{21,17},{22,18},{23,19}} | collective-permute-start | bytes 786440 | tf_op jit(solution)/shard_map/ppermute | solution.py:372
  62.6 2.0 %pair.3 = (bf16[512,256]{1,0:T(8,128)(2,1)}, f32[512,512]{1,0:T(8,128)S(1)}, f32[512,128]{1,0:T(8,128)S(1)}) custom-call(bf16[512,256]{1,0:T(8,128)(2,1)S(1)} %copy-done.1, bf16[512,256]{1,0:T(8,128)(2,1)S(1)} %copy-done.2, f32[8,512]{1,0:T(8,128)S(1)} %get-tuple-element.134.refs_2_.refs_4_, ...), custom_call_target="tpu_custom_call", output_to_operand_aliasing={{0}: (7, {})} | custom-call | bytes 7380000 | tf_op jit(solution)/shard_map/pair/pallas_call | solution.py:351
  65.3 2.7 %input.2 = (bf16[512,1024]{1,0:T(8,128)(2,1)}, bf16[512,256]{1,0:T(8,128)(2,1)}, f32[16,512]{1,0:T(8,128)}, f32[1,512]{1,0:T(1,128)}) custom-call(f32[512,512]{1,0:T(8,128)S(1)} %get-tuple-element.143.refs_0_, f32[512,128]{1,0:T(8,128)S(1)} %get-tuple-element.130.refs_1_, bf16[512,128]{1,0:T(8,128)(2,1)S(1)} %copy-done.11, ...), custom_call_target="tpu_custom_call" | custom-call | bytes 9225000 | tf_op jit(solution)/shard_map/input/pallas_call | solution.py:351
  68.1 3.4 %collective-permute-done.17 = f32[64,1024]{1,0:T(8,128)S(1)} collective-permute-done((f32[64,1024]{1,0:T(8,128)S(1)}, f32[64,1024]{1,0:T(8,128)S(1)}, u32[]{:S(2)}, u32[]{:S(2)}) %collective-permute-start.17) | collective-permute-done | bytes 262176 | tf_op jit(solution)/shard_map/ppermute | solution.py:372
  71.6 1.4 %output.1 = bf16[512,1024]{1,0:T(8,128)(2,1)} custom-call(bf16[64,512]{1,0:T(8,128)(2,1)S(1)} %get-tuple-element.139.refs_0_, bf16[64,1024]{1,0:T(8,128)(2,1)S(1)} %copy-done.8), custom_call_target="tpu_custom_call" | custom-call | bytes 3690000 | tf_op jit(solution)/shard_map/output/pallas_call | solution.py:351
  73.0 1.6 %collective-permute-done.15.refs_9_ = f32[128,512]{1,0:T(8,128)S(1)} collective-permute-done((f32[128,512]{1,0:T(8,128)S(1)}, f32[128,512]{1,0:T(8,128)S(1)}, u32[]{:S(2)}, u32[]{:S(2)}) %collective-permute-start.15) | collective-permute-done | bytes 262176 | tf_op jit(solution)/shard_map/ppermute | solution.py:372
  74.6 2.8 %input.3 = (bf16[512,1024]{1,0:T(8,128)(2,1)}, bf16[512,256]{1,0:T(8,128)(2,1)}, f32[16,512]{1,0:T(8,128)}, f32[1,512]{1,0:T(1,128)}) custom-call(f32[512,512]{1,0:T(8,128)S(1)} %get-tuple-element.140.refs_0_, f32[512,128]{1,0:T(8,128)S(1)} %get-tuple-element.138.refs_1_, ...), custom_call_target="tpu_custom_call", output_to_operand_aliasing={{0}: (18, {}), {1}: (19, {}), {2}: (20, {})} | custom-call | bytes 9225000 | tf_op jit(solution)/shard_map/input/pallas_call | solution.py:351
  77.4 2.0 %collective-permute-done.18.refs_2_ = f32[64,1024]{1,0:T(8,128)S(1)} collective-permute-done((f32[64,1024]{1,0:T(8,128)S(1)}, f32[64,1024]{1,0:T(8,128)S(1)}, u32[]{:S(2)}, u32[]{:S(2)}) %collective-permute-start.18) | collective-permute-done | bytes 262176 | tf_op jit(solution)/shard_map/ppermute | solution.py:372
  (75 shorter events, 12.4 us)
Async XLA Ops:
  0.6 7.5 %copy-start.3 = (bf16[512,1024]{1,0:T(8,128)(2,1)S(1)}, bf16[512,1024]{1,0:T(8,128)(2,1)}, u32[]{:S(2)}) copy-start(bf16[512,1024]{1,0:T(8,128)(2,1)} %refs_3_.5) | copy-start | bytes 3145732
  0.7 7.5 %copy-start.8 = (bf16[64,1024]{1,0:T(8,128)(2,1)S(1)}, bf16[64,1024]{1,0:T(8,128)(2,1)}, u32[]{:S(2)}) copy-start(bf16[64,1024]{1,0:T(8,128)(2,1)} %refs_1_.15) | copy-start | bytes 393220
  3.2 10.6 %collective-permute-start.1 = (f32[128,512]{1,0:T(8,128)S(1)}, f32[128,512]{1,0:T(8,128)S(1)}, u32[]{:S(2)}, u32[]{:S(2)}) collective-permute-start(f32[128,512]{1,0:T(8,128)S(1)} %get-tuple-element.97), channel_id=1, source_target_pairs={{0,4},{1,5},{2,6},{3,7},{16,20},{17,21},{18,22},{19,23}} | collective-permute-start | bytes 786440 | tf_op jit(solution)/shard_map/ppermute | solution.py:372
  8.6 4.0 %collective-permute-start = (f32[64,512]{1,0:T(8,128)S(1)}, f32[64,512]{1,0:T(8,128)S(1)}, u32[]{:S(2)}, u32[]{:S(2)}) collective-permute-start(f32[64,512]{1,0:T(8,128)S(1)} %get-tuple-element.92), channel_id=1, source_target_pairs={{0,1},{1,0},{2,3},{3,2},{4,5},{5,4},{6,7},{7,6},{8,9},{9,8},{10,11... | collective-permute-start | bytes 393224 | tf_op jit(solution)/shard_map/ppermute | solution.py:393
  11.2 8.1 %collective-permute-start.3 = (f32[128,512]{1,0:T(8,128)S(1)}, f32[128,512]{1,0:T(8,128)S(1)}, u32[]{:S(2)}, u32[]{:S(2)}) collective-permute-start(f32[128,512]{1,0:T(8,128)S(1)} %get-tuple-element.102), channel_id=1, source_target_pairs={{0,4},{1,5},{2,6},{3,7},{16,20},{17,21},{18,22},{19,23}} | collective-permute-start | bytes 786440 | tf_op jit(solution)/shard_map/ppermute | solution.py:372
  13.8 7.8 %collective-permute-start.2 = (f32[128,512]{1,0:T(8,128)S(1)}, f32[128,512]{1,0:T(8,128)S(1)}, u32[]{:S(2)}, u32[]{:S(2)}) collective-permute-start(f32[128,512]{1,0:T(8,128)S(1)} %multiply_add_fusion.7), channel_id=1, source_target_pairs={{4,8},{5,9},{6,10},{7,11},{20,24},{21,25},{22,26},{23,27}} | collective-permute-start | bytes 786440 | tf_op jit(solution)/shard_map/ppermute | solution.py:372
  19.4 6.2 %collective-permute-start.4 = (f32[128,512]{1,0:T(8,128)S(1)}, f32[128,512]{1,0:T(8,128)S(1)}, u32[]{:S(2)}, u32[]{:S(2)}) collective-permute-start(f32[128,512]{1,0:T(8,128)S(1)} %multiply_add_fusion.5), channel_id=1, source_target_pairs={{4,8},{5,9},{6,10},{7,11},{20,24},{21,25},{22,26},{23,27}} | collective-permute-start | bytes 786440 | tf_op jit(solution)/shard_map/ppermute | solution.py:372
  20.0 5.5 %collective-permute-start.5 = (f32[64,512]{1,0:T(8,128)S(1)}, f32[64,512]{1,0:T(8,128)S(1)}, u32[]{:S(2)}, u32[]{:S(2)}) collective-permute-start(f32[64,512]{1,0:T(8,128)S(1)} %add.41.refs_13_), channel_id=1, source_target_pairs={{0,2},{2,0},{1,3},{3,1},{4,6},{6,4},{5,7},{7,5},{8,10},{10,8},{9,1... | collective-permute-start | bytes 393224 | tf_op jit(solution)/shard_map/ppermute | solution.py:393
  21.6 4.7 %copy-start.7 = (bf16[1024,64]{0,1:T(8,128)(2,1)S(1)}, bf16[1024,64]{0,1:T(8,128)(2,1)}, u32[]{:S(2)}) copy-start(bf16[1024,64]{0,1:T(8,128)(2,1)} %param.24) | copy-start | bytes 393220
  21.7 4.6 %collective-permute-start.7 = (f32[128,512]{1,0:T(8,128)S(1)}, f32[128,512]{1,0:T(8,128)S(1)}, u32[]{:S(2)}, u32[]{:S(2)}) collective-permute-start(f32[128,512]{1,0:T(8,128)S(1)} %multiply_add_fusion.6), channel_id=1, source_target_pairs={{8,12},{9,13},{10,14},{11,15},{24,28},{25,29},{26,30},{27,31}} | collective-permute-start | bytes 786440 | tf_op jit(solution)/shard_map/ppermute | solution.py:372
  25.6 5.2 %collective-permute-start.6 = (f32[128,512]{1,0:T(8,128)S(1)}, f32[128,512]{1,0:T(8,128)S(1)}, u32[]{:S(2)}, u32[]{:S(2)}) collective-permute-start(f32[128,512]{1,0:T(8,128)S(1)} %multiply_add_fusion.4), channel_id=1, source_target_pairs={{8,12},{9,13},{10,14},{11,15},{24,28},{25,29},{26,30},{27,31}} | collective-permute-start | bytes 786440 | tf_op jit(solution)/shard_map/ppermute | solution.py:372
  30.1 4.3 %collective-permute-start.8 = (f32[128,512]{1,0:T(8,128)S(1)}, f32[128,512]{1,0:T(8,128)S(1)}, u32[]{:S(2)}, u32[]{:S(2)}) collective-permute-start(f32[128,512]{1,0:T(8,128)S(1)} %get-tuple-element.117.refs_10_), channel_id=1, source_target_pairs={{12,8},{13,9},{14,10},{15,11},{28,24},{29,25},{30,26},{31,27}} | collective-permute-start | bytes 786440 | tf_op jit(solution)/shard_map/ppermute | solution.py:372
  33.7 1.3 %collective-permute-start.9 = (f32[64,512]{1,0:T(8,128)S(1)}, f32[64,512]{1,0:T(8,128)S(1)}, u32[]{:S(2)}, u32[]{:S(2)}) collective-permute-start(f32[64,512]{1,0:T(8,128)S(1)} %get-tuple-element.118), channel_id=1, source_target_pairs={{0,1},{1,0},{2,3},{3,2},{4,5},{5,4},{6,7},{7,6},{8,9},{9,8},{10,11... | collective-permute-start | bytes 393224 | tf_op jit(solution)/shard_map/ppermute | solution.py:393
  33.7 8.3 %collective-permute-start.11 = (f32[128,512]{1,0:T(8,128)S(1)}, f32[128,512]{1,0:T(8,128)S(1)}, u32[]{:S(2)}, u32[]{:S(2)}) collective-permute-start(f32[128,512]{1,0:T(8,128)S(1)} %get-tuple-element.125.refs_10_), channel_id=1, source_target_pairs={{12,8},{13,9},{14,10},{15,11},{28,24},{29,25},{30,26},{31,27}} | collective-permute-start | bytes 786440 | tf_op jit(solution)/shard_map/ppermute | solution.py:372
  35.1 5.6 %collective-permute-start.10 = (f32[64,512]{1,0:T(8,128)S(1)}, f32[64,512]{1,0:T(8,128)S(1)}, u32[]{:S(2)}, u32[]{:S(2)}) collective-permute-start(f32[64,512]{1,0:T(8,128)S(1)} %add.47.refs_1_), channel_id=1, source_target_pairs={{0,2},{2,0},{1,3},{3,1},{4,6},{6,4},{5,7},{7,5},{8,10},{10,8},{9,1... | collective-permute-start | bytes 393224 | tf_op jit(solution)/shard_map/ppermute | solution.py:393
  36.6 10.5 %collective-permute-start.12 = (f32[128,512]{1,0:T(8,128)S(1)}, f32[128,512]{1,0:T(8,128)S(1)}, u32[]{:S(2)}, u32[]{:S(2)}) collective-permute-start(f32[128,512]{1,0:T(8,128)S(1)} %multiply_add_fusion.3), channel_id=1, source_target_pairs={{8,4},{9,5},{10,6},{11,7},{24,20},{25,21},{26,22},{27,23}} | collective-permute-start | bytes 786440 | tf_op jit(solution)/shard_map/ppermute | solution.py:372
  42.0 6.6 %copy-start.6 = (bf16[512,512]{1,0:T(8,128)(2,1)S(1)}, bf16[512,512]{1,0:T(8,128)(2,1)}, u32[]{:S(2)}) copy-start(bf16[512,512]{1,0:T(8,128)(2,1)} %get-tuple-element.128.refs_5_.refs_6_) | copy-start | bytes 1572868
  42.0 8.2 %collective-permute-start.13 = (f32[128,512]{1,0:T(8,128)S(1)}, f32[128,512]{1,0:T(8,128)S(1)}, u32[]{:S(2)}, u32[]{:S(2)}) collective-permute-start(f32[128,512]{1,0:T(8,128)S(1)} %multiply_add_fusion.2), channel_id=1, source_target_pairs={{8,4},{9,5},{10,6},{11,7},{24,20},{25,21},{26,22},{27,23}} | collective-permute-start | bytes 786440 | tf_op jit(solution)/shard_map/ppermute | solution.py:372
  42.9 10.1 %collective-permute-start.14 = (f32[64,1024]{1,0:T(8,128)S(1)}, f32[64,1024]{1,0:T(8,128)S(1)}, u32[]{:S(2)}, u32[]{:S(2)}) collective-permute-start(f32[64,1024]{1,0:T(8,128)S(1)} %get-tuple-element.133), channel_id=1, source_target_pairs={{0,4},{4,0},{8,12},{12,8},{1,5},{5,1},{9,13},{13,9},{2,6},{6,2},{1... | collective-permute-start | bytes 786440 | tf_op jit(solution)/shard_map/ppermute | solution.py:372
  47.2 17.5 %collective-permute-start.16 = (f32[128,512]{1,0:T(8,128)S(1)}, f32[128,512]{1,0:T(8,128)S(1)}, u32[]{:S(2)}, u32[]{:S(2)}) collective-permute-start(f32[128,512]{1,0:T(8,128)S(1)} %multiply_add_fusion.1), channel_id=1, source_target_pairs={{4,0},{5,1},{6,2},{7,3},{20,16},{21,17},{22,18},{23,19}} | collective-permute-start | bytes 786440 | tf_op jit(solution)/shard_map/ppermute | solution.py:372
  50.3 12.3 %copy-start.9 = (bf16[128,512]{1,0:T(8,128)(2,1)S(1)}, bf16[128,512]{1,0:T(8,128)(2,1)}, u32[]{:S(2)}) copy-start(bf16[128,512]{1,0:T(8,128)(2,1)} %get-tuple-element.136.refs_6_.refs_11_) | copy-start | bytes 393220
  53.0 18.5 %collective-permute-start.17 = (f32[64,1024]{1,0:T(8,128)S(1)}, f32[64,1024]{1,0:T(8,128)S(1)}, u32[]{:S(2)}, u32[]{:S(2)}) collective-permute-start(f32[64,1024]{1,0:T(8,128)S(1)} %add.51), channel_id=1, source_target_pairs={{0,8},{8,0},{4,12},{12,4},{1,9},{9,1},{5,13},{13,5},{2,10},{10,2},... | collective-permute-start | bytes 786440 | tf_op jit(solution)/shard_map/ppermute | solution.py:372
  61.1 13.4 %collective-permute-start.15 = (f32[128,512]{1,0:T(8,128)S(1)}, f32[128,512]{1,0:T(8,128)S(1)}, u32[]{:S(2)}, u32[]{:S(2)}) collective-permute-start(f32[128,512]{1,0:T(8,128)S(1)} %multiply_add_fusion), channel_id=1, source_target_pairs={{4,0},{5,1},{6,2},{7,3},{20,16},{21,17},{22,18},{23,19}} | collective-permute-start | bytes 786440 | tf_op jit(solution)/shard_map/ppermute | solution.py:372
  71.5 7.9 %collective-permute-start.18 = (f32[64,1024]{1,0:T(8,128)S(1)}, f32[64,1024]{1,0:T(8,128)S(1)}, u32[]{:S(2)}, u32[]{:S(2)}) collective-permute-start(f32[64,1024]{1,0:T(8,128)S(1)} %add.52.refs_1_), channel_id=1, source_target_pairs={{0,4},{4,0},{8,12},{12,8},{1,5},{5,1},{9,13},{13,9},{2,6},{6,2},{1... | collective-permute-start | bytes 786440 | tf_op jit(solution)/shard_map/ppermute | solution.py:372
  (11 other events, 26.0 us)

commit v5 on v4

--- a/solution.py
+++ b/solution.py
@@ -151,8 +151,8 @@
     (gu_here, gu_there, down) = refs[12:15]
     refs = refs[15:]
     u_before = None if first == 0 else refs.pop(0)
-    (mixed, gate_grad, keep, send, gye, scaled, state_grad, u_part, y_dot, decay) = refs[:10]
-    (inner, falls, g_mixed, product) = refs[10:]
+    (mixed, gate_grad, keep, send, gye, scaled, state_grad, u_part, y_dot, decay, gye_low) = refs[:11]
+    (inner, falls, g_mixed, product) = refs[11:]
     decay[...] = rows[0:1]
     length, channels = x.shape
     heads = channels // HEAD
@@ -182,8 +182,10 @@
         mean = jnp.sum(g_norm * normed, axis=1, keepdims=True) * (1.0 / channels)
         g_grouped = inv * (g_norm - normed * mean)
         gate_grad[at] = (g_grouped * y * (sig + act * (1.0 - sig))).astype(bf16)
-        g = (g_grouped * act * fall).astype(bf16)
+        exact = g_grouped * act * fall
+        g = exact.astype(bf16)
         gye[at] = g
+        gye_low[at] = (exact - g.astype(f32)).astype(bf16)
         high, low = split2(g.astype(f32) * within)
         product[0, at] = high
         product[1, at] = low
@@ -199,7 +201,7 @@
     y_dot[...] = dot(ones, product[0], 1, 1) + dot(ones, product[1], 1, 1)
 
 
-def pair_kernel(b, c, ids_row, ids_col, xw, gye, scaled_in, c_grad, z_loc, b_loc):
+def pair_kernel(b, c, ids_row, ids_col, xw, gye, gye_low, scaled_in, c_grad, z_loc, b_loc):
     length = b.shape[0]
     half = length // 2
     scaled = scaled_in[...]
@@ -214,7 +216,8 @@
                 r = lax.broadcasted_iota(jnp.int32, (half, half), 0)
                 s = lax.broadcasted_iota(jnp.int32, (half, half), 1)
                 same = same & (r >= s)
-            pair = jnp.where(same, dot(gye[here], xw[there], 1, 1), 0.0).astype(bf16)
+            cross = dot(gye[here], xw[there], 1, 1) + dot(gye_low[here], xw[there], 1, 1)
+            pair = jnp.where(same, cross, 0.0).astype(bf16)
             total += dot(pair, b[there], 1, 0)
         c_grad[here] = total.astype(bf16)
     for j in range(2):
@@ -228,7 +231,8 @@
                 r = lax.broadcasted_iota(jnp.int32, (half, half), 1)
                 same = same & (r >= s)
             m = jnp.where(same, dot(b[there], c[here], 1, 1), 0.0).astype(bf16)
-            pair = jnp.where(same, dot(xw[there], gye[here], 1, 1), 0.0).astype(bf16)
+            cross = dot(xw[there], gye[here], 1, 1) + dot(xw[there], gye_low[here], 1, 1)
+            pair = jnp.where(same, cross, 0.0).astype(bf16)
             z_term = dot(m, gye[here], 1, 0)
             b_term = dot(pair, c[here], 1, 0)
             z_total = z_term if z_total is None else z_total + z_term
@@ -547,6 +551,7 @@
                 whole(ids_col),
                 whole(xw),
                 whole(normed[g][0]),
+                slow(whole(normed[g][5])),
                 whole(normed[g][1]),
             ],
             [
@@ -589,6 +594,7 @@
                 fresh((rank, length), f32),
                 slow(fresh((heads, length), f32)),
                 (slow if g == groups - 1 else tuple)(fresh((1, width), f32)),
+                slow(fresh((length, width), bf16)),
             ],
             [
                 pltpu.VMEM((length, width), f32),
@@ -599,8 +605,8 @@
             cost=4.0,
             name="norm",
         )
-        mixed, gate_grad, keep_down, send_down, gye, scaled, state_grad, u_part, y_dot, decay = results
-        normed.append((gye, scaled, state_grad, y_dot, decay))
+        mixed, gate_grad, keep_down, send_down, gye, scaled, state_grad, u_part, y_dot, decay, gye_low = results
+        normed.append((gye, scaled, state_grad, y_dot, decay, gye_low))
     def input_call(g, leaving, held, passing, *before):
         xw, state, bend, cstart, small, rows, ids_row, ids_col = states[g]
         x_grad, b_grad, step_grad = held

time: 80.7 us -> 81.1 us (level)
  Pallas kernels: 25.6 us -> 29 us
  waiting for transfers between devices: 21.2 us -> 17.8 us
    ppermute x15, waiting for transfers between devices: 14.7 us -> 11.3 us  [hop(): return lax.ppermute(part, axis, list(pairs))]
    pallas_call x14, Pallas kernels: 25.6 us -> 29 us  [call(): pl.pallas_call(body, grid=(1,), in_specs=in_specs, out_specs=out_specs, o...]
  transfers between devices with their start and end apart: 19 -> 19, of which waited for: 9 -> 9; matrix products, arithmetic and copies ran while one was open for 1% -> 1% of each run, Pallas kernels for 28% -> 32%
where the time goes in v5:
time: 81.1 us; the launch traced here: 80.5 us
  starting transfers between devices  30.8 us (38%)
  Pallas kernels  29 us (36%)
  waiting for transfers between devices  17.8 us (22%)
  local copies, waits for them, and re-layouts  1.35 us (2%)
  between operations  1.14 us (1%)
    pallas_call x14, Pallas kernels, call(): pl.pallas_call(body, grid=(1,), in_specs=in_specs, out_specs=out_specs, o...  29 us
    ppermute x15, starting transfers between devices, hop(): return lax.ppermute(part, axis, list(pairs))  27.6 us
    ppermute x15, waiting for transfers between devices, hop(): return lax.ppermute(part, axis, list(pairs))  11.3 us
    ppermute x4, waiting for transfers between devices, exchange_pair(): other = lax.ppermute(part, axis, [(i, i ^ span) for i in range(count)])  6.47 us
    ppermute x4, starting transfers between devices, exchange_pair(): other = lax.ppermute(part, axis, [(i, i ^ span) for i in range(count)])  3.19 us
  transfers between devices with their start and end apart: 19, of which 9 were waited for; matrix products, arithmetic and copies ran while one was open for 1% of the time, Pallas kernels for 32%

profile of v5, /device:TPU:0, one launch (start us, length us, event | category | flops | bytes accessed | tf_op | source)
XLA Modules:
  0.0 80.5 jit_solution(16489667564967878196)
XLA Ops:
  0.7 2.6 %state.2 = (bf16[512,512]{1,0:T(8,128)(2,1)S(1)}, f32[128,512]{1,0:T(8,128)S(1)}, bf16[512,128]{1,0:T(8,128)(2,1)}, bf16[512,128]{1,0:T(8,128)(2,1)S(1)}, f32[32...) custom-call(bf16[512,1024]{1,0:T(8,128)(2,1)} %refs_8_.3, ...), custom_call_target="tpu_custom_call" | custom-call | bytes 5535000 | tf_op jit(solution)/shard_map/state/pallas_call | solution.py:355
  3.2 4.9 %collective-permute-start.1 = (f32[128,512]{1,0:T(8,128)S(1)}, f32[128,512]{1,0:T(8,128)S(1)}, u32[]{:S(2)}, u32[]{:S(2)}) collective-permute-start(f32[128,512]{1,0:T(8,128)S(1)} %get-tuple-element.99), channel_id=1, source_target_pairs={{0,4},{1,5},{2,6},{3,7},{16,20},{17,21},{18,22},{19,23}} | collective-permute-start | bytes 786440 | tf_op jit(solution)/shard_map/ppermute | solution.py:376
  8.7 2.5 %state.3 = (bf16[512,512]{1,0:T(8,128)(2,1)S(1)}, f32[128,512]{1,0:T(8,128)S(1)}, bf16[512,128]{1,0:T(8,128)(2,1)}, bf16[512,128]{1,0:T(8,128)(2,1)S(1)}, f32[32...) custom-call(bf16[512,1024]{1,0:T(8,128)(2,1)} %refs_8_.3, ...), custom_call_target="tpu_custom_call" | custom-call | bytes 5535000 | tf_op jit(solution)/shard_map/state/pallas_call | solution.py:355
  11.2 1.4 %collective-permute-start.3 = (f32[128,512]{1,0:T(8,128)S(1)}, f32[128,512]{1,0:T(8,128)S(1)}, u32[]{:S(2)}, u32[]{:S(2)}) collective-permute-start(f32[128,512]{1,0:T(8,128)S(1)} %get-tuple-element.104), channel_id=1, source_target_pairs={{0,4},{1,5},{2,6},{3,7},{16,20},{17,21},{18,22},{19,23}} | collective-permute-start | bytes 786440 | tf_op jit(solution)/shard_map/ppermute | solution.py:376
  14.5 4.8 %collective-permute-done.3.refs_3_ = f32[128,512]{1,0:T(8,128)S(1)} collective-permute-done((f32[128,512]{1,0:T(8,128)S(1)}, f32[128,512]{1,0:T(8,128)S(1)}, u32[]{:S(2)}, u32[]{:S(2)}) %collective-permute-start.3) | collective-permute-done | bytes 262176 | tf_op jit(solution)/shard_map/ppermute | solution.py:376
  20.0 1.6 %collective-permute-start.5 = (f32[64,512]{1,0:T(8,128)S(1)}, f32[64,512]{1,0:T(8,128)S(1)}, u32[]{:S(2)}, u32[]{:S(2)}) collective-permute-start(f32[64,512]{1,0:T(8,128)S(1)} %add.41.refs_13_), channel_id=1, source_target_pairs={{0,2},{2,0},{1,3},{3,1},{4,6},{6,4},{5,7},{7,5},{8,10},{10,8},{9,1... | collective-permute-start | bytes 393224 | tf_op jit(solution)/shard_map/ppermute | solution.py:397
  23.0 2.5 %collective-permute-done.5.refs_14_ = f32[64,512]{1,0:T(8,128)S(1)} collective-permute-done((f32[64,512]{1,0:T(8,128)S(1)}, f32[64,512]{1,0:T(8,128)S(1)}, u32[]{:S(2)}, u32[]{:S(2)}) %collective-permute-start.5) | collective-permute-done | bytes 131104 | tf_op jit(solution)/shard_map/ppermute | solution.py:397
  27.0 3.3 %norm.2 = (bf16[512,1024]{1,0:T(8,128)(2,1)}, bf16[512,1024]{1,0:T(8,128)(2,1)}, f32[32,1024]{1,0:T(8,128)}, f32[32,1024]{1,0:T(8,128)}, bf16[512,512]{1,0:T(8,1...) custom-call(s32[8,128]{1,0:T(8,128)S(1)} %get-tuple-element.88.refs_, ...), custom_call_target="tpu_custom_call" | custom-call | bytes 14760000 | tf_op jit(solution)/shard_map/norm/pallas_call | solution.py:355
  30.9 3.2 %norm.3 = (bf16[512,1024]{1,0:T(8,128)(2,1)}, bf16[512,1024]{1,0:T(8,128)(2,1)}, f32[32,1024]{1,0:T(8,128)}, f32[32,1024]{1,0:T(8,128)}, bf16[512,512]{1,0:T(8,1...) custom-call(s32[8,128]{1,0:T(8,128)S(1)} %get-tuple-element.88.refs_, ...), custom_call_target="tpu_custom_call", output_to_operand_aliasing={{0}: (17, {}), {1}: (18, {}), {2}: (19, {}), {3}: (20, {})} | custom-call | bytes 14760000 | tf_op jit(solution)/shard_map/norm/pallas_call | solution.py:355
  35.5 1.6 %collective-permute-start.10 = (f32[64,512]{1,0:T(8,128)S(1)}, f32[64,512]{1,0:T(8,128)S(1)}, u32[]{:S(2)}, u32[]{:S(2)}) collective-permute-start(f32[64,512]{1,0:T(8,128)S(1)} %add.47.refs_1_), channel_id=1, source_target_pairs={{0,2},{2,0},{1,3},{3,1},{4,6},{6,4},{5,7},{7,5},{8,10},{10,8},{9,1... | collective-permute-start | bytes 393224 | tf_op jit(solution)/shard_map/ppermute | solution.py:397
  37.7 3.4 %collective-permute-done.10.refs_2_ = f32[64,512]{1,0:T(8,128)S(1)} collective-permute-done((f32[64,512]{1,0:T(8,128)S(1)}, f32[64,512]{1,0:T(8,128)S(1)}, u32[]{:S(2)}, u32[]{:S(2)}) %collective-permute-start.10) | collective-permute-done | bytes 131104 | tf_op jit(solution)/shard_map/ppermute | solution.py:397
  41.1 1.3 %halves.1 = (bf16[64,512]{1,0:T(8,128)(2,1)S(1)}, f32[64,1024]{1,0:T(8,128)S(1)}, f32[64,1024]{1,0:T(8,128)S(1)}, f32[1,512]{1,0:T(1,128)S(1)}) custom-call(s32[8,128]{1,0:T(8,128)S(1)} %broadcast_in_dim.3.refs_2_.refs_0_, f32[64,512]{1,0:T(8,128)S(1)} %add.47.refs_1_, f32[64,512]{1,0:T(8,128)S(1)} %collective-permute-done.10.refs_2_, ...), custom_call_target="tpu_custom_call" | custom-call | bytes 5535000 | tf_op jit(solution)/shard_map/halves/pallas_call | solution.py:355
  43.3 4.3 %collective-permute-start.14 = (f32[64,1024]{1,0:T(8,128)S(1)}, f32[64,1024]{1,0:T(8,128)S(1)}, u32[]{:S(2)}, u32[]{:S(2)}) collective-permute-start(f32[64,1024]{1,0:T(8,128)S(1)} %get-tuple-element.136), channel_id=1, source_target_pairs={{0,4},{4,0},{8,12},{12,8},{1,5},{5,1},{9,13},{13,9},{2,6},{6,2},{1... | collective-permute-start | bytes 786440 | tf_op jit(solution)/shard_map/ppermute | solution.py:376
  47.6 1.4 %collective-permute-start.16 = (f32[128,512]{1,0:T(8,128)S(1)}, f32[128,512]{1,0:T(8,128)S(1)}, u32[]{:S(2)}, u32[]{:S(2)}) collective-permute-start(f32[128,512]{1,0:T(8,128)S(1)} %multiply_add_fusion.1), channel_id=1, source_target_pairs={{4,0},{5,1},{6,2},{7,3},{20,16},{21,17},{22,18},{23,19}} | collective-permute-start | bytes 786440 | tf_op jit(solution)/shard_map/ppermute | solution.py:376
  49.1 3.3 %pair.2 = (bf16[512,256]{1,0:T(8,128)(2,1)}, f32[512,512]{1,0:T(8,128)S(1)}, f32[512,128]{1,0:T(8,128)S(1)}) custom-call(bf16[512,256]{1,0:T(8,128)(2,1)S(1)} %copy-done.1, bf16[512,256]{1,0:T(8,128)(2,1)S(1)} %copy-done.2, f32[8,512]{1,0:T(8,128)S(1)} %get-tuple-element.129.refs_2_.refs_4_, f32[512,8]{1,0:T(8,128)S(1)} %get-tuple-element.96.refs_3_, ...), custom_call_target="tpu_custom_call" | custom-call | bytes 7380000 | tf_op jit(solution)/shard_map/pair/pallas_call | solution.py:355
  52.4 0.9 %collective-permute-done.14 = f32[64,1024]{1,0:T(8,128)S(1)} collective-permute-done((f32[64,1024]{1,0:T(8,128)S(1)}, f32[64,1024]{1,0:T(8,128)S(1)}, u32[]{:S(2)}, u32[]{:S(2)}) %collective-permute-start.14) | collective-permute-done | bytes 262176 | tf_op jit(solution)/shard_map/ppermute | solution.py:376
  53.4 8.1 %collective-permute-start.17 = (f32[64,1024]{1,0:T(8,128)S(1)}, f32[64,1024]{1,0:T(8,128)S(1)}, u32[]{:S(2)}, u32[]{:S(2)}) collective-permute-start(f32[64,1024]{1,0:T(8,128)S(1)} %add.51), channel_id=1, source_target_pairs={{0,8},{8,0},{4,12},{12,4},{1,9},{9,1},{5,13},{13,5},{2,10},{10,2},... | collective-permute-start | bytes 786440 | tf_op jit(solution)/shard_map/ppermute | solution.py:376
  61.5 1.5 %collective-permute-start.15 = (f32[128,512]{1,0:T(8,128)S(1)}, f32[128,512]{1,0:T(8,128)S(1)}, u32[]{:S(2)}, u32[]{:S(2)}) collective-permute-start(f32[128,512]{1,0:T(8,128)S(1)} %multiply_add_fusion), channel_id=1, source_target_pairs={{4,0},{5,1},{6,2},{7,3},{20,16},{21,17},{22,18},{23,19}} | collective-permute-start | bytes 786440 | tf_op jit(solution)/shard_map/ppermute | solution.py:376
  62.9 3.3 %pair.3 = (bf16[512,256]{1,0:T(8,128)(2,1)}, f32[512,512]{1,0:T(8,128)S(1)}, f32[512,128]{1,0:T(8,128)S(1)}) custom-call(bf16[512,256]{1,0:T(8,128)(2,1)S(1)} %copy-done.1, bf16[512,256]{1,0:T(8,128)(2,1)S(1)} %copy-done.2, f32[8,512]{1,0:T(8,128)S(1)} %get-tuple-element.137.refs_2_.refs_4_, ...), custom_call_target="tpu_custom_call", output_to_operand_aliasing={{0}: (8, {})} | custom-call | bytes 7380000 | tf_op jit(solution)/shard_map/pair/pallas_call | solution.py:355
  67.0 2.8 %input.2 = (bf16[512,1024]{1,0:T(8,128)(2,1)}, bf16[512,256]{1,0:T(8,128)(2,1)}, f32[16,512]{1,0:T(8,128)}, f32[1,512]{1,0:T(1,128)}) custom-call(f32[512,512]{1,0:T(8,128)S(1)} %get-tuple-element.147.refs_0_, f32[512,128]{1,0:T(8,128)S(1)} %get-tuple-element.133.refs_1_, bf16[512,128]{1,0:T(8,128)(2,1)S(1)} %copy-done.11, ...), custom_call_target="tpu_custom_call" | custom-call | bytes 9225000 | tf_op jit(solution)/shard_map/input/pallas_call | solution.py:355
  69.7 2.2 %collective-permute-done.17 = f32[64,1024]{1,0:T(8,128)S(1)} collective-permute-done((f32[64,1024]{1,0:T(8,128)S(1)}, f32[64,1024]{1,0:T(8,128)S(1)}, u32[]{:S(2)}, u32[]{:S(2)}) %collective-permute-start.17) | collective-permute-done | bytes 262176 | tf_op jit(solution)/shard_map/ppermute | solution.py:376
  72.5 1.4 %output.1 = bf16[512,1024]{1,0:T(8,128)(2,1)} custom-call(bf16[64,512]{1,0:T(8,128)(2,1)S(1)} %get-tuple-element.143.refs_0_, bf16[64,1024]{1,0:T(8,128)(2,1)S(1)} %copy-done.8), custom_call_target="tpu_custom_call" | custom-call | bytes 3690000 | tf_op jit(solution)/shard_map/output/pallas_call | solution.py:355
  74.7 2.8 %input.3 = (bf16[512,1024]{1,0:T(8,128)(2,1)}, bf16[512,256]{1,0:T(8,128)(2,1)}, f32[16,512]{1,0:T(8,128)}, f32[1,512]{1,0:T(1,128)}) custom-call(f32[512,512]{1,0:T(8,128)S(1)} %get-tuple-element.144.refs_0_, f32[512,128]{1,0:T(8,128)S(1)} %get-tuple-element.142.refs_1_, ...), custom_call_target="tpu_custom_call", output_to_operand_aliasing={{0}: (18, {}), {1}: (19, {}), {2}: (20, {})} | custom-call | bytes 9225000 | tf_op jit(solution)/shard_map/input/pallas_call | solution.py:355
  77.5 2.2 %collective-permute-done.18.refs_2_ = f32[64,1024]{1,0:T(8,128)S(1)} collective-permute-done((f32[64,1024]{1,0:T(8,128)S(1)}, f32[64,1024]{1,0:T(8,128)S(1)}, u32[]{:S(2)}, u32[]{:S(2)}) %collective-permute-start.18) | collective-permute-done | bytes 262176 | tf_op jit(solution)/shard_map/ppermute | solution.py:376
  (75 shorter events, 12.4 us)
Async XLA Ops:
  0.6 7.5 %copy-start.3 = (bf16[512,1024]{1,0:T(8,128)(2,1)S(1)}, bf16[512,1024]{1,0:T(8,128)(2,1)}, u32[]{:S(2)}) copy-start(bf16[512,1024]{1,0:T(8,128)(2,1)} %refs_3_.5) | copy-start | bytes 3145732
  0.7 7.5 %copy-start.8 = (bf16[64,1024]{1,0:T(8,128)(2,1)S(1)}, bf16[64,1024]{1,0:T(8,128)(2,1)}, u32[]{:S(2)}) copy-start(bf16[64,1024]{1,0:T(8,128)(2,1)} %refs_1_.15) | copy-start | bytes 393220
  3.2 10.6 %collective-permute-start.1 = (f32[128,512]{1,0:T(8,128)S(1)}, f32[128,512]{1,0:T(8,128)S(1)}, u32[]{:S(2)}, u32[]{:S(2)}) collective-permute-start(f32[128,512]{1,0:T(8,128)S(1)} %get-tuple-element.99), channel_id=1, source_target_pairs={{0,4},{1,5},{2,6},{3,7},{16,20},{17,21},{18,22},{19,23}} | collective-permute-start | bytes 786440 | tf_op jit(solution)/shard_map/ppermute | solution.py:376
  8.6 4.0 %collective-permute-start = (f32[64,512]{1,0:T(8,128)S(1)}, f32[64,512]{1,0:T(8,128)S(1)}, u32[]{:S(2)}, u32[]{:S(2)}) collective-permute-start(f32[64,512]{1,0:T(8,128)S(1)} %get-tuple-element.94), channel_id=1, source_target_pairs={{0,1},{1,0},{2,3},{3,2},{4,5},{5,4},{6,7},{7,6},{8,9},{9,8},{10,11... | collective-permute-start | bytes 393224 | tf_op jit(solution)/shard_map/ppermute | solution.py:397
  11.2 8.1 %collective-permute-start.3 = (f32[128,512]{1,0:T(8,128)S(1)}, f32[128,512]{1,0:T(8,128)S(1)}, u32[]{:S(2)}, u32[]{:S(2)}) collective-permute-start(f32[128,512]{1,0:T(8,128)S(1)} %get-tuple-element.104), channel_id=1, source_target_pairs={{0,4},{1,5},{2,6},{3,7},{16,20},{17,21},{18,22},{19,23}} | collective-permute-start | bytes 786440 | tf_op jit(solution)/shard_map/ppermute | solution.py:376
  13.8 7.8 %collective-permute-start.2 = (f32[128,512]{1,0:T(8,128)S(1)}, f32[128,512]{1,0:T(8,128)S(1)}, u32[]{:S(2)}, u32[]{:S(2)}) collective-permute-start(f32[128,512]{1,0:T(8,128)S(1)} %multiply_add_fusion.7), channel_id=1, source_target_pairs={{4,8},{5,9},{6,10},{7,11},{20,24},{21,25},{22,26},{23,27}} | collective-permute-start | bytes 786440 | tf_op jit(solution)/shard_map/ppermute | solution.py:376
  19.4 6.2 %collective-permute-start.4 = (f32[128,512]{1,0:T(8,128)S(1)}, f32[128,512]{1,0:T(8,128)S(1)}, u32[]{:S(2)}, u32[]{:S(2)}) collective-permute-start(f32[128,512]{1,0:T(8,128)S(1)} %multiply_add_fusion.5), channel_id=1, source_target_pairs={{4,8},{5,9},{6,10},{7,11},{20,24},{21,25},{22,26},{23,27}} | collective-permute-start | bytes 786440 | tf_op jit(solution)/shard_map/ppermute | solution.py:376
  20.0 5.5 %collective-permute-start.5 = (f32[64,512]{1,0:T(8,128)S(1)}, f32[64,512]{1,0:T(8,128)S(1)}, u32[]{:S(2)}, u32[]{:S(2)}) collective-permute-start(f32[64,512]{1,0:T(8,128)S(1)} %add.41.refs_13_), channel_id=1, source_target_pairs={{0,2},{2,0},{1,3},{3,1},{4,6},{6,4},{5,7},{7,5},{8,10},{10,8},{9,1... | collective-permute-start | bytes 393224 | tf_op jit(solution)/shard_map/ppermute | solution.py:397
  21.6 4.7 %copy-start.7 = (bf16[1024,64]{0,1:T(8,128)(2,1)S(1)}, bf16[1024,64]{0,1:T(8,128)(2,1)}, u32[]{:S(2)}) copy-start(bf16[1024,64]{0,1:T(8,128)(2,1)} %param.24) | copy-start | bytes 393220
  21.7 4.6 %collective-permute-start.7 = (f32[128,512]{1,0:T(8,128)S(1)}, f32[128,512]{1,0:T(8,128)S(1)}, u32[]{:S(2)}, u32[]{:S(2)}) collective-permute-start(f32[128,512]{1,0:T(8,128)S(1)} %multiply_add_fusion.6), channel_id=1, source_target_pairs={{8,12},{9,13},{10,14},{11,15},{24,28},{25,29},{26,30},{27,31}} | collective-permute-start | bytes 786440 | tf_op jit(solution)/shard_map/ppermute | solution.py:376
  25.6 5.3 %collective-permute-start.6 = (f32[128,512]{1,0:T(8,128)S(1)}, f32[128,512]{1,0:T(8,128)S(1)}, u32[]{:S(2)}, u32[]{:S(2)}) collective-permute-start(f32[128,512]{1,0:T(8,128)S(1)} %multiply_add_fusion.4), channel_id=1, source_target_pairs={{8,12},{9,13},{10,14},{11,15},{24,28},{25,29},{26,30},{27,31}} | collective-permute-start | bytes 786440 | tf_op jit(solution)/shard_map/ppermute | solution.py:376
  30.2 4.6 %collective-permute-start.8 = (f32[128,512]{1,0:T(8,128)S(1)}, f32[128,512]{1,0:T(8,128)S(1)}, u32[]{:S(2)}, u32[]{:S(2)}) collective-permute-start(f32[128,512]{1,0:T(8,128)S(1)} %get-tuple-element.119.refs_10_), channel_id=1, source_target_pairs={{12,8},{13,9},{14,10},{15,11},{28,24},{29,25},{30,26},{31,27}} | collective-permute-start | bytes 786440 | tf_op jit(solution)/shard_map/ppermute | solution.py:376
  34.1 1.3 %collective-permute-start.9 = (f32[64,512]{1,0:T(8,128)S(1)}, f32[64,512]{1,0:T(8,128)S(1)}, u32[]{:S(2)}, u32[]{:S(2)}) collective-permute-start(f32[64,512]{1,0:T(8,128)S(1)} %get-tuple-element.120), channel_id=1, source_target_pairs={{0,1},{1,0},{2,3},{3,2},{4,5},{5,4},{6,7},{7,6},{8,9},{9,8},{10,11... | collective-permute-start | bytes 393224 | tf_op jit(solution)/shard_map/ppermute | solution.py:397
  34.1 8.3 %collective-permute-start.11 = (f32[128,512]{1,0:T(8,128)S(1)}, f32[128,512]{1,0:T(8,128)S(1)}, u32[]{:S(2)}, u32[]{:S(2)}) collective-permute-start(f32[128,512]{1,0:T(8,128)S(1)} %get-tuple-element.127.refs_10_), channel_id=1, source_target_pairs={{12,8},{13,9},{14,10},{15,11},{28,24},{29,25},{30,26},{31,27}} | collective-permute-start | bytes 786440 | tf_op jit(solution)/shard_map/ppermute | solution.py:376
  35.5 5.6 %collective-permute-start.10 = (f32[64,512]{1,0:T(8,128)S(1)}, f32[64,512]{1,0:T(8,128)S(1)}, u32[]{:S(2)}, u32[]{:S(2)}) collective-permute-start(f32[64,512]{1,0:T(8,128)S(1)} %add.47.refs_1_), channel_id=1, source_target_pairs={{0,2},{2,0},{1,3},{3,1},{4,6},{6,4},{5,7},{7,5},{8,10},{10,8},{9,1... | collective-permute-start | bytes 393224 | tf_op jit(solution)/shard_map/ppermute | solution.py:397
  37.0 10.5 %collective-permute-start.12 = (f32[128,512]{1,0:T(8,128)S(1)}, f32[128,512]{1,0:T(8,128)S(1)}, u32[]{:S(2)}, u32[]{:S(2)}) collective-permute-start(f32[128,512]{1,0:T(8,128)S(1)} %multiply_add_fusion.3), channel_id=1, source_target_pairs={{8,4},{9,5},{10,6},{11,7},{24,20},{25,21},{26,22},{27,23}} | collective-permute-start | bytes 786440 | tf_op jit(solution)/shard_map/ppermute | solution.py:376
  42.4 6.6 %copy-start.6 = (bf16[512,512]{1,0:T(8,128)(2,1)S(1)}, bf16[512,512]{1,0:T(8,128)(2,1)}, u32[]{:S(2)}) copy-start(bf16[512,512]{1,0:T(8,128)(2,1)} %get-tuple-element.130.refs_5_.refs_6_) | copy-start | bytes 1572868
  42.5 9.9 %collective-permute-start.13 = (f32[128,512]{1,0:T(8,128)S(1)}, f32[128,512]{1,0:T(8,128)S(1)}, u32[]{:S(2)}, u32[]{:S(2)}) collective-permute-start(f32[128,512]{1,0:T(8,128)S(1)} %multiply_add_fusion.2), channel_id=1, source_target_pairs={{8,4},{9,5},{10,6},{11,7},{24,20},{25,21},{26,22},{27,23}} | collective-permute-start | bytes 786440 | tf_op jit(solution)/shard_map/ppermute | solution.py:376
  43.3 10.1 %collective-permute-start.14 = (f32[64,1024]{1,0:T(8,128)S(1)}, f32[64,1024]{1,0:T(8,128)S(1)}, u32[]{:S(2)}, u32[]{:S(2)}) collective-permute-start(f32[64,1024]{1,0:T(8,128)S(1)} %get-tuple-element.136), channel_id=1, source_target_pairs={{0,4},{4,0},{8,12},{12,8},{1,5},{5,1},{9,13},{13,9},{2,6},{6,2},{1... | collective-permute-start | bytes 786440 | tf_op jit(solution)/shard_map/ppermute | solution.py:376
  47.6 18.7 %collective-permute-start.16 = (f32[128,512]{1,0:T(8,128)S(1)}, f32[128,512]{1,0:T(8,128)S(1)}, u32[]{:S(2)}, u32[]{:S(2)}) collective-permute-start(f32[128,512]{1,0:T(8,128)S(1)} %multiply_add_fusion.1), channel_id=1, source_target_pairs={{4,0},{5,1},{6,2},{7,3},{20,16},{21,17},{22,18},{23,19}} | collective-permute-start | bytes 786440 | tf_op jit(solution)/shard_map/ppermute | solution.py:376
  52.4 10.5 %copy-start.10 = (bf16[128,512]{1,0:T(8,128)(2,1)S(1)}, bf16[128,512]{1,0:T(8,128)(2,1)}, u32[]{:S(2)}) copy-start(bf16[128,512]{1,0:T(8,128)(2,1)} %get-tuple-element.140.refs_7_.refs_11_) | copy-start | bytes 393220
  53.4 18.5 %collective-permute-start.17 = (f32[64,1024]{1,0:T(8,128)S(1)}, f32[64,1024]{1,0:T(8,128)S(1)}, u32[]{:S(2)}, u32[]{:S(2)}) collective-permute-start(f32[64,1024]{1,0:T(8,128)S(1)} %add.51), channel_id=1, source_target_pairs={{0,8},{8,0},{4,12},{12,4},{1,9},{9,1},{5,13},{13,5},{2,10},{10,2},... | collective-permute-start | bytes 786440 | tf_op jit(solution)/shard_map/ppermute | solution.py:376
  61.5 13.3 %collective-permute-start.15 = (f32[128,512]{1,0:T(8,128)S(1)}, f32[128,512]{1,0:T(8,128)S(1)}, u32[]{:S(2)}, u32[]{:S(2)}) collective-permute-start(f32[128,512]{1,0:T(8,128)S(1)} %multiply_add_fusion), channel_id=1, source_target_pairs={{4,0},{5,1},{6,2},{7,3},{20,16},{21,17},{22,18},{23,19}} | collective-permute-start | bytes 786440 | tf_op jit(solution)/shard_map/ppermute | solution.py:376
  72.0 7.7 %collective-permute-start.18 = (f32[64,1024]{1,0:T(8,128)S(1)}, f32[64,1024]{1,0:T(8,128)S(1)}, u32[]{:S(2)}, u32[]{:S(2)}) collective-permute-start(f32[64,1024]{1,0:T(8,128)S(1)} %add.52.refs_1_), channel_id=1, source_target_pairs={{0,4},{4,0},{8,12},{12,8},{1,5},{5,1},{9,13},{13,9},{2,6},{6,2},{1... | collective-permute-start | bytes 786440 | tf_op jit(solution)/shard_map/ppermute | solution.py:376
  (11 other events, 26.5 us)
